TPU v7x, 256 devices: a whole 4x4x8 slice. The times are simulated.
256 devices in a mesh: dp: 16 (over z, core), own: 16 (over x, y).
Axes of the slice: x: 4, y: 4, z: 8, core: 2. Of those that a mesh axis runs over, the one named last changes fastest.
Arguments:
- tokens: bfloat16 [512, 256, 1024], P(('dp', 'own')), may hold values from -6 to 6
- cotangent: bfloat16 [512, 256, 1024], P(('dp', 'own')), may hold values from -6 to 6
- lengths: int32 [512], P(('dp', 'own')), may hold values from 1 to 256, as said below
- norm_gain: float32 [1024], replicated, may hold values from 0.1 to 12
- weight_in: bfloat16 [1024, 4096], P('own'), may hold values from -0.1875 to 0.1875
- weight_out: bfloat16 [1024, 1024], P('own'), may hold values from -0.1875 to 0.1875
- moment_in: float32 [1024, 4096], P('own'), may hold values from -6 to 6
- square_in: float32 [1024, 4096], P('own'), may hold values from 0.25 to 4
- moment_out: float32 [1024, 1024], P('own'), may hold values from -6 to 6
- square_out: float32 [1024, 1024], P('own'), may hold values from 0.25 to 4
Outputs:
- new_weight_in: float32 [1024, 4096], P('own')
- new_moment_in: float32 [1024, 4096], P('own')
- new_square_in: float32 [1024, 4096], P('own')
- new_weight_out: float32 [1024, 1024], P('own')
- new_moment_out: float32 [1024, 1024], P('own')
- new_square_out: float32 [1024, 1024], P('own')
Inputs may be any that keep to these rules, and one draw needn't show every extreme that they name: `lengths`: the live events of a history are its first ones; some history holds 256.
All inputs are finite; a program needn't handle non-finite values.
Results may differ from a plain program's by a relative error of at most 0.004.
Values may be sent and summed in bfloat16 or wider, within the bound.
No kernel may reach another device: no remote copies, remote signals or barrier semaphores. Data moves between devices by JAX's collectives and lax.ppermute only.
A program may use at most 128 MiB of HBM per device.

v0:
```python
import functools

import jax
import jax.numpy as jnp
from jax import lax
from jax.experimental import pallas as pl
from jax.experimental.pallas import tpu as pltpu
from jax.sharding import Mesh
from jax.sharding import PartitionSpec as P

BLK = 256
HEAD_WIDTH = 256

norm_eps = 1e-06
beta_first = 0.9
beta_second = 0.95
learn_rate = 0.01
step_number = 10.0
update_eps = 1e-08
ratio_eps = 1e-06

OWN = ("x", "y")
SWAP = ((0, 1), (1, 0))

LINKS = (("x", 1), ("y", 1), ("x", 3), ("y", 3))
LINK_MASKS = (0b0100, 0b0001, 0b1100, 0b0011)


def rms_scale(values):
    return values * lax.rsqrt(jnp.mean(values * values, axis=-1, keepdims=True) + norm_eps)


def sigmoid(values):
    return 1.0 / (1.0 + jnp.exp(-values))


def allowed_mask(length):
    row = lax.broadcasted_iota(jnp.int32, (BLK, BLK), 0)
    col = lax.broadcasted_iota(jnp.int32, (BLK, BLK), 1)
    return ((col <= row) & (row < length)).astype(jnp.float32) * (1.0 / BLK)


def dot_nt(left, right):
    return lax.dot_general(
        left, right, (((1,), (1,)), ((), ())), preferred_element_type=jnp.float32
    )


def dot_tn(left, right):
    return lax.dot_general(
        left, right, (((0,), (0,)), ((), ())), preferred_element_type=jnp.float32
    )


def dot_nn(left, right):
    return jnp.dot(left, right, preferred_element_type=jnp.float32)


def silu_slope(values):
    sig = sigmoid(values)
    act = values * sig
    return act, sig + act * (1.0 - sig)


def relative_slot(mask, turn):
    x_far, x_near = (mask >> 3) & 1, ((mask >> 3) ^ (mask >> 2)) & 1
    y_far, y_near = (mask >> 1) & 1, ((mask >> 1) ^ mask) & 1
    bits = (x_near, y_near, x_far, y_far)
    slot = 0
    for step in range(4):
        slot = slot + (bits[(turn + step) % 4] << step)
    return slot


def owner_mask(slot, turn):
    mask = 0
    for step in range(4):
        if slot >> step & 1:
            mask ^= LINK_MASKS[(turn + step) % 4]
    return mask


def place_rows(turn, own, near, far, weight):
    count, rows, _ = near.shape
    for slot in range(2 * count):
        block = near[slot] if slot < count else far[slot - count]
        start = pl.multiple_of((own ^ owner_mask(slot, turn)) * rows, rows)
        weight[pl.ds(start, rows), :] = block


def project_kernel(turn, place, normed, near, far, projected, rest, weight):
    width = projected.shape[2]

    @pl.when(pl.program_id(0) == 0)
    def _():
        place_rows(turn, place[0], near, far, weight)
        rest[...] = weight[:, width:]

    projected[0] = dot_nn(normed[0], weight[:, :width])


def attention_kernel(
    turn, place, lengths, normed, near, far, queries_in, keys_in, values_out, scores, mixed, weight
):
    @pl.when(pl.program_id(0) == 0)
    def _():
        place_rows(turn, place[0], near, far, weight)

    proj = dot_nn(normed[0], weight[...])
    values_out[0] = proj
    allowed = allowed_mask(lengths[pl.program_id(0)])
    for head in range(proj.shape[1] // HEAD_WIDTH):
        part = slice(head * HEAD_WIDTH, (head + 1) * HEAD_WIDTH)
        values, queries, key_part = (
            (block * sigmoid(block)).astype(jnp.bfloat16)
            for block in (proj[:, part], queries_in[0, :, part], keys_in[0, :, part])
        )
        score = dot_nt(queries, key_part) * HEAD_WIDTH ** (-0.5)
        scores[0, head] = score
        attention = (score * sigmoid(score) * allowed).astype(jnp.bfloat16)
        mixed[0, :, part] = dot_nn(attention, values)


def gating_kernel(
    turn, place, normed, near, far, masked, keep, recv, mixed, gating_out, grad_gated, stats, weight
):
    width = keep.shape[0]

    @pl.when(pl.program_id(0) == 0)
    def _():
        place_rows(turn, place[0], near, far, weight)

    proj = dot_nn(normed[0], weight[...])
    gating_out[0] = proj
    core = place[1]
    mine = masked[0, :, pl.ds(pl.multiple_of(core * width, width), width)]
    others = masked[0, :, pl.ds(pl.multiple_of((1 - core) * width, width), width)]
    grad = (dot_nt(mine, keep[...]) + dot_nt(others, recv[...])).astype(jnp.bfloat16)
    grad_gated[0] = grad
    mix = mixed[0]
    square = jnp.sum(mix * mix, axis=1, keepdims=True)
    cross = jnp.sum(
        grad.astype(jnp.float32) * (proj * sigmoid(proj)) * mix, axis=1, keepdims=True
    )
    lane = lax.broadcasted_iota(jnp.int32, (BLK, 128), 1)
    stats[0] = jnp.where(lane == 0, square, cross)


def norm_back_kernel(
    projected, mixed, grad_gated, stats, stats_other, gated, grad_gating, grad_mixed
):
    model_width = 2 * mixed.shape[2]
    total = stats[0] + stats_other[0]
    inv = lax.rsqrt(total[:, 0:1] / model_width + norm_eps)
    back = inv * inv * inv * (total[:, 1:2] / model_width)
    gating, slope = silu_slope(projected[0])
    mix = mixed[0]
    grad = grad_gated[0].astype(jnp.float32)
    scaled = mix * inv
    gated[0] = (scaled * gating).astype(jnp.bfloat16)
    grad_gating[0] = (grad * scaled * slope).astype(jnp.bfloat16)
    grad_mixed[0] = (inv * (grad * gating) - mix * back).astype(jnp.bfloat16)


def attention_back_kernel(
    lengths, values_in, queries_in, keys_in, scores, grad_mixed, grad_values, grad_queries, grad_keys
):
    allowed = allowed_mask(lengths[pl.program_id(0)])
    for head in range(grad_mixed.shape[2] // HEAD_WIDTH):
        part = slice(head * HEAD_WIDTH, (head + 1) * HEAD_WIDTH)
        values, values_slope = silu_slope(values_in[0, :, part])
        queries, queries_slope = silu_slope(queries_in[0, :, part])
        key_part, keys_slope = silu_slope(keys_in[0, :, part])
        act, slope = silu_slope(scores[0, head])
        attention = (act * allowed).astype(jnp.bfloat16)
        grad_head = grad_mixed[0, :, part]
        grad_att = dot_nt(grad_head, values.astype(jnp.bfloat16)).astype(jnp.bfloat16)
        grad_score = (
            grad_att.astype(jnp.float32) * allowed * slope * HEAD_WIDTH ** (-0.5)
        ).astype(jnp.bfloat16)
        for out, grad, side in (
            (grad_values, dot_tn(attention, grad_head), values_slope),
            (grad_queries, dot_nn(grad_score, key_part.astype(jnp.bfloat16)), queries_slope),
            (grad_keys, dot_tn(grad_score, queries.astype(jnp.bfloat16)), keys_slope),
        ):
            held = grad.astype(jnp.bfloat16).astype(jnp.float32)
            out[0, :, part] = (held * side).astype(jnp.bfloat16)


def store_slot(slot, value, columns, near, far):
    count = near.shape[0]

    @pl.when(slot < count)
    def _():
        near[jnp.minimum(slot, count - 1), :, columns] = value

    @pl.when(slot >= count)
    def _():
        far[jnp.maximum(slot - count, 0), :, columns] = value


def term_kernel(turn, place, normed_t, grads, *refs):
    near, far = refs[-2:]
    rows, width = near.shape[1], grads.shape[1]
    term = dot_nn(normed_t[...], grads[...]).astype(jnp.bfloat16)
    step = pl.program_id(0)
    per_step = term.shape[0] // rows
    for block in range(per_step):
        slot = relative_slot((step * per_step + block) ^ place[0], turn)
        store_slot(slot, term[block * rows : (block + 1) * rows], slice(0, width), near, far)
    if len(refs) == 4:
        half = refs[0].shape[0] // rows
        per_step = half // pl.num_programs(0)
        for side, held in ((place[1], refs[0]), (1 - place[1], refs[1])):
            for block in range(per_step):
                at = step * per_step + block
                value = held[pl.ds(pl.multiple_of(at * rows, rows), rows), :]
                slot = relative_slot((side * half + at) ^ place[0], turn)
                store_slot(slot, value, slice(width, width + value.shape[1]), near, far)


def term_out_kernel(place, gated, masked, term):
    term[0] = dot_tn(gated[...], masked[...]).astype(jnp.bfloat16)


def rows_of(*dims):
    return pl.BlockSpec((1, *dims), lambda i, *_: (i,) + (0,) * len(dims))


def whole(*dims):
    return pl.BlockSpec(dims, lambda i, *_: (0,) * len(dims))


def call(kernel, name, grid, prefetch, in_specs, out, inputs, scratch=(), flops=0):
    moved = sum(v.size * v.dtype.itemsize for v in inputs)
    return pl.pallas_call(
        kernel,
        grid_spec=pltpu.PrefetchScalarGridSpec(
            num_scalar_prefetch=len(prefetch),
            grid=grid,
            in_specs=in_specs,
            out_specs=[spec for spec, _, _ in out],
            scratch_shapes=list(scratch),
        ),
        out_shape=[jax.ShapeDtypeStruct(shape, dtype) for _, shape, dtype in out],
        compiler_params=pltpu.CompilerParams(vmem_limit_bytes=20 * 1024 * 1024),
        cost_estimate=pl.CostEstimate(flops=1, bytes_accessed=1, transcendentals=0),
        name=name,
    )(*prefetch, *inputs)


def project(turn, place, normed, near, far, width):
    count, rows, depth = normed.shape
    columns = near.shape[2]
    return call(
        functools.partial(project_kernel, turn),
        "project",
        (count,),
        (place,),
        [rows_of(rows, depth), whole(*near.shape), whole(*far.shape)],
        [
            (rows_of(rows, width), (count, rows, width), jnp.float32),
            (whole(depth, columns - width), (depth, columns - width), jnp.bfloat16),
        ],
        (normed, near, far),
        [pltpu.VMEM((depth, columns), jnp.bfloat16)],
        2 * count * rows * depth * width,
    )


def attention_forward(turn, place, lengths, normed, near, far, queries, keys_in):
    count, rows, depth = normed.shape
    width = near.shape[2]
    heads = width // HEAD_WIDTH
    return call(
        functools.partial(attention_kernel, turn),
        "attention_forward",
        (count,),
        (place, lengths),
        [rows_of(rows, depth), whole(*near.shape), whole(*far.shape)] + [rows_of(rows, width)] * 2,
        [
            (rows_of(rows, width), (count, rows, width), jnp.float32),
            (rows_of(heads, rows, rows), (count, heads, rows, rows), jnp.float32),
            (rows_of(rows, width), (count, rows, width), jnp.float32),
        ],
        (normed, near, far, queries, keys_in),
        [pltpu.VMEM((depth, width), jnp.bfloat16)],
        3 * count * rows * depth * width,
    )


def gating_forward(turn, place, normed, near, far, masked, keep, recv, mixed):
    count, rows, depth = normed.shape
    width = near.shape[2]
    return call(
        functools.partial(gating_kernel, turn),
        "gating_forward",
        (count,),
        (place,),
        [
            rows_of(rows, depth),
            whole(*near.shape),
            whole(*far.shape),
            rows_of(rows, depth),
            whole(*keep.shape),
            whole(*recv.shape),
            rows_of(rows, width),
        ],
        [
            (rows_of(rows, width), (count, rows, width), jnp.float32),
            (rows_of(rows, width), (count, rows, width), jnp.bfloat16),
            (rows_of(rows, 128), (count, rows, 128), jnp.float32),
        ],
        (normed, near, far, masked, keep, recv, mixed),
        [pltpu.VMEM((depth, width), jnp.bfloat16)],
        4 * count * rows * depth * width,
    )


def norm_back(projected, mixed, grad_gated, stats, stats_other):
    count, rows, width = projected.shape
    block = rows_of(rows, width)
    return call(
        norm_back_kernel,
        "norm_back",
        (count,),
        (),
        [
            block,
            block,
            block,
            rows_of(rows, 128),
            pl.BlockSpec((1, rows, 128), lambda i, *_: ((i + count // 2) % count, 0, 0)),
        ],
        [(block, projected.shape, jnp.bfloat16)] * 3,
        (projected, mixed, grad_gated, stats, stats_other),
    )


def attention_back(lengths, values, queries, keys_in, scores, grad_mixed):
    count, rows, width = values.shape
    heads = width // HEAD_WIDTH
    block = rows_of(rows, width)
    return call(
        attention_back_kernel,
        "attention_back",
        (count,),
        (lengths,),
        [block, block, block, rows_of(heads, rows, rows), block],
        [(block, values.shape, jnp.bfloat16)] * 3,
        (values, queries, keys_in, scores, grad_mixed),
        flops=8 * count * rows * rows * width,
    )


def term(turn, place, owned, normed_t, grads, extra=None):
    depth, rows = normed_t.shape
    width = grads.shape[1]
    steps = 4
    owners = depth // owned
    columns = width
    in_specs = [
        pl.BlockSpec((depth // steps, rows), lambda i, *_: (i, 0)),
        whole(rows, width),
    ]
    inputs = [normed_t, grads]
    if extra is not None:
        keep, recv, at = extra
        share = keep.shape[1] // 2
        columns += share
        in_specs += [pl.BlockSpec((keep.shape[0], share), lambda i, *_: (0, at))] * 2
        inputs += [keep, recv]
    shape = (owners // 2, owned, columns)
    return call(
        functools.partial(term_kernel, turn),
        "term",
        (steps,),
        (place,),
        in_specs,
        [(whole(*shape), shape, jnp.bfloat16)] * 2,
        inputs,
        flops=2 * depth * rows * width,
    )


def term_out(place, gated, masked):
    rows, width = gated.shape
    return call(
        term_out_kernel,
        "term_out",
        (2,),
        (place,),
        [whole(rows, width), pl.BlockSpec((rows, width), lambda i, s: (0, (i + s[1]) % 2))],
        [(rows_of(width, width), (2, width, width), jnp.bfloat16)],
        (gated, masked),
        flops=4 * rows * width * width,
    )[0]


def sum_squares(values):
    values = values.astype(jnp.float32)
    return jnp.sum(values * values)


def update_kernel(place, squares, mine, other, *refs):
    half = mine.shape[1] // 5
    model_width = 2 * half
    first = place[1] == 0
    owners = squares.shape[0] // 8
    total = sum(squares[8 * i : 8 * i + 1, 0:1] for i in range(owners))
    clip = jnp.minimum(1.0, jnp.sqrt(5.0 * model_width * model_width / (total + norm_eps)))
    for parts, (weight, moment, square, new_weight, new_moment, new_square) in (
        (range(4), (refs[0], refs[1], refs[2], refs[6], refs[7], refs[8])),
        (range(4, 5), (refs[3], refs[4], refs[5], refs[9], refs[10], refs[11])),
    ):
        update_sq = weight_sq = 0.0
        for part in parts:
            at = slice(part * half, (part + 1) * half)
            both = (mine[:, at].astype(jnp.float32), other[:, at].astype(jnp.float32))
            for core in (0, 1):
                grad = jnp.where(first, both[core], both[1 - core]) * clip
                start = (part - parts[0]) * model_width + core * half
                col = slice(start, start + half)
                held = beta_first * moment[:, col] + (1.0 - beta_first) * grad
                held_sq = beta_second * square[:, col] + (1.0 - beta_second) * grad * grad
                new_moment[:, col] = held
                new_square[:, col] = held_sq
                update = (held * (1.0 / (1.0 - beta_first**step_number))) / (
                    jnp.sqrt(held_sq * (1.0 / (1.0 - beta_second**step_number))) + update_eps
                )
                new_weight[:, col] = update
                update_sq += jnp.sum(update * update, axis=1, keepdims=True)
                held = weight[:, col].astype(jnp.float32)
                weight_sq += jnp.sum(held * held, axis=1, keepdims=True)
        ratio = learn_rate * jnp.sqrt(weight_sq) / (jnp.sqrt(update_sq) + ratio_eps)
        new_weight[...] = weight[...].astype(jnp.float32) - ratio * new_weight[...]


def update_rows(place, squares, mine, other, *state):
    rows = 16
    count = mine.shape[0] // rows

    def block(value):
        return pl.BlockSpec((rows, value.shape[1]), lambda i, *_: (i, 0))

    return call(
        update_kernel,
        "update_rows",
        (count,),
        (place,),
        [whole(*squares.shape)] + [block(v) for v in (mine, other, *state)],
        [(block(v), v.shape, jnp.float32) for v in state],
        (squares, mine, other, *state),
    )


def swap_cores(values):
    return lax.ppermute(values, "c", SWAP)


def over_link(values, link):
    axis, mask = LINKS[link % 4]
    return lax.ppermute(values, axis, [(i, i ^ mask) for i in range(4)])


def gather_parts(parts):
    held = [part[None] for part in parts]
    for step in range(3):
        got = [over_link(part, turn + step) for turn, part in enumerate(held)]
        held = [jnp.concatenate(pair, axis=0) for pair in zip(held, got)]
    return [(part, over_link(part, turn + 3)) for turn, part in enumerate(held)]


def add_halves(mine, got):
    return (mine.astype(jnp.float32) + got.astype(jnp.float32)).astype(jnp.bfloat16)


def scatter_parts(pairs):
    for step in (3, 2, 1, 0):
        got = [over_link(far, turn + step) for turn, (_, far) in enumerate(pairs)]
        mine, got = lax.optimization_barrier(([near for near, _ in pairs], got))
        held = [add_halves(*pair) for pair in zip(mine, got)]
        if step:
            pairs = [jnp.split(part, 2, axis=0) for part in held]
    return [part[0] for part in held]


def after(value, done):
    return lax.optimization_barrier((value, done))[0]


def exchange(blocks, axes):
    return lax.all_to_all(blocks, axes, 0, 0, tiled=True)


def per_device(
    tokens,
    cotangent,
    lengths,
    norm_gain,
    weight_in,
    weight_out,
    moment_in,
    square_in,
    moment_out,
    square_out,
):
    slots, rows, model_width = tokens.shape
    half = model_width // 2
    quarter = half // 2
    core = lax.axis_index("c")
    own = lax.axis_index(OWN)
    owners = lax.axis_size(OWN)
    planes = lax.axis_size("z")
    owned = weight_in.shape[0]
    place = jnp.stack([own, core]).astype(jnp.int32)

    mine = [
        lax.dynamic_slice_in_dim(weight_in, part * model_width + core * half, half, axis=1)
        for part in range(4)
    ]
    mine_out = lax.dynamic_slice_in_dim(weight_out, core * half, half, axis=1)
    (q_near, q_far), (k_near, k_far), (v_near, v_far), (g_near, g_far) = gather_parts(
        [
            jnp.concatenate([mine[2], mine_out[:, :quarter]], axis=1),
            jnp.concatenate([mine[3], mine_out[:, quarter:]], axis=1),
            mine[1],
            mine[0],
        ]
    )

    normed = (rms_scale(tokens.astype(jnp.float32)) * norm_gain).astype(jnp.bfloat16)
    row_index = jnp.arange(rows, dtype=jnp.int32)
    live = row_index[None, :] < lengths[:, None]
    masked = jnp.where(live[:, :, None], cotangent, jnp.zeros_like(cotangent))
    normed = jnp.concatenate([normed, swap_cores(normed)], axis=0)
    masked = jnp.concatenate([masked, swap_cores(masked)], axis=0)
    lengths = jnp.concatenate([lengths, swap_cores(lengths)], axis=0)
    normed, masked, normed_t = lax.optimization_barrier(
        (normed, masked, normed.reshape(-1, model_width).T)
    )

    queries, out_first = project(0, place, normed, q_near, q_far, half)
    keys_in, out_second = project(1, place, normed, k_near, k_far, half)
    out_cols = jnp.concatenate([out_first, out_second], axis=1).reshape(2, half, half)
    keep = lax.dynamic_index_in_dim(out_cols, core, axis=0, keepdims=False)
    recv = swap_cores(lax.dynamic_index_in_dim(out_cols, 1 - core, axis=0, keepdims=False))
    values, scores, mixed = attention_forward(
        2, place, lengths, normed, v_near, v_far, queries, keys_in
    )
    gating, grad_gated, stats = gating_forward(
        3, place, normed, g_near, g_far, masked, keep, recv, mixed
    )
    gated, grad_gating, grad_mixed = norm_back(
        gating, mixed, grad_gated, stats, swap_cores(stats)
    )

    def flat(part):
        return part.reshape(-1, part.shape[2])

    term_g = term(0, place, owned, normed_t, flat(grad_gating))
    grad_mixed = after(grad_mixed, term_g)
    outer = term_out(place, flat(gated), flat(masked))
    outer_recv = swap_cores(outer[1])
    grad_values, grad_queries, grad_keys = attention_back(
        lengths, values, queries, keys_in, scores, grad_mixed
    )
    term_v = term(1, place, owned, normed_t, flat(grad_values), (outer[0], outer_recv, 0))
    grad_queries = after(grad_queries, term_v)
    term_q = term(2, place, owned, normed_t, flat(grad_queries), (outer[0], outer_recv, 1))
    grad_keys = after(grad_keys, term_q)
    term_k = term(3, place, owned, normed_t, flat(grad_keys))
    part_g, part_v, part_q, part_k = scatter_parts([term_g, term_v, term_q, term_k])
    part = jnp.concatenate(
        [part_g, part_v[:, :half], part_q[:, :half], part_k, part_v[:, half:], part_q[:, half:]],
        axis=1,
    )

    piece = jnp.sum(
        exchange(part, "z").reshape(planes, owned // planes, -1).astype(jnp.float32), axis=0
    ).astype(jnp.bfloat16)
    shard = exchange(
        jnp.broadcast_to(piece[None], (planes, *piece.shape)).reshape(owned, -1), "z"
    )
    other = swap_cores(shard)
    local_square = sum_squares(shard) + sum_squares(other)
    squares = exchange(jnp.broadcast_to(local_square, (owners * 8, 128)), OWN)
    return update_rows(
        place,
        squares,
        shard,
        other,
        weight_in,
        moment_in,
        square_in,
        weight_out,
        moment_out,
        square_out,
    )


def solution(mesh):
    fine = Mesh(mesh.devices.reshape(8, 2, 4, 4), ("z", "c", "x", "y"))
    histories = ("z", "c", "x", "y")
    placed = (
        P(histories, None, None),
        P(histories, None, None),
        P(histories),
        P(),
        P(OWN, None),
        P(OWN, None),
        P(OWN, None),
        P(OWN, None),
        P(OWN, None),
        P(OWN, None),
    )
    return jax.shard_map(
        per_device,
        mesh=fine,
        in_specs=placed,
        out_specs=(P(OWN, None),) * 6,
        check_vma=False,
    )
```

profile of v0, /device:TPU:1, one launch (start us, length us, event | category | flops | bytes accessed | tf_op | source)
XLA Modules:
  0.0 216.3 jit_solution(12598885462368588030)
XLA Ops:
  1.7 3.4 %collective-permute-start.16 = (bf16[1,64,512]{2,1,0:T(8,128)(2,1)S(1)}, bf16[1,64,512]{2,1,0:T(8,128)(2,1)S(1)}, u32[]{:S(2)}, u32[]{:S(2)}) collective-permute-start(bf16[1,64,512]{2,1,0:T(8,128)(2,1)S(1)} %get-tuple-element.142), channel_id=1, source_target_pairs={{0,12},{4,8},{8,4},{12,0},{1,13},{5,9},{9,5},{13,1},{2,14},{6,10},... | collective-permute-start | bytes 196616 | tf_op jit(solution)/shard_map/ppermute | solution.py:463
  5.1 2.7 %collective-permute-start.2 = (bf16[1,64,512]{2,1,0:T(8,128)(2,1)S(1)}, bf16[1,64,512]{2,1,0:T(8,128)(2,1)S(1)}, u32[]{:S(2)}, u32[]{:S(2)}) collective-permute-start(bf16[1,64,512]{2,1,0:T(8,128)(2,1)S(1)} %get-tuple-element.145), channel_id=1, source_target_pairs={{0,3},{1,2},{2,1},{3,0},{4,7},{5,6},{6,5},{7,4},{8,11},{9,10},{10,... | collective-permute-start | bytes 196616 | tf_op jit(solution)/shard_map/ppermute | solution.py:463
  24.3 3.0 %collective-permute-start.17 = (bf16[2,64,512]{2,1,0:T(8,128)(2,1)S(1)}, bf16[2,64,512]{2,1,0:T(8,128)(2,1)S(1)}, u32[]{:S(2)}, u32[]{:S(2)}) collective-permute-start(bf16[2,64,512]{2,1,0:T(8,128)(2,1)S(1)} %pad_maximum_fusion.14), channel_id=1, source_target_pairs={{0,3},{1,2},{2,1},{3,0},{4,7},{5,6},{6,5},{7,4},{8,11},{9,10},{10,... | collective-permute-start | bytes 393224 | tf_op jit(solution)/shard_map/ppermute | solution.py:463
  27.4 4.0 %collective-permute-done.12 = bf16[4,64,768]{2,1,0:T(8,128)(2,1)S(1)} collective-permute-done((bf16[4,64,768]{2,1,0:T(8,128)(2,1)S(1)}, bf16[4,64,768]{2,1,0:T(8,128)(2,1)S(1)}, u32[]{:S(2)}, u32[]{:S(2)}) %collective-permute-start.12) | collective-permute-done | bytes 393248 | tf_op jit(solution)/shard_map/ppermute | solution.py:463
  37.2 14.9 %collective-permute-done.18 = bf16[4,64,512]{2,1,0:T(8,128)(2,1)} collective-permute-done((bf16[4,64,512]{2,1,0:T(8,128)(2,1)S(1)}, bf16[4,64,512]{2,1,0:T(8,128)(2,1)}, u32[]{:S(2)}, u32[]{:S(2)}) %collective-permute-start.18) | collective-permute-done | bytes 262176 | tf_op jit(solution)/shard_map/ppermute | solution.py:463
  62.5 3.6 %project.3 = (f32[4,256,512]{2,1,0:T(8,128)S(1)}, bf16[1024,256]{1,0:T(8,128)(2,1)S(1)}) custom-call(s32[2]{0:T(128)S(1)} %pad_add_fusion.place, bf16[4,256,1024]{2,1,0:T(8,128)(2,1)S(1)} %pad_maximum_fusion.normed, bf16[8,64,768]{2,1,0:T(8,128)(2,1)S(1)} %pad_maximum_fusion.4.near, bf16[8,64,768]{2,1,0:T(8,128)(2,1)} %collective-permute-done.13.far), custom_call_target="tpu_custom_call" | custom-call | flops 1 | bytes 1 | tf_op jit(solution)/shard_map/project/pallas_call | solution.py:236
  66.2 3.9 %project.2 = (f32[4,256,512]{2,1,0:T(8,128)S(1)}, bf16[1024,256]{1,0:T(8,128)(2,1)S(1)}) custom-call(s32[2]{0:T(128)S(1)} %pad_add_fusion.place, bf16[4,256,1024]{2,1,0:T(8,128)(2,1)S(1)} %pad_maximum_fusion.normed, bf16[8,64,768]{2,1,0:T(8,128)(2,1)} %pad_maximum_fusion.3.near, bf16[8,64,768]{2,1,0:T(8,128)(2,1)} %collective-permute-done.9.far), custom_call_target="tpu_custom_call" | custom-call | flops 1 | bytes 1 | tf_op jit(solution)/shard_map/project/pallas_call | solution.py:236
  70.2 5.8 %collective-permute-start.14 = (bf16[512,512]{1,0:T(8,128)(2,1)S(1)}, bf16[512,512]{1,0:T(8,128)(2,1)S(1)}, u32[]{:S(2)}, u32[]{:S(2)}) collective-permute-start(bf16[512,512]{1,0:T(8,128)(2,1)S(1)} %get-tuple-element.132), channel_id=1, source_target_pairs={{0,16},{16,0},{1,17},{17,1},{2,18},{18,2},{3,19},{19,3},{4,20},{20... | collective-permute-start | bytes 1572872 | tf_op jit(solution)/shard_map/ppermute | solution.py:458
  77.6 5.5 %attention_forward.1 = (f32[4,256,512]{2,1,0:T(8,128)S(1)}, f32[4,2,256,256]{3,2,1,0:T(8,128)S(1)}, f32[4,256,512]{2,1,0:T(8,128)S(1)}) custom-call(s32[2]{0:T(128)S(1)} %pad_add_fusion.place, s32[4]{0:T(128)S(1)} %pad_add_fusion.1.lengths, bf16[4,256,1024]{2,1,0:T(8,128)(2,1)S(1)} %pad_maximum_fusion.normed, bf16[8,64,512]{2,1,0:T(8,128)(2,1)} %pad_maximum_fusion.6.near, ...), custom_call_target="tpu_custom_call" | custom-call | flops 1 | bytes 1 | tf_op jit(solution)/shard_map/attention_forward/pallas_call | solution.py:236
  83.2 5.1 %gating_forward.1 = (f32[4,256,512]{2,1,0:T(8,128)S(1)}, bf16[4,256,512]{2,1,0:T(8,128)(2,1)S(1)}, f32[4,256,128]{2,1,0:T(8,128)S(1)}) custom-call(s32[2]{0:T(128)S(1)} %pad_add_fusion.place, bf16[4,256,1024]{2,1,0:T(8,128)(2,1)S(1)} %pad_maximum_fusion.normed, bf16[8,64,512]{2,1,0:T(8,128)(2,1)S(1)} %pad_maximum_fusion.5.near, ...), custom_call_target="tpu_custom_call" | custom-call | flops 1 | bytes 1 | tf_op jit(solution)/shard_map/gating_forward/pallas_call | solution.py:236
  95.8 2.6 %term.4 = (bf16[8,64,512]{2,1,0:T(8,128)(2,1)S(1)}, bf16[8,64,512]{2,1,0:T(8,128)(2,1)S(1)}) custom-call(s32[2]{0:T(128)S(1)} %pad_add_fusion.place, bf16[1024,1024]{1,0:T(8,128)(2,1)S(1)} %bitcast.58, bf16[1024,512]{1,0:T(8,128)(2,1)S(1)} %bitcast.69), custom_call_target="tpu_custom_call" | custom-call | flops 1 | bytes 1 | tf_op jit(solution)/shard_map/term/pallas_call | solution.py:236
  98.5 4.7 %attention_back.1 = (bf16[4,256,512]{2,1,0:T(8,128)(2,1)S(1)}, bf16[4,256,512]{2,1,0:T(8,128)(2,1)S(1)}, bf16[4,256,512]{2,1,0:T(8,128)(2,1)S(1)}) custom-call(s32[4]{0:T(128)S(1)} %pad_add_fusion.1.lengths, f32[4,256,512]{2,1,0:T(8,128)S(1)} %get-tuple-element.81.values_in, f32[4,256,512]{2,1,0:T(8,128)S(1)} %get-tuple-element.73.queries_in, ...), custom_call_target="tpu_custom_call" | custom-call | flops 1 | bytes 1 | tf_op jit(solution)/shard_map/attention_back/pallas_call | solution.py:236
  103.2 3.0 %term.5 = (bf16[8,64,768]{2,1,0:T(8,128)(2,1)S(1)}, bf16[8,64,768]{2,1,0:T(8,128)(2,1)S(1)}) custom-call(s32[2]{0:T(128)S(1)} %pad_add_fusion.place, bf16[1024,1024]{1,0:T(8,128)(2,1)S(1)} %bitcast.59, bf16[1024,512]{1,0:T(8,128)(2,1)S(1)} %bitcast.66, bf16[512,512]{1,0:T(8,128)(2,1)S(1)} %get-tuple-element.131.refs_0_, ...), custom_call_target="tpu_custom_call" | custom-call | flops 1 | bytes 1 | tf_op jit(solution)/shard_map/term/pallas_call | solution.py:236
  106.3 3.1 %term.6 = (bf16[8,64,768]{2,1,0:T(8,128)(2,1)S(1)}, bf16[8,64,768]{2,1,0:T(8,128)(2,1)S(1)}) custom-call(s32[2]{0:T(128)S(1)} %pad_add_fusion.place, bf16[1024,1024]{1,0:T(8,128)(2,1)S(1)} %bitcast.60, bf16[1024,512]{1,0:T(8,128)(2,1)S(1)} %bitcast.65, bf16[512,512]{1,0:T(8,128)(2,1)S(1)} %get-tuple-element.131.refs_0_, ...), custom_call_target="tpu_custom_call" | custom-call | flops 1 | bytes 1 | tf_op jit(solution)/shard_map/term/pallas_call | solution.py:236
  115.3 8.8 %collective-permute-done.22 = bf16[8,64,512]{2,1,0:T(8,128)(2,1)S(1)} collective-permute-done((bf16[8,64,512]{2,1,0:T(8,128)(2,1)S(1)}, bf16[8,64,512]{2,1,0:T(8,128)(2,1)S(1)}, u32[]{:S(2)}, u32[]{:S(2)}) %collective-permute-start.22) | collective-permute-done | bytes 524320 | tf_op jit(solution)/shard_map/ppermute | solution.py:463
  124.2 3.6 %collective-permute-done.25 = bf16[8,64,512]{2,1,0:T(8,128)(2,1)S(1)} collective-permute-done((bf16[8,64,512]{2,1,0:T(8,128)(2,1)S(1)}, bf16[8,64,512]{2,1,0:T(8,128)(2,1)S(1)}, u32[]{:S(2)}, u32[]{:S(2)}) %collective-permute-start.25) | collective-permute-done | bytes 524320 | tf_op jit(solution)/shard_map/ppermute | solution.py:463
  134.8 3.8 %collective-permute-done.26 = bf16[4,64,512]{2,1,0:T(8,128)(2,1)S(1)} collective-permute-done((bf16[4,64,512]{2,1,0:T(8,128)(2,1)S(1)}, bf16[4,64,512]{2,1,0:T(8,128)(2,1)S(1)}, u32[]{:S(2)}, u32[]{:S(2)}) %collective-permute-start.26) | collective-permute-done | bytes 262176 | tf_op jit(solution)/shard_map/ppermute | solution.py:463
  144.5 2.8 %collective-permute-done.33 = bf16[2,64,512]{2,1,0:T(8,128)(2,1)S(1)} collective-permute-done((bf16[2,64,512]{2,1,0:T(8,128)(2,1)S(1)}, bf16[2,64,512]{2,1,0:T(8,128)(2,1)S(1)}, u32[]{:S(2)}, u32[]{:S(2)}) %collective-permute-start.33) | collective-permute-done | bytes 131104 | tf_op jit(solution)/shard_map/ppermute | solution.py:463
  153.0 2.8 %collective-permute-done.37 = bf16[1,64,512]{2,1,0:T(8,128)(2,1)S(1)} collective-permute-done((bf16[1,64,512]{2,1,0:T(8,128)(2,1)S(1)}, bf16[1,64,512]{2,1,0:T(8,128)(2,1)S(1)}, u32[]{:S(2)}, u32[]{:S(2)}) %collective-permute-start.37) | collective-permute-done | bytes 65568 | tf_op jit(solution)/shard_map/ppermute | solution.py:463
  155.9 18.2 %all_to_all.22 = bf16[8,8,2560]{2,1,0:T(8,128)(2,1)S(1)} all-to-all(bf16[8,8,2560]{2,1,0:T(8,128)(2,1)S(1)} %fusion.11), channel_id=1, replica_groups=mesh['z'=8,'c'=2,'x'=4,'y'=4] {'z'}, dimensions={0} | all-to-all | bytes 655360 | tf_op jit(solution)/shard_map/all_to_all | solution.py:493
  174.2 12.4 %all_to_all.23 = bf16[8,8,2560]{2,1,0:T(8,128)(2,1)S(1)} all-to-all(bf16[8,8,2560]{2,1,0:T(8,128)(2,1)S(1)} %broadcast_in_dim.43), channel_id=1, replica_groups=mesh['z'=8,'c'=2,'x'=4,'y'=4] {'z'}, dimensions={0} | all-to-all | bytes 655360 | tf_op jit(solution)/shard_map/all_to_all | solution.py:493
  186.6 9.6 %collective-permute-start.38 = (bf16[64,2560]{1,0:T(8,128)(2,1)S(1)}, bf16[64,2560]{1,0:T(8,128)(2,1)S(1)}, u32[]{:S(2)}, u32[]{:S(2)}) collective-permute-start(bf16[64,2560]{1,0:T(8,128)(2,1)S(1)} %bitcast.63), channel_id=1, source_target_pairs={{0,16},{16,0},{1,17},{17,1},{2,18},{18,2},{3,19},{19,3},{4,20},{20... | collective-permute-start | bytes 983048 | tf_op jit(solution)/shard_map/ppermute | solution.py:458
  199.6 11.0 %all_to_all.24 = f32[16,8,128]{2,1,0:T(8,128)S(1)} all-to-all(f32[16,8,128]{2,1,0:T(8,128)S(1)} %broadcast_in_dim.44), channel_id=1, replica_groups=mesh['z'=8,'c'=2,'x'=4,'y'=4] {'x','y'}, dimensions={0} | all-to-all | bytes 131072 | tf_op jit(solution)/shard_map/all_to_all | solution.py:493
  212.5 3.6 %update_rows.1 = (f32[64,4096]{1,0:T(8,128)}, f32[64,4096]{1,0:T(8,128)}, f32[64,4096]{1,0:T(8,128)}, f32[64,1024]{1,0:T(8,128)}, f32[64,1024]{1,0:T(8,128)}, /*index=5*/f32[64,1024]{1,0:T(8,128)}) custom-call(s32[2]{0:T(128)S(1)} %pad_add_fusion.place, f32[128,128]{1,0:T(8,128)S(1)} %bitcast.70, bf16[64,2560]{1,0:T(8,128)(2,1)S(1)} %bitcast.64, ...), custom_call_target="tpu_custom_call" | custom-call | flops 1 | bytes 1 | tf_op jit(solution)/shard_map/update_rows/pallas_call | solution.py:236
  (157 shorter events, 71.5 us)
Async XLA Ops:
  1.7 20.8 %collective-permute-start.16 = (bf16[1,64,512]{2,1,0:T(8,128)(2,1)S(1)}, bf16[1,64,512]{2,1,0:T(8,128)(2,1)S(1)}, u32[]{:S(2)}, u32[]{:S(2)}) collective-permute-start(bf16[1,64,512]{2,1,0:T(8,128)(2,1)S(1)} %get-tuple-element.142), channel_id=1, source_target_pairs={{0,12},{4,8},{8,4},{12,0},{1,13},{5,9},{9,5},{13,1},{2,14},{6,10},... | collective-permute-start | bytes 196616 | tf_op jit(solution)/shard_map/ppermute | solution.py:463
  5.1 10.0 %collective-permute-start.2 = (bf16[1,64,512]{2,1,0:T(8,128)(2,1)S(1)}, bf16[1,64,512]{2,1,0:T(8,128)(2,1)S(1)}, u32[]{:S(2)}, u32[]{:S(2)}) collective-permute-start(bf16[1,64,512]{2,1,0:T(8,128)(2,1)S(1)} %get-tuple-element.145), channel_id=1, source_target_pairs={{0,3},{1,2},{2,1},{3,0},{4,7},{5,6},{6,5},{7,4},{8,11},{9,10},{10,... | collective-permute-start | bytes 196616 | tf_op jit(solution)/shard_map/ppermute | solution.py:463
  10.7 44.8 %collective-permute-start = (bf16[2,256,1024]{2,1,0:T(8,128)(2,1)S(1)}, bf16[2,256,1024]{2,1,0:T(8,128)(2,1)}, u32[]{:S(2)}, u32[]{:S(2)}) collective-permute-start(bf16[2,256,1024]{2,1,0:T(8,128)(2,1)S(1)} %fusion.2), channel_id=1, source_target_pairs={{0,16},{16,0},{1,17},{17,1},{2,18},{18,2},{3,19},{19,3},{4,20},{20... | collective-permute-start | bytes 3145736 | tf_op jit(solution)/shard_map/ppermute | solution.py:458
  14.2 7.0 %collective-permute-start.11 = (bf16[2,64,768]{2,1,0:T(8,128)(2,1)S(1)}, bf16[2,64,768]{2,1,0:T(8,128)(2,1)S(1)}, u32[]{:S(2)}, u32[]{:S(2)}) collective-permute-start(bf16[2,64,768]{2,1,0:T(8,128)(2,1)S(1)} %pad_maximum_fusion.12), channel_id=1, source_target_pairs={{0,12},{4,8},{8,4},{12,0},{1,13},{5,9},{9,5},{13,1},{2,14},{6,10},... | collective-permute-start | bytes 589832 | tf_op jit(solution)/shard_map/ppermute | solution.py:463
  15.2 9.2 %collective-permute-start.3 = (bf16[2,64,512]{2,1,0:T(8,128)(2,1)S(1)}, bf16[2,64,512]{2,1,0:T(8,128)(2,1)S(1)}, u32[]{:S(2)}, u32[]{:S(2)}) collective-permute-start(bf16[2,64,512]{2,1,0:T(8,128)(2,1)S(1)} %pad_maximum_fusion.13), channel_id=1, source_target_pairs={{0,4},{4,0},{8,12},{12,8},{1,5},{5,1},{9,13},{13,9},{2,6},{6,2},{1... | collective-permute-start | bytes 393224 | tf_op jit(solution)/shard_map/ppermute | solution.py:463
  18.1 13.3 %collective-permute-start.8 = (bf16[4,64,768]{2,1,0:T(8,128)(2,1)S(1)}, bf16[4,64,768]{2,1,0:T(8,128)(2,1)S(1)}, u32[]{:S(2)}, u32[]{:S(2)}) collective-permute-start(bf16[4,64,768]{2,1,0:T(8,128)(2,1)S(1)} %pad_maximum_fusion.7), channel_id=1, source_target_pairs={{0,12},{4,8},{8,4},{12,0},{1,13},{5,9},{9,5},{13,1},{2,14},{6,10},... | collective-permute-start | bytes 1179656 | tf_op jit(solution)/shard_map/ppermute | solution.py:463
  21.3 10.1 %collective-permute-start.12 = (bf16[4,64,768]{2,1,0:T(8,128)(2,1)S(1)}, bf16[4,64,768]{2,1,0:T(8,128)(2,1)S(1)}, u32[]{:S(2)}, u32[]{:S(2)}) collective-permute-start(bf16[4,64,768]{2,1,0:T(8,128)(2,1)S(1)} %pad_maximum_fusion.8), channel_id=1, source_target_pairs={{0,3},{1,2},{2,1},{3,0},{4,7},{5,6},{6,5},{7,4},{8,11},{9,10},{10,... | collective-permute-start | bytes 1179656 | tf_op jit(solution)/shard_map/ppermute | solution.py:463
  22.5 38.3 %collective-permute-start.1 = (bf16[2,256,1024]{2,1,0:T(8,128)(2,1)}, bf16[2,256,1024]{2,1,0:T(8,128)(2,1)}, u32[]{:S(2)}, u32[]{:S(2)}) collective-permute-start(bf16[2,256,1024]{2,1,0:T(8,128)(2,1)} %broadcast_select_fusion), channel_id=1, source_target_pairs={{0,16},{16,0},{1,17},{17,1},{2,18},{18,2},{3,19},{19,3},{4,20},{20... | collective-permute-start | bytes 3145736 | tf_op jit(solution)/shard_map/ppermute | solution.py:458
  24.3 9.8 %collective-permute-start.17 = (bf16[2,64,512]{2,1,0:T(8,128)(2,1)S(1)}, bf16[2,64,512]{2,1,0:T(8,128)(2,1)S(1)}, u32[]{:S(2)}, u32[]{:S(2)}) collective-permute-start(bf16[2,64,512]{2,1,0:T(8,128)(2,1)S(1)} %pad_maximum_fusion.14), channel_id=1, source_target_pairs={{0,3},{1,2},{2,1},{3,0},{4,7},{5,6},{6,5},{7,4},{8,11},{9,10},{10,... | collective-permute-start | bytes 393224 | tf_op jit(solution)/shard_map/ppermute | solution.py:463
  31.4 31.1 %collective-permute-start.13 = (bf16[8,64,768]{2,1,0:T(8,128)(2,1)S(1)}, bf16[8,64,768]{2,1,0:T(8,128)(2,1)}, u32[]{:S(2)}, u32[]{:S(2)}) collective-permute-start(bf16[8,64,768]{2,1,0:T(8,128)(2,1)S(1)} %pad_maximum_fusion.4.near), channel_id=1, source_target_pairs={{0,4},{4,0},{8,12},{12,8},{1,5},{5,1},{9,13},{13,9},{2,6},{6,2},{1... | collective-permute-start | bytes 2359304 | tf_op jit(solution)/shard_map/ppermute | solution.py:463
  34.2 32.0 %collective-permute-start.9 = (bf16[8,64,768]{2,1,0:T(8,128)(2,1)}, bf16[8,64,768]{2,1,0:T(8,128)(2,1)}, u32[]{:S(2)}, u32[]{:S(2)}) collective-permute-start(bf16[8,64,768]{2,1,0:T(8,128)(2,1)} %pad_maximum_fusion.3.near), channel_id=1, source_target_pairs={{0,3},{1,2},{2,1},{3,0},{4,7},{5,6},{6,5},{7,4},{8,11},{9,10},{10,... | collective-permute-start | bytes 2359304 | tf_op jit(solution)/shard_map/ppermute | solution.py:463
  36.6 15.6 %collective-permute-start.18 = (bf16[4,64,512]{2,1,0:T(8,128)(2,1)S(1)}, bf16[4,64,512]{2,1,0:T(8,128)(2,1)}, u32[]{:S(2)}, u32[]{:S(2)}) collective-permute-start(bf16[4,64,512]{2,1,0:T(8,128)(2,1)S(1)} %pad_maximum_fusion.10), channel_id=1, source_target_pairs={{0,4},{4,0},{8,12},{12,8},{1,5},{5,1},{9,13},{13,9},{2,6},{6,2},{1... | collective-permute-start | bytes 786440 | tf_op jit(solution)/shard_map/ppermute | solution.py:463
  52.2 31.0 %collective-permute-start.5 = (bf16[8,64,512]{2,1,0:T(8,128)(2,1)S(1)}, bf16[8,64,512]{2,1,0:T(8,128)(2,1)}, u32[]{:S(2)}, u32[]{:S(2)}) collective-permute-start(bf16[8,64,512]{2,1,0:T(8,128)(2,1)S(1)} %pad_maximum_fusion.5.near), channel_id=1, source_target_pairs={{0,12},{4,8},{8,4},{12,0},{1,13},{5,9},{9,5},{13,1},{2,14},{6,10},... | collective-permute-start | bytes 1572872 | tf_op jit(solution)/shard_map/ppermute | solution.py:463
  55.5 22.1 %collective-permute-start.19 = (bf16[8,64,512]{2,1,0:T(8,128)(2,1)}, bf16[8,64,512]{2,1,0:T(8,128)(2,1)}, u32[]{:S(2)}, u32[]{:S(2)}) collective-permute-start(bf16[8,64,512]{2,1,0:T(8,128)(2,1)} %pad_maximum_fusion.6.near), channel_id=1, source_target_pairs={{0,1},{1,0},{2,3},{3,2},{4,5},{5,4},{6,7},{7,6},{8,9},{9,8},{10,11... | collective-permute-start | bytes 1572872 | tf_op jit(solution)/shard_map/ppermute | solution.py:463
  70.2 12.9 %collective-permute-start.14 = (bf16[512,512]{1,0:T(8,128)(2,1)S(1)}, bf16[512,512]{1,0:T(8,128)(2,1)S(1)}, u32[]{:S(2)}, u32[]{:S(2)}) collective-permute-start(bf16[512,512]{1,0:T(8,128)(2,1)S(1)} %get-tuple-element.132), channel_id=1, source_target_pairs={{0,16},{16,0},{1,17},{17,1},{2,18},{18,2},{3,19},{19,3},{4,20},{20... | collective-permute-start | bytes 1572872 | tf_op jit(solution)/shard_map/ppermute | solution.py:458
  94.3 8.9 %collective-permute-start.21 = (bf16[512,512]{1,0:T(8,128)(2,1)S(1)}, bf16[512,512]{1,0:T(8,128)(2,1)S(1)}, u32[]{:S(2)}, u32[]{:S(2)}) collective-permute-start(bf16[512,512]{1,0:T(8,128)(2,1)S(1)} %get-tuple-element.130), channel_id=1, source_target_pairs={{0,16},{16,0},{1,17},{17,1},{2,18},{18,2},{3,19},{19,3},{4,20},{20... | collective-permute-start | bytes 1572872 | tf_op jit(solution)/shard_map/ppermute | solution.py:458
  109.4 18.8 %collective-permute-start.24 = (bf16[8,64,768]{2,1,0:T(8,128)(2,1)S(1)}, bf16[8,64,768]{2,1,0:T(8,128)(2,1)S(1)}, u32[]{:S(2)}, u32[]{:S(2)}) collective-permute-start(bf16[8,64,768]{2,1,0:T(8,128)(2,1)S(1)} %get-tuple-element.94), channel_id=1, source_target_pairs={{0,1},{1,0},{2,3},{3,2},{4,5},{5,4},{6,7},{7,6},{8,9},{9,8},{10,11... | collective-permute-start | bytes 2359304 | tf_op jit(solution)/shard_map/ppermute | solution.py:463
  109.6 18.6 %collective-permute-start.23 = (bf16[8,64,768]{2,1,0:T(8,128)(2,1)S(1)}, bf16[8,64,768]{2,1,0:T(8,128)(2,1)S(1)}, u32[]{:S(2)}, u32[]{:S(2)}) collective-permute-start(bf16[8,64,768]{2,1,0:T(8,128)(2,1)S(1)} %get-tuple-element.90), channel_id=1, source_target_pairs={{0,4},{4,0},{8,12},{12,8},{1,5},{5,1},{9,13},{13,9},{2,6},{6,2},{1... | collective-permute-start | bytes 2359304 | tf_op jit(solution)/shard_map/ppermute | solution.py:463
  110.5 13.7 %collective-permute-start.22 = (bf16[8,64,512]{2,1,0:T(8,128)(2,1)S(1)}, bf16[8,64,512]{2,1,0:T(8,128)(2,1)S(1)}, u32[]{:S(2)}, u32[]{:S(2)}) collective-permute-start(bf16[8,64,512]{2,1,0:T(8,128)(2,1)S(1)} %get-tuple-element.84), channel_id=1, source_target_pairs={{0,3},{1,2},{2,1},{3,0},{4,7},{5,6},{6,5},{7,4},{8,11},{9,10},{10,... | collective-permute-start | bytes 1572872 | tf_op jit(solution)/shard_map/ppermute | solution.py:463
  114.0 13.7 %collective-permute-start.25 = (bf16[8,64,512]{2,1,0:T(8,128)(2,1)S(1)}, bf16[8,64,512]{2,1,0:T(8,128)(2,1)S(1)}, u32[]{:S(2)}, u32[]{:S(2)}) collective-permute-start(bf16[8,64,512]{2,1,0:T(8,128)(2,1)S(1)} %get-tuple-element.97), channel_id=1, source_target_pairs={{0,12},{4,8},{8,4},{12,0},{1,13},{5,9},{9,5},{13,1},{2,14},{6,10},... | collective-permute-start | bytes 1572872 | tf_op jit(solution)/shard_map/ppermute | solution.py:463
  130.4 8.9 %collective-permute-start.28 = (bf16[4,64,768]{2,1,0:T(8,128)(2,1)S(1)}, bf16[4,64,768]{2,1,0:T(8,128)(2,1)S(1)}, u32[]{:S(2)}, u32[]{:S(2)}) collective-permute-start(bf16[4,64,768]{2,1,0:T(8,128)(2,1)S(1)} %get-tuple-element.134), channel_id=1, source_target_pairs={{0,4},{4,0},{8,12},{12,8},{1,5},{5,1},{9,13},{13,9},{2,6},{6,2},{1... | collective-permute-start | bytes 1179656 | tf_op jit(solution)/shard_map/ppermute | solution.py:463
  130.6 9.9 %collective-permute-start.27 = (bf16[4,64,768]{2,1,0:T(8,128)(2,1)S(1)}, bf16[4,64,768]{2,1,0:T(8,128)(2,1)S(1)}, u32[]{:S(2)}, u32[]{:S(2)}) collective-permute-start(bf16[4,64,768]{2,1,0:T(8,128)(2,1)S(1)} %get-tuple-element.136), channel_id=1, source_target_pairs={{0,3},{1,2},{2,1},{3,0},{4,7},{5,6},{6,5},{7,4},{8,11},{9,10},{10,... | collective-permute-start | bytes 1179656 | tf_op jit(solution)/shard_map/ppermute | solution.py:463
  131.7 6.8 %collective-permute-start.26 = (bf16[4,64,512]{2,1,0:T(8,128)(2,1)S(1)}, bf16[4,64,512]{2,1,0:T(8,128)(2,1)S(1)}, u32[]{:S(2)}, u32[]{:S(2)}) collective-permute-start(bf16[4,64,512]{2,1,0:T(8,128)(2,1)S(1)} %get-tuple-element.140), channel_id=1, source_target_pairs={{0,12},{4,8},{8,4},{12,0},{1,13},{5,9},{9,5},{13,1},{2,14},{6,10},... | collective-permute-start | bytes 786440 | tf_op jit(solution)/shard_map/ppermute | solution.py:463
  186.6 10.9 %collective-permute-start.38 = (bf16[64,2560]{1,0:T(8,128)(2,1)S(1)}, bf16[64,2560]{1,0:T(8,128)(2,1)S(1)}, u32[]{:S(2)}, u32[]{:S(2)}) collective-permute-start(bf16[64,2560]{1,0:T(8,128)(2,1)S(1)} %bitcast.63), channel_id=1, source_target_pairs={{0,16},{16,0},{1,17},{17,1},{2,18},{18,2},{3,19},{19,3},{4,20},{20... | collective-permute-start | bytes 983048 | tf_op jit(solution)/shard_map/ppermute | solution.py:458
  (27 other events, 347.9 us)
where the time goes:
time: 217 us; the launch traced here: 216 us
  waiting for transfers between devices  57.4 us (26%)
  starting transfers between devices  52 us (24%)
  Pallas kernels  41.8 us (19%)
  blocking collectives  41.5 us (19%)
  other arithmetic  12.8 us (6%)
  local copies, waits for them, and re-layouts  7.94 us (4%)
  between operations  2.75 us (1%)
    ppermute x32, waiting for transfers between devices, over_link(): return lax.ppermute(values, axis, [(i, i ^ mask) for i in range(4)])  53.9 us
    pallas_call x12, Pallas kernels, call(): pl.pallas_call(kernel, grid_spec=pltpu.PrefetchScalarGridSpec(num_scalar_...  41.8 us
    all_to_all x3, blocking collectives, exchange(): return lax.all_to_all(blocks, axes, 0, 0, tiled=True)  41.5 us
    ppermute x32, starting transfers between devices, over_link(): return lax.ppermute(values, axis, [(i, i ^ mask) for i in range(4)])  32.2 us
    ppermute x7, starting transfers between devices, swap_cores(): return lax.ppermute(values, 'c', SWAP)  19.9 us
  transfers between devices with their start and end apart: 39, of which 20 were waited for; matrix products, arithmetic and copies ran while one was open for 7% of the time, Pallas kernels for 11%

commit v1 on v0

--- a/solution.py
+++ b/solution.py
@@ -22,8 +22,8 @@
 OWN = ("x", "y")
 SWAP = ((0, 1), (1, 0))
 
-LINKS = (("x", 1), ("y", 1), ("x", 3), ("y", 3))
-LINK_MASKS = (0b0100, 0b0001, 0b1100, 0b0011)
+DIRECT = ("x", "y", "x", "y")
+STEPS = ((("y", 1), ("y", 3)), (("x", 1), ("x", 3)), (("y", 3), ("y", 1)), (("x", 3), ("x", 1)))
 
 
 def rms_scale(values):
@@ -63,21 +63,14 @@
 
 
 def relative_slot(mask, turn):
-    x_far, x_near = (mask >> 3) & 1, ((mask >> 3) ^ (mask >> 2)) & 1
-    y_far, y_near = (mask >> 1) & 1, ((mask >> 1) ^ mask) & 1
-    bits = (x_near, y_near, x_far, y_far)
-    slot = 0
-    for step in range(4):
-        slot = slot + (bits[(turn + step) % 4] << step)
-    return slot
+    direct, other = (mask >> 2, mask & 3) if turn % 2 == 0 else (mask & 3, mask >> 2)
+    high, odd = other >> 1, (other >> 1) ^ (other & 1)
+    first, second = (odd, high) if turn < 2 else (high, odd)
+    return direct + 4 * first + 8 * second
 
 
 def owner_mask(slot, turn):
-    mask = 0
-    for step in range(4):
-        if slot >> step & 1:
-            mask ^= LINK_MASKS[(turn + step) % 4]
-    return mask
+    return next(mask for mask in range(16) if relative_slot(mask, turn) == slot)
 
 
 def place_rows(turn, own, near, far, weight):
@@ -458,31 +451,49 @@
     return lax.ppermute(values, "c", SWAP)
 
 
-def over_link(values, link):
-    axis, mask = LINKS[link % 4]
+def over_link(values, axis, mask):
     return lax.ppermute(values, axis, [(i, i ^ mask) for i in range(4)])
 
 
-def gather_parts(parts):
-    held = [part[None] for part in parts]
-    for step in range(3):
-        got = [over_link(part, turn + step) for turn, part in enumerate(held)]
-        held = [jnp.concatenate(pair, axis=0) for pair in zip(held, got)]
-    return [(part, over_link(part, turn + 3)) for turn, part in enumerate(held)]
-
-
-def add_halves(mine, got):
-    return (mine.astype(jnp.float32) + got.astype(jnp.float32)).astype(jnp.bfloat16)
+def direct_round(blocks_of, groups):
+    got = [[None] * 4, [None] * 4]
+    for mask in (1, 3, 2):
+        for group, axis in enumerate(("x", "y")):
+            got[group][mask] = over_link(blocks_of(groups[group], mask), axis, mask)
+    return got
+
+
+def gather_parts(parts, beside):
+    groups = [jnp.concatenate([parts[0], parts[2]], axis=1), jnp.concatenate([parts[1], parts[3]], axis=1)]
+    got = direct_round(lambda group, mask: group, groups)
+    for group, mine in zip(got, groups):
+        group[0] = mine
+    got = lax.optimization_barrier(got)
+    held = []
+    for turn in range(4):
+        width = parts[turn % 2].shape[1]
+        cut = slice(0, width) if turn < 2 else slice(width, None)
+        held.append(jnp.stack([block[:, cut] for block in got[turn % 2]]))
+    got = [over_link(part, *STEPS[turn][0]) for turn, part in enumerate(held)]
+    held, got, beside = lax.optimization_barrier((held, got, beside))
+    held = [jnp.concatenate(pair, axis=0) for pair in zip(held, got)]
+    return [(part, over_link(part, *STEPS[turn][1])) for turn, part in enumerate(held)], beside
+
+
+def add_blocks(*blocks):
+    return sum(block.astype(jnp.float32) for block in blocks).astype(jnp.bfloat16)
 
 
 def scatter_parts(pairs):
-    for step in (3, 2, 1, 0):
-        got = [over_link(far, turn + step) for turn, (_, far) in enumerate(pairs)]
+    for step in (1, 0):
+        got = [over_link(far, *STEPS[turn][step]) for turn, (_, far) in enumerate(pairs)]
         mine, got = lax.optimization_barrier(([near for near, _ in pairs], got))
-        held = [add_halves(*pair) for pair in zip(mine, got)]
+        held = [add_blocks(*pair) for pair in zip(mine, got)]
         if step:
             pairs = [jnp.split(part, 2, axis=0) for part in held]
-    return [part[0] for part in held]
+    groups = [jnp.concatenate([held[0], held[2]], axis=2), jnp.concatenate([held[1], held[3]], axis=2)]
+    got = direct_round(lambda group, mask: group[mask], groups)
+    return [add_blocks(group[0], *blocks[1:]) for group, blocks in zip(groups, got)]
 
 
 def after(value, done):
@@ -520,15 +531,6 @@
         for part in range(4)
     ]
     mine_out = lax.dynamic_slice_in_dim(weight_out, core * half, half, axis=1)
-    (q_near, q_far), (k_near, k_far), (v_near, v_far), (g_near, g_far) = gather_parts(
-        [
-            jnp.concatenate([mine[2], mine_out[:, :quarter]], axis=1),
-            jnp.concatenate([mine[3], mine_out[:, quarter:]], axis=1),
-            mine[1],
-            mine[0],
-        ]
-    )
-
     normed = (rms_scale(tokens.astype(jnp.float32)) * norm_gain).astype(jnp.bfloat16)
     row_index = jnp.arange(rows, dtype=jnp.int32)
     live = row_index[None, :] < lengths[:, None]
@@ -536,9 +538,17 @@
     normed = jnp.concatenate([normed, swap_cores(normed)], axis=0)
     masked = jnp.concatenate([masked, swap_cores(masked)], axis=0)
     lengths = jnp.concatenate([lengths, swap_cores(lengths)], axis=0)
-    normed, masked, normed_t = lax.optimization_barrier(
-        (normed, masked, normed.reshape(-1, model_width).T)
-    )
+    normed_t = normed.reshape(-1, model_width).T
+    parts, (normed, masked, lengths, normed_t) = gather_parts(
+        [
+            jnp.concatenate([mine[2], mine_out[:, :quarter]], axis=1),
+            jnp.concatenate([mine[3], mine_out[:, quarter:]], axis=1),
+            mine[1],
+            mine[0],
+        ],
+        (normed, masked, lengths, normed_t),
+    )
+    (q_near, q_far), (k_near, k_far), (v_near, v_far), (g_near, g_far) = parts
 
     queries, out_first = project(0, place, normed, q_near, q_far, half)
     keys_in, out_second = project(1, place, normed, k_near, k_far, half)
@@ -570,9 +580,17 @@
     term_q = term(2, place, owned, normed_t, flat(grad_queries), (outer[0], outer_recv, 1))
     grad_keys = after(grad_keys, term_q)
     term_k = term(3, place, owned, normed_t, flat(grad_keys))
-    part_g, part_v, part_q, part_k = scatter_parts([term_g, term_v, term_q, term_k])
+    part_gq, part_vk = scatter_parts([term_g, term_v, term_q, term_k])
+    wide = half + quarter
     part = jnp.concatenate(
-        [part_g, part_v[:, :half], part_q[:, :half], part_k, part_v[:, half:], part_q[:, half:]],
+        [
+            part_gq[:, :half],
+            part_vk[:, :half],
+            part_gq[:, half : 2 * half],
+            part_vk[:, wide:],
+            part_vk[:, half:wide],
+            part_gq[:, 2 * half :],
+        ],
         axis=1,
     )
 

time: 217 us -> 198 us (0.912)
  waiting for transfers between devices: 57.4 us -> 42.4 us
  local copies, waits for them, and re-layouts: 7.94 us -> 14.8 us
  starting transfers between devices: 52 us -> 48 us
  other arithmetic: 12.8 us -> 9.49 us
  Pallas kernels: 41.8 us -> 39.1 us
    ppermute x32 -> x28, waiting for transfers between devices: 53.9 us -> 40 us  [over_link(): return lax.ppermute(values, axis, [(i, i ^ mask) for i in range(4)])]
    concatenate x1 -> x5, local copies, waits for them, and re-layouts: 0.01 us -> 4.73 us  [the longest x4 4.73 us: gather_parts(): held = [jnp.concatenate(pair, axis=0) for pair in zip(held, got)]]
    ppermute x7, starting transfers between devices: 19.9 us -> 15.6 us  [swap_cores(): return lax.ppermute(values, 'c', SWAP)]
    concatenate x12 -> x2, other arithmetic: 3.09 us -> 0.02 us  [the longest x1 0.01 us: gather_parts(): jnp.concatenate([parts[0], parts[2]], axis=1)]
    pallas_call x12, Pallas kernels: 41.8 us -> 39.1 us  [call(): pl.pallas_call(kernel, grid_spec=pltpu.PrefetchScalarGridSpec(num_scalar_...]
    unnamed x27 -> x35, local copies, waits for them, and re-layouts: 3 us -> 5.05 us
    ppermute x32 -> x28, starting transfers between devices: 32.2 us -> 32.4 us  [over_link(): return lax.ppermute(values, axis, [(i, i ^ mask) for i in range(4)])]
  transfers between devices with their start and end apart: 39 -> 35, of which waited for: 20 -> 15; matrix products, arithmetic and copies ran while one was open for 7% -> 8% of each run, Pallas kernels for 11% -> 11%
where the time goes in v1:
time: 198 us
  starting transfers between devices  48 us (24%)
  waiting for transfers between devices  42.4 us (21%)
  blocking collectives  41 us (21%)
  Pallas kernels  39.1 us (20%)
  local copies, waits for them, and re-layouts  14.8 us (7%)
  other arithmetic  9.49 us (5%)
  between operations  2.76 us (1%)
    all_to_all x3, blocking collectives, exchange(): return lax.all_to_all(blocks, axes, 0, 0, tiled=True)  41 us
    ppermute x28, waiting for transfers between devices, over_link(): return lax.ppermute(values, axis, [(i, i ^ mask) for i in range(4)])  40 us
    pallas_call x12, Pallas kernels, call(): pl.pallas_call(kernel, grid_spec=pltpu.PrefetchScalarGridSpec(num_scalar_...  39.1 us
    ppermute x28, starting transfers between devices, over_link(): return lax.ppermute(values, axis, [(i, i ^ mask) for i in range(4)])  32.4 us
    ppermute x7, starting transfers between devices, swap_cores(): return lax.ppermute(values, 'c', SWAP)  15.6 us
    unnamed x35, local copies, waits for them, and re-layouts  5.05 us
    concatenate x4, local copies, waits for them, and re-layouts, gather_parts(): held = [jnp.concatenate(pair, axis=0) for pair in zip(held, got)]  4.73 us
  transfers between devices with their start and end apart: 35, of which 15 were waited for; matrix products, arithmetic and copies ran while one was open for 8% of the time, Pallas kernels for 11%

profile of v1, /device:TPU:1, one launch (start us, length us, event | category | flops | bytes accessed | tf_op | source)
XLA Modules:
  0.0 197.5 jit_solution(2800447315321643704)
XLA Ops:
  2.6 3.4 %collective-permute-start.2 = (bf16[64,1280]{1,0:T(8,128)(2,1)S(1)}, bf16[64,1280]{1,0:T(8,128)(2,1)S(1)}, u32[]{:S(2)}, u32[]{:S(2)}) collective-permute-start(bf16[64,1280]{1,0:T(8,128)(2,1)S(1)} %pad_maximum_fusion.9), channel_id=1, source_target_pairs={{0,12},{4,8},{8,4},{12,0},{1,13},{5,9},{9,5},{13,1},{2,14},{6,10},... | collective-permute-start | bytes 491528 | tf_op jit(solution)/shard_map/ppermute | solution.py:455
  6.7 3.3 %collective-permute-start.12 = (s32[2]{0:T(128)}, s32[2]{0:T(128)S(1)}, u32[]{:S(2)}, u32[]{:S(2)}) collective-permute-start(s32[2]{0:T(128)} %param.12), channel_id=1, source_target_pairs={{0,16},{16,0},{1,17},{17,1},{2,18},{18,2},{3,19},{19,3},{4,20},{20... | collective-permute-start | bytes 32 | tf_op jit(solution)/shard_map/ppermute | solution.py:451
  17.5 2.6 %collective-permute-done.4 = bf16[64,1280]{1,0:T(8,128)(2,1)S(1)} collective-permute-done((bf16[64,1280]{1,0:T(8,128)(2,1)S(1)}, bf16[64,1280]{1,0:T(8,128)(2,1)S(1)}, u32[]{:S(2)}, u32[]{:S(2)}) %collective-permute-start.4) | collective-permute-done | bytes 163872 | tf_op jit(solution)/shard_map/ppermute | solution.py:455
  20.2 2.7 %collective-permute-done.3 = bf16[64,1280]{1,0:T(8,128)(2,1)S(1)} collective-permute-done((bf16[64,1280]{1,0:T(8,128)(2,1)S(1)}, bf16[64,1280]{1,0:T(8,128)(2,1)S(1)}, u32[]{:S(2)}, u32[]{:S(2)}) %collective-permute-start.3) | collective-permute-done | bytes 163872 | tf_op jit(solution)/shard_map/ppermute | solution.py:455
  30.4 3.1 %pad_maximum_fusion.1.masked = bf16[4,256,1024]{2,1,0:T(8,128)(2,1)} fusion(bf16[2,256,1024]{2,1,0:T(8,128)(2,1)} %collective-permute-done.11, bf16[2,256,1024]{2,1,0:T(8,128)(2,1)} %broadcast_select_fusion), kind=kLoop, calls=%fused_computation.6 | loop fusion | flops 1048576 | bytes 4194304 | tf_op jit(solution)/shard_map/concatenate | solution.py:539
  44.5 9.8 %collective-permute-done.14.far = bf16[8,64,768]{2,1,0:T(8,128)(2,1)} collective-permute-done((bf16[8,64,768]{2,1,0:T(8,128)(2,1)}, bf16[8,64,768]{2,1,0:T(8,128)(2,1)}, u32[]{:S(2)}, u32[]{:S(2)}) %collective-permute-start.14) | collective-permute-done | bytes 786464 | tf_op jit(solution)/shard_map/ppermute | solution.py:455
  54.3 3.9 %project.2 = (f32[4,256,512]{2,1,0:T(8,128)S(1)}, bf16[1024,256]{1,0:T(8,128)(2,1)S(1)}) custom-call(s32[2]{0:T(128)S(1)} %pad_add_fusion.place, bf16[4,256,1024]{2,1,0:T(8,128)(2,1)S(1)} %pad_maximum_fusion.normed, bf16[8,64,768]{2,1,0:T(8,128)(2,1)} %constant_dynamic-update-slice_fusion.2.near, bf16[8,64,768]{2,1,0:T(8,128)(2,1)} %collective-permute-done.14.far), custom_call_target="tpu_custom_call" | custom-call | flops 1 | bytes 1 | tf_op jit(solution)/shard_map/project/pallas_call | solution.py:229
  58.3 3.7 %project.3 = (f32[4,256,512]{2,1,0:T(8,128)S(1)}, bf16[1024,256]{1,0:T(8,128)(2,1)S(1)}) custom-call(s32[2]{0:T(128)S(1)} %pad_add_fusion.place, bf16[4,256,1024]{2,1,0:T(8,128)(2,1)S(1)} %pad_maximum_fusion.normed, bf16[8,64,768]{2,1,0:T(8,128)(2,1)S(1)} %constant_dynamic-update-slice_fusion.4.near, bf16[8,64,768]{2,1,0:T(8,128)(2,1)} %collective-permute-done.15.far), custom_call_target="tpu_custom_call" | custom-call | flops 1 | bytes 1 | tf_op jit(solution)/shard_map/project/pallas_call | solution.py:229
  62.1 3.4 %collective-permute-start.16 = (bf16[512,512]{1,0:T(8,128)(2,1)S(1)}, bf16[512,512]{1,0:T(8,128)(2,1)S(1)}, u32[]{:S(2)}, u32[]{:S(2)}) collective-permute-start(bf16[512,512]{1,0:T(8,128)(2,1)S(1)} %get-tuple-element.134), channel_id=1, source_target_pairs={{0,16},{16,0},{1,17},{17,1},{2,18},{18,2},{3,19},{19,3},{4,20},{20... | collective-permute-start | bytes 1572872 | tf_op jit(solution)/shard_map/ppermute | solution.py:451
  65.5 4.3 %attention_forward.1 = (f32[4,256,512]{2,1,0:T(8,128)S(1)}, f32[4,2,256,256]{3,2,1,0:T(8,128)S(1)}, f32[4,256,512]{2,1,0:T(8,128)S(1)}) custom-call(s32[2]{0:T(128)S(1)} %pad_add_fusion.place, s32[4]{0:T(128)S(1)} %pad_add_fusion.1.lengths, bf16[4,256,1024]{2,1,0:T(8,128)(2,1)S(1)} %pad_maximum_fusion.normed, ...), custom_call_target="tpu_custom_call" | custom-call | flops 1 | bytes 1 | tf_op jit(solution)/shard_map/attention_forward/pallas_call | solution.py:229
  69.8 4.0 %gating_forward.1 = (f32[4,256,512]{2,1,0:T(8,128)S(1)}, bf16[4,256,512]{2,1,0:T(8,128)(2,1)S(1)}, f32[4,256,128]{2,1,0:T(8,128)S(1)}) custom-call(s32[2]{0:T(128)S(1)} %pad_add_fusion.place, bf16[4,256,1024]{2,1,0:T(8,128)(2,1)S(1)} %pad_maximum_fusion.normed, bf16[8,64,512]{2,1,0:T(8,128)(2,1)S(1)} %constant_dynamic-update-slice_fusion.near, ...), custom_call_target="tpu_custom_call" | custom-call | flops 1 | bytes 1 | tf_op jit(solution)/shard_map/gating_forward/pallas_call | solution.py:229
  81.3 2.6 %term.4 = (bf16[8,64,512]{2,1,0:T(8,128)(2,1)S(1)}, bf16[8,64,512]{2,1,0:T(8,128)(2,1)S(1)}) custom-call(s32[2]{0:T(128)S(1)} %pad_add_fusion.place, bf16[1024,1024]{1,0:T(8,128)(2,1)S(1)} %bitcast.77, bf16[1024,512]{1,0:T(8,128)(2,1)S(1)} %bitcast.88), custom_call_target="tpu_custom_call" | custom-call | flops 1 | bytes 1 | tf_op jit(solution)/shard_map/term/pallas_call | solution.py:229
  83.9 4.6 %attention_back.1 = (bf16[4,256,512]{2,1,0:T(8,128)(2,1)S(1)}, bf16[4,256,512]{2,1,0:T(8,128)(2,1)S(1)}, bf16[4,256,512]{2,1,0:T(8,128)(2,1)S(1)}) custom-call(s32[4]{0:T(128)S(1)} %pad_add_fusion.1.lengths, f32[4,256,512]{2,1,0:T(8,128)S(1)} %get-tuple-element.99.values_in, f32[4,256,512]{2,1,0:T(8,128)S(1)} %get-tuple-element.91.queries_in, ...), custom_call_target="tpu_custom_call" | custom-call | flops 1 | bytes 1 | tf_op jit(solution)/shard_map/attention_back/pallas_call | solution.py:229
  88.5 3.0 %term.5 = (bf16[8,64,768]{2,1,0:T(8,128)(2,1)S(1)}, bf16[8,64,768]{2,1,0:T(8,128)(2,1)S(1)}) custom-call(s32[2]{0:T(128)S(1)} %pad_add_fusion.place, bf16[1024,1024]{1,0:T(8,128)(2,1)S(1)} %bitcast.78, bf16[1024,512]{1,0:T(8,128)(2,1)S(1)} %bitcast.85, bf16[512,512]{1,0:T(8,128)(2,1)S(1)} %get-tuple-element.133.refs_0_, ...), custom_call_target="tpu_custom_call" | custom-call | flops 1 | bytes 1 | tf_op jit(solution)/shard_map/term/pallas_call | solution.py:229
  91.5 3.0 %term.6 = (bf16[8,64,768]{2,1,0:T(8,128)(2,1)S(1)}, bf16[8,64,768]{2,1,0:T(8,128)(2,1)S(1)}) custom-call(s32[2]{0:T(128)S(1)} %pad_add_fusion.place, bf16[1024,1024]{1,0:T(8,128)(2,1)S(1)} %bitcast.79, bf16[1024,512]{1,0:T(8,128)(2,1)S(1)} %bitcast.84, bf16[512,512]{1,0:T(8,128)(2,1)S(1)} %get-tuple-element.133.refs_0_, ...), custom_call_target="tpu_custom_call" | custom-call | flops 1 | bytes 1 | tf_op jit(solution)/shard_map/term/pallas_call | solution.py:229
  101.4 9.5 %collective-permute-done.20 = bf16[8,64,512]{2,1,0:T(8,128)(2,1)S(1)} collective-permute-done((bf16[8,64,512]{2,1,0:T(8,128)(2,1)S(1)}, bf16[8,64,512]{2,1,0:T(8,128)(2,1)S(1)}, u32[]{:S(2)}, u32[]{:S(2)}) %collective-permute-start.20) | collective-permute-done | bytes 524320 | tf_op jit(solution)/shard_map/ppermute | solution.py:455
  117.0 2.7 %collective-permute-start.26 = (bf16[4,64,768]{2,1,0:T(8,128)(2,1)S(1)}, bf16[4,64,768]{2,1,0:T(8,128)(2,1)S(1)}, u32[]{:S(2)}, u32[]{:S(2)}) collective-permute-start(bf16[4,64,768]{2,1,0:T(8,128)(2,1)S(1)} %get-tuple-element.136), channel_id=1, source_target_pairs={{0,3},{1,2},{2,1},{3,0},{4,7},{5,6},{6,5},{7,4},{8,11},{9,10},{10,... | collective-permute-start | bytes 1179656 | tf_op jit(solution)/shard_map/ppermute | solution.py:455
  122.1 4.8 %collective-permute-done.27 = bf16[4,64,512]{2,1,0:T(8,128)(2,1)S(1)} collective-permute-done((bf16[4,64,512]{2,1,0:T(8,128)(2,1)S(1)}, bf16[4,64,512]{2,1,0:T(8,128)(2,1)S(1)}, u32[]{:S(2)}, u32[]{:S(2)}) %collective-permute-start.27) | collective-permute-done | bytes 262176 | tf_op jit(solution)/shard_map/ppermute | solution.py:455
  134.8 3.5 %collective-permute-done.29 = bf16[64,1280]{1,0:T(8,128)(2,1)S(1)} collective-permute-done((bf16[64,1280]{1,0:T(8,128)(2,1)S(1)}, bf16[64,1280]{1,0:T(8,128)(2,1)S(1)}, u32[]{:S(2)}, u32[]{:S(2)}) %collective-permute-start.29) | collective-permute-done | bytes 163872 | tf_op jit(solution)/shard_map/ppermute | solution.py:455
  139.9 17.8 %all_to_all.25 = bf16[8,8,2560]{2,1,0:T(8,128)(2,1)S(1)} all-to-all(bf16[8,8,2560]{2,1,0:T(8,128)(2,1)S(1)} %bitcast.91), channel_id=1, replica_groups=mesh['z'=8,'c'=2,'x'=4,'y'=4] {'z'}, dimensions={0} | all-to-all | bytes 655360 | tf_op jit(solution)/shard_map/all_to_all | solution.py:504
  157.7 12.4 %all_to_all.26 = bf16[8,8,2560]{2,1,0:T(8,128)(2,1)S(1)} all-to-all(bf16[8,8,2560]{2,1,0:T(8,128)(2,1)S(1)} %broadcast_in_dim.16), channel_id=1, replica_groups=mesh['z'=8,'c'=2,'x'=4,'y'=4] {'z'}, dimensions={0} | all-to-all | bytes 655360 | tf_op jit(solution)/shard_map/all_to_all | solution.py:504
  170.2 7.5 %collective-permute-start.34 = (bf16[64,2560]{1,0:T(8,128)(2,1)S(1)}, bf16[64,2560]{1,0:T(8,128)(2,1)S(1)}, u32[]{:S(2)}, u32[]{:S(2)}) collective-permute-start(bf16[64,2560]{1,0:T(8,128)(2,1)S(1)} %bitcast.82), channel_id=1, source_target_pairs={{0,16},{16,0},{1,17},{17,1},{2,18},{18,2},{3,19},{19,3},{4,20},{20... | collective-permute-start | bytes 983048 | tf_op jit(solution)/shard_map/ppermute | solution.py:451
  181.0 10.7 %all_to_all.27 = f32[16,8,128]{2,1,0:T(8,128)S(1)} all-to-all(f32[16,8,128]{2,1,0:T(8,128)S(1)} %broadcast_in_dim.28), channel_id=1, replica_groups=mesh['z'=8,'c'=2,'x'=4,'y'=4] {'x','y'}, dimensions={0} | all-to-all | bytes 131072 | tf_op jit(solution)/shard_map/all_to_all | solution.py:504
  193.7 3.6 %update_rows.1 = (f32[64,4096]{1,0:T(8,128)}, f32[64,4096]{1,0:T(8,128)}, f32[64,4096]{1,0:T(8,128)}, f32[64,1024]{1,0:T(8,128)}, f32[64,1024]{1,0:T(8,128)}, /*index=5*/f32[64,1024]{1,0:T(8,128)}) custom-call(s32[2]{0:T(128)S(1)} %pad_add_fusion.place, f32[128,128]{1,0:T(8,128)S(1)} %bitcast.89, bf16[64,2560]{1,0:T(8,128)(2,1)S(1)} %bitcast.83, ...), custom_call_target="tpu_custom_call" | custom-call | flops 1 | bytes 1 | tf_op jit(solution)/shard_map/update_rows/pallas_call | solution.py:229
  (151 shorter events, 64.6 us)
Async XLA Ops:
  2.6 10.8 %collective-permute-start.2 = (bf16[64,1280]{1,0:T(8,128)(2,1)S(1)}, bf16[64,1280]{1,0:T(8,128)(2,1)S(1)}, u32[]{:S(2)}, u32[]{:S(2)}) collective-permute-start(bf16[64,1280]{1,0:T(8,128)(2,1)S(1)} %pad_maximum_fusion.9), channel_id=1, source_target_pairs={{0,12},{4,8},{8,4},{12,0},{1,13},{5,9},{9,5},{13,1},{2,14},{6,10},... | collective-permute-start | bytes 491528 | tf_op jit(solution)/shard_map/ppermute | solution.py:455
  6.0 10.6 %collective-permute-start.1 = (bf16[64,1280]{1,0:T(8,128)(2,1)S(1)}, bf16[64,1280]{1,0:T(8,128)(2,1)S(1)}, u32[]{:S(2)}, u32[]{:S(2)}) collective-permute-start(bf16[64,1280]{1,0:T(8,128)(2,1)S(1)} %pad_maximum_fusion.9), channel_id=1, source_target_pairs={{0,8},{4,12},{8,0},{12,4},{1,9},{5,13},{9,1},{13,5},{2,10},{6,14},... | collective-permute-start | bytes 491528 | tf_op jit(solution)/shard_map/ppermute | solution.py:455
  6.5 10.9 %collective-permute-start = (bf16[64,1280]{1,0:T(8,128)(2,1)S(1)}, bf16[64,1280]{1,0:T(8,128)(2,1)S(1)}, u32[]{:S(2)}, u32[]{:S(2)}) collective-permute-start(bf16[64,1280]{1,0:T(8,128)(2,1)S(1)} %pad_maximum_fusion.9), channel_id=1, source_target_pairs={{0,4},{4,0},{8,12},{12,8},{1,5},{5,1},{9,13},{13,9},{2,6},{6,2},{1... | collective-permute-start | bytes 491528 | tf_op jit(solution)/shard_map/ppermute | solution.py:455
  13.5 9.5 %collective-permute-start.3 = (bf16[64,1280]{1,0:T(8,128)(2,1)S(1)}, bf16[64,1280]{1,0:T(8,128)(2,1)S(1)}, u32[]{:S(2)}, u32[]{:S(2)}) collective-permute-start(bf16[64,1280]{1,0:T(8,128)(2,1)S(1)} %pad_maximum_fusion.10), channel_id=1, source_target_pairs={{0,1},{1,0},{2,3},{3,2},{4,5},{5,4},{6,7},{7,6},{8,9},{9,8},{10,11... | collective-permute-start | bytes 491528 | tf_op jit(solution)/shard_map/ppermute | solution.py:455
  16.6 13.9 %collective-permute-start.11 = (bf16[2,256,1024]{2,1,0:T(8,128)(2,1)}, bf16[2,256,1024]{2,1,0:T(8,128)(2,1)}, u32[]{:S(2)}, u32[]{:S(2)}) collective-permute-start(bf16[2,256,1024]{2,1,0:T(8,128)(2,1)} %broadcast_select_fusion), channel_id=1, source_target_pairs={{0,16},{16,0},{1,17},{17,1},{2,18},{18,2},{3,19},{19,3},{4,20},{20... | collective-permute-start | bytes 3145736 | tf_op jit(solution)/shard_map/ppermute | solution.py:451
  17.4 8.2 %collective-permute-start.10 = (bf16[2,256,1024]{2,1,0:T(8,128)(2,1)S(1)}, bf16[2,256,1024]{2,1,0:T(8,128)(2,1)S(1)}, u32[]{:S(2)}, u32[]{:S(2)}) collective-permute-start(bf16[2,256,1024]{2,1,0:T(8,128)(2,1)S(1)} %fusion.2), channel_id=1, source_target_pairs={{0,16},{16,0},{1,17},{17,1},{2,18},{18,2},{3,19},{19,3},{4,20},{20... | collective-permute-start | bytes 3145736 | tf_op jit(solution)/shard_map/ppermute | solution.py:451
  23.0 10.5 %collective-permute-start.9 = (bf16[4,64,512]{2,1,0:T(8,128)(2,1)S(1)}, bf16[4,64,512]{2,1,0:T(8,128)(2,1)}, u32[]{:S(2)}, u32[]{:S(2)}) collective-permute-start(bf16[4,64,512]{2,1,0:T(8,128)(2,1)S(1)} %pad_maximum_fusion.6), channel_id=1, source_target_pairs={{0,12},{4,8},{8,4},{12,0},{1,13},{5,9},{9,5},{13,1},{2,14},{6,10},... | collective-permute-start | bytes 786440 | tf_op jit(solution)/shard_map/ppermute | solution.py:455
  24.1 9.5 %collective-permute-start.7 = (bf16[4,64,768]{2,1,0:T(8,128)(2,1)S(1)}, bf16[4,64,768]{2,1,0:T(8,128)(2,1)}, u32[]{:S(2)}, u32[]{:S(2)}) collective-permute-start(bf16[4,64,768]{2,1,0:T(8,128)(2,1)S(1)} %pad_maximum_fusion.4), channel_id=1, source_target_pairs={{0,4},{4,0},{8,12},{12,8},{1,5},{5,1},{9,13},{13,9},{2,6},{6,2},{1... | collective-permute-start | bytes 1179656 | tf_op jit(solution)/shard_map/ppermute | solution.py:455
  24.3 9.3 %collective-permute-start.6 = (bf16[4,64,768]{2,1,0:T(8,128)(2,1)S(1)}, bf16[4,64,768]{2,1,0:T(8,128)(2,1)}, u32[]{:S(2)}, u32[]{:S(2)}) collective-permute-start(bf16[4,64,768]{2,1,0:T(8,128)(2,1)S(1)} %pad_maximum_fusion.3), channel_id=1, source_target_pairs={{0,1},{1,0},{2,3},{3,2},{4,5},{5,4},{6,7},{7,6},{8,9},{9,8},{10,11... | collective-permute-start | bytes 1179656 | tf_op jit(solution)/shard_map/ppermute | solution.py:455
  25.6 7.9 %collective-permute-start.8 = (bf16[4,64,512]{2,1,0:T(8,128)(2,1)S(1)}, bf16[4,64,512]{2,1,0:T(8,128)(2,1)}, u32[]{:S(2)}, u32[]{:S(2)}) collective-permute-start(bf16[4,64,512]{2,1,0:T(8,128)(2,1)S(1)} %pad_maximum_fusion.5), channel_id=1, source_target_pairs={{0,3},{1,2},{2,1},{3,0},{4,7},{5,6},{6,5},{7,4},{8,11},{9,10},{10,... | collective-permute-start | bytes 786440 | tf_op jit(solution)/shard_map/ppermute | solution.py:455
  36.2 18.1 %collective-permute-start.14 = (bf16[8,64,768]{2,1,0:T(8,128)(2,1)}, bf16[8,64,768]{2,1,0:T(8,128)(2,1)}, u32[]{:S(2)}, u32[]{:S(2)}) collective-permute-start(bf16[8,64,768]{2,1,0:T(8,128)(2,1)} %constant_dynamic-update-slice_fusion.2.near), channel_id=1, source_target_pairs={{0,3},{1,2},{2,1},{3,0},{4,7},{5,6},{6,5},{7,4},{8,11},{9,10},{10,... | collective-permute-start | bytes 2359304 | tf_op jit(solution)/shard_map/ppermute | solution.py:455
  39.7 18.6 %collective-permute-start.15 = (bf16[8,64,768]{2,1,0:T(8,128)(2,1)S(1)}, bf16[8,64,768]{2,1,0:T(8,128)(2,1)}, u32[]{:S(2)}, u32[]{:S(2)}) collective-permute-start(bf16[8,64,768]{2,1,0:T(8,128)(2,1)S(1)} %constant_dynamic-update-slice_fusion.4.near), channel_id=1, source_target_pairs={{0,12},{4,8},{8,4},{12,0},{1,13},{5,9},{9,5},{13,1},{2,14},{6,10},... | collective-permute-start | bytes 2359304 | tf_op jit(solution)/shard_map/ppermute | solution.py:455
  42.5 23.0 %collective-permute-start.17 = (bf16[8,64,512]{2,1,0:T(8,128)(2,1)S(1)}, bf16[8,64,512]{2,1,0:T(8,128)(2,1)S(1)}, u32[]{:S(2)}, u32[]{:S(2)}) collective-permute-start(bf16[8,64,512]{2,1,0:T(8,128)(2,1)S(1)} %constant_dynamic-update-slice_fusion.6.near), channel_id=1, source_target_pairs={{0,1},{1,0},{2,3},{3,2},{4,5},{5,4},{6,7},{7,6},{8,9},{9,8},{10,11... | collective-permute-start | bytes 1572872 | tf_op jit(solution)/shard_map/ppermute | solution.py:455
  43.6 26.2 %collective-permute-start.13 = (bf16[8,64,512]{2,1,0:T(8,128)(2,1)S(1)}, bf16[8,64,512]{2,1,0:T(8,128)(2,1)S(1)}, u32[]{:S(2)}, u32[]{:S(2)}) collective-permute-start(bf16[8,64,512]{2,1,0:T(8,128)(2,1)S(1)} %constant_dynamic-update-slice_fusion.near), channel_id=1, source_target_pairs={{0,4},{4,0},{8,12},{12,8},{1,5},{5,1},{9,13},{13,9},{2,6},{6,2},{1... | collective-permute-start | bytes 1572872 | tf_op jit(solution)/shard_map/ppermute | solution.py:455
  62.1 7.7 %collective-permute-start.16 = (bf16[512,512]{1,0:T(8,128)(2,1)S(1)}, bf16[512,512]{1,0:T(8,128)(2,1)S(1)}, u32[]{:S(2)}, u32[]{:S(2)}) collective-permute-start(bf16[512,512]{1,0:T(8,128)(2,1)S(1)} %get-tuple-element.134), channel_id=1, source_target_pairs={{0,16},{16,0},{1,17},{17,1},{2,18},{18,2},{3,19},{19,3},{4,20},{20... | collective-permute-start | bytes 1572872 | tf_op jit(solution)/shard_map/ppermute | solution.py:451
  79.8 8.8 %collective-permute-start.19 = (bf16[512,512]{1,0:T(8,128)(2,1)S(1)}, bf16[512,512]{1,0:T(8,128)(2,1)S(1)}, u32[]{:S(2)}, u32[]{:S(2)}) collective-permute-start(bf16[512,512]{1,0:T(8,128)(2,1)S(1)} %get-tuple-element.132), channel_id=1, source_target_pairs={{0,16},{16,0},{1,17},{17,1},{2,18},{18,2},{3,19},{19,3},{4,20},{20... | collective-permute-start | bytes 1572872 | tf_op jit(solution)/shard_map/ppermute | solution.py:451
  94.6 19.1 %collective-permute-start.22 = (bf16[8,64,768]{2,1,0:T(8,128)(2,1)S(1)}, bf16[8,64,768]{2,1,0:T(8,128)(2,1)S(1)}, u32[]{:S(2)}, u32[]{:S(2)}) collective-permute-start(bf16[8,64,768]{2,1,0:T(8,128)(2,1)S(1)} %get-tuple-element.112), channel_id=1, source_target_pairs={{0,1},{1,0},{2,3},{3,2},{4,5},{5,4},{6,7},{7,6},{8,9},{9,8},{10,11... | collective-permute-start | bytes 2359304 | tf_op jit(solution)/shard_map/ppermute | solution.py:455
  94.7 20.3 %collective-permute-start.21 = (bf16[8,64,768]{2,1,0:T(8,128)(2,1)S(1)}, bf16[8,64,768]{2,1,0:T(8,128)(2,1)S(1)}, u32[]{:S(2)}, u32[]{:S(2)}) collective-permute-start(bf16[8,64,768]{2,1,0:T(8,128)(2,1)S(1)} %get-tuple-element.108), channel_id=1, source_target_pairs={{0,12},{4,8},{8,4},{12,0},{1,13},{5,9},{9,5},{13,1},{2,14},{6,10},... | collective-permute-start | bytes 2359304 | tf_op jit(solution)/shard_map/ppermute | solution.py:455
  96.6 14.3 %collective-permute-start.20 = (bf16[8,64,512]{2,1,0:T(8,128)(2,1)S(1)}, bf16[8,64,512]{2,1,0:T(8,128)(2,1)S(1)}, u32[]{:S(2)}, u32[]{:S(2)}) collective-permute-start(bf16[8,64,512]{2,1,0:T(8,128)(2,1)S(1)} %get-tuple-element.102), channel_id=1, source_target_pairs={{0,3},{1,2},{2,1},{3,0},{4,7},{5,6},{6,5},{7,4},{8,11},{9,10},{10,... | collective-permute-start | bytes 1572872 | tf_op jit(solution)/shard_map/ppermute | solution.py:455
  100.5 12.8 %collective-permute-start.23 = (bf16[8,64,512]{2,1,0:T(8,128)(2,1)S(1)}, bf16[8,64,512]{2,1,0:T(8,128)(2,1)S(1)}, u32[]{:S(2)}, u32[]{:S(2)}) collective-permute-start(bf16[8,64,512]{2,1,0:T(8,128)(2,1)S(1)} %get-tuple-element.115), channel_id=1, source_target_pairs={{0,4},{4,0},{8,12},{12,8},{1,5},{5,1},{9,13},{13,9},{2,6},{6,2},{1... | collective-permute-start | bytes 1572872 | tf_op jit(solution)/shard_map/ppermute | solution.py:455
  116.6 10.4 %collective-permute-start.25 = (bf16[4,64,768]{2,1,0:T(8,128)(2,1)S(1)}, bf16[4,64,768]{2,1,0:T(8,128)(2,1)S(1)}, u32[]{:S(2)}, u32[]{:S(2)}) collective-permute-start(bf16[4,64,768]{2,1,0:T(8,128)(2,1)S(1)} %get-tuple-element.138), channel_id=1, source_target_pairs={{0,4},{4,0},{8,12},{12,8},{1,5},{5,1},{9,13},{13,9},{2,6},{6,2},{1... | collective-permute-start | bytes 1179656 | tf_op jit(solution)/shard_map/ppermute | solution.py:455
  117.0 10.3 %collective-permute-start.26 = (bf16[4,64,768]{2,1,0:T(8,128)(2,1)S(1)}, bf16[4,64,768]{2,1,0:T(8,128)(2,1)S(1)}, u32[]{:S(2)}, u32[]{:S(2)}) collective-permute-start(bf16[4,64,768]{2,1,0:T(8,128)(2,1)S(1)} %get-tuple-element.136), channel_id=1, source_target_pairs={{0,3},{1,2},{2,1},{3,0},{4,7},{5,6},{6,5},{7,4},{8,11},{9,10},{10,... | collective-permute-start | bytes 1179656 | tf_op jit(solution)/shard_map/ppermute | solution.py:455
  130.8 7.5 %collective-permute-start.29 = (bf16[64,1280]{1,0:T(8,128)(2,1)S(1)}, bf16[64,1280]{1,0:T(8,128)(2,1)S(1)}, u32[]{:S(2)}, u32[]{:S(2)}) collective-permute-start(bf16[64,1280]{1,0:T(8,128)(2,1)S(1)} %get-tuple-element.145), channel_id=1, source_target_pairs={{0,8},{4,12},{8,0},{12,4},{1,9},{5,13},{9,1},{13,5},{2,10},{6,14},... | collective-permute-start | bytes 491528 | tf_op jit(solution)/shard_map/ppermute | solution.py:455
  170.2 8.8 %collective-permute-start.34 = (bf16[64,2560]{1,0:T(8,128)(2,1)S(1)}, bf16[64,2560]{1,0:T(8,128)(2,1)S(1)}, u32[]{:S(2)}, u32[]{:S(2)}) collective-permute-start(bf16[64,2560]{1,0:T(8,128)(2,1)S(1)} %bitcast.82), channel_id=1, source_target_pairs={{0,16},{16,0},{1,17},{17,1},{2,18},{18,2},{3,19},{19,3},{4,20},{20... | collective-permute-start | bytes 983048 | tf_op jit(solution)/shard_map/ppermute | solution.py:451
  (24 other events, 342.1 us)

commit v2 on v1

v2 whole, which is shorter than its diff:
```python
import functools

import jax
import jax.numpy as jnp
from jax import lax
from jax.experimental import pallas as pl
from jax.experimental.pallas import tpu as pltpu
from jax.sharding import Mesh
from jax.sharding import PartitionSpec as P

BLK = 256
HEAD_WIDTH = 256

norm_eps = 1e-06
beta_first = 0.9
beta_second = 0.95
learn_rate = 0.01
step_number = 10.0
update_eps = 1e-08
ratio_eps = 1e-06

OWN = ("x", "y")
SWAP = ((0, 1), (1, 0))

DIRECT = ("x", "y", "x", "y")
STEPS = ((("y", 1), ("y", 3)), (("x", 1), ("x", 3)), (("y", 3), ("y", 1)), (("x", 3), ("x", 1)))


def rms_scale(values):
    return values * lax.rsqrt(jnp.mean(values * values, axis=-1, keepdims=True) + norm_eps)


def sigmoid(values):
    return 1.0 / (1.0 + jnp.exp(-values))


def allowed_mask(length):
    row = lax.broadcasted_iota(jnp.int32, (BLK, BLK), 0)
    col = lax.broadcasted_iota(jnp.int32, (BLK, BLK), 1)
    return ((col <= row) & (row < length)).astype(jnp.float32) * (1.0 / BLK)


def dot_nt(left, right):
    return lax.dot_general(
        left, right, (((1,), (1,)), ((), ())), preferred_element_type=jnp.float32
    )


def dot_tn(left, right):
    return lax.dot_general(
        left, right, (((0,), (0,)), ((), ())), preferred_element_type=jnp.float32
    )


def dot_nn(left, right):
    return jnp.dot(left, right, preferred_element_type=jnp.float32)


def silu_slope(values):
    sig = sigmoid(values)
    act = values * sig
    return act, sig + act * (1.0 - sig)


def relative_slot(mask, turn):
    direct, other = (mask >> 2, mask & 3) if turn % 2 == 0 else (mask & 3, mask >> 2)
    high, odd = other >> 1, (other >> 1) ^ (other & 1)
    first, second = (odd, high) if turn < 2 else (high, odd)
    return direct + 4 * first + 8 * second


def owner_mask(slot, turn):
    return next(mask for mask in range(16) if relative_slot(mask, turn) == slot)


def gathered(held, forwarded, slot):
    count = held[0].shape[0]
    if slot < 3 * count:
        return held[slot // count][slot % count]
    return jnp.concatenate([part[slot % count] for part in forwarded], axis=1)


def place_rows(turn, own, rows, held, forwarded, store):
    for slot in range(16):
        start = pl.multiple_of((own ^ owner_mask(slot, turn)) * rows, rows)
        store(pl.ds(start, rows), gathered(held, forwarded, slot))


def forward_kernel(
    place,
    lengths,
    normed,
    a0,
    a1,
    a2,
    a_low,
    a_high,
    b0,
    b1,
    b2,
    b_low,
    b_high,
    projected,
    scores,
    mixed,
    outer,
    weight,
):
    width = mixed.shape[2]
    quarter = outer.shape[1] // 2

    @pl.when(pl.program_id(0) == 0)
    def _():
        rows = a0.shape[1]

        def store_a(at, block):
            weight[at, : 2 * width] = block[:, : 2 * width]
            outer[at, :quarter] = block[:, 2 * width :]

        def store_b(at, block):
            weight[at, 2 * width :] = block[:, :width]
            outer[at, quarter:] = block[:, 2 * width :]

        place_rows(0, place[0], rows, (a0, a1, a2), (a_low, a_high), store_a)
        place_rows(1, place[0], rows, (b0, b1, b2), (b_low, b_high), store_b)

    proj = dot_nn(normed[0], weight[...])
    projected[0] = proj
    held = (proj * sigmoid(proj)).astype(jnp.bfloat16)
    allowed = allowed_mask(lengths[pl.program_id(0)])
    for start in range(0, width, HEAD_WIDTH):
        queries, values, key_part = (
            held[:, part * width + start : part * width + start + HEAD_WIDTH] for part in range(3)
        )
        score = dot_nt(queries, key_part) * HEAD_WIDTH ** (-0.5)
        scores[0, start // HEAD_WIDTH] = score
        attention = (score * sigmoid(score) * allowed).astype(jnp.bfloat16)
        mixed[0, :, start : start + HEAD_WIDTH] = dot_nn(attention, values)


def gating_kernel(
    place,
    normed,
    b0,
    b1,
    b2,
    b_high,
    masked,
    keep,
    recv,
    mixed,
    gating_out,
    grad_gated,
    stats,
    weight,
):
    width = keep.shape[0]

    @pl.when(pl.program_id(0) == 0)
    def _():
        def store(at, block):
            weight[at, :] = block

        place_rows(1, place[0], b0.shape[1], (b0, b1, b2), (b_high,), store)

    proj = dot_nn(normed[0], weight[...])
    gating_out[0] = proj
    core = place[1]
    mine = masked[0, :, pl.ds(pl.multiple_of(core * width, width), width)]
    others = masked[0, :, pl.ds(pl.multiple_of((1 - core) * width, width), width)]
    grad = (dot_nt(mine, keep[...]) + dot_nt(others, recv[...])).astype(jnp.bfloat16)
    grad_gated[0] = grad
    mix = mixed[0]
    square = jnp.sum(mix * mix, axis=1, keepdims=True)
    cross = jnp.sum(
        grad.astype(jnp.float32) * (proj * sigmoid(proj)) * mix, axis=1, keepdims=True
    )
    lane = lax.broadcasted_iota(jnp.int32, (BLK, 128), 1)
    stats[0] = jnp.where(lane == 0, square, cross)


def norm_scale(model_width, stats, stats_other):
    total = stats[0] + stats_other[0]
    inv = lax.rsqrt(total[:, 0:1] / model_width + norm_eps)
    return inv, inv * inv * inv * (total[:, 1:2] / model_width)


def outer_kernel(place, projected, mixed, stats, stats_other, masked, term, total):
    width = mixed.shape[2]
    inv, _ = norm_scale(2 * width, stats, stats_other)
    proj = projected[0]
    gated = (mixed[0] * inv * (proj * sigmoid(proj))).astype(jnp.bfloat16)
    step = pl.program_id(0)
    for side in range(2):
        column = (place[1] + side) % 2
        part = masked[0, :, pl.ds(pl.multiple_of(column * width, width), width)]
        value = dot_tn(gated, part)

        @pl.when(step == 0)
        def _():
            total[side] = value

        @pl.when(step > 0)
        def _():
            total[side] += value

    @pl.when(step == pl.num_programs(0) - 1)
    def _():
        term[...] = total[...].astype(jnp.bfloat16)


def backward_kernel(
    lengths, gating_in, projected, scores, mixed, grad_gated, stats, stats_other, grads
):
    width = mixed.shape[2]
    inv, back = norm_scale(2 * width, stats, stats_other)
    gating, slope = silu_slope(gating_in[0])
    mix = mixed[0]
    grad = grad_gated[0].astype(jnp.float32)
    grads[0, :, :width] = (grad * (mix * inv) * slope).astype(jnp.bfloat16)
    grad_mixed = (inv * (grad * gating) - mix * back).astype(jnp.bfloat16)
    allowed = allowed_mask(lengths[pl.program_id(0)])
    for start in range(0, width, HEAD_WIDTH):
        (queries, queries_slope), (values, values_slope), (key_part, keys_slope) = (
            silu_slope(projected[0, :, part * width + start : part * width + start + HEAD_WIDTH])
            for part in range(3)
        )
        act, slope = silu_slope(scores[0, start // HEAD_WIDTH])
        attention = (act * allowed).astype(jnp.bfloat16)
        grad_head = grad_mixed[:, start : start + HEAD_WIDTH]
        grad_att = dot_nt(grad_head, values.astype(jnp.bfloat16)).astype(jnp.bfloat16)
        grad_score = (
            grad_att.astype(jnp.float32) * allowed * slope * HEAD_WIDTH ** (-0.5)
        ).astype(jnp.bfloat16)
        for part, (grad_part, side) in enumerate(
            (
                (dot_tn(attention, grad_head), values_slope),
                (dot_nn(grad_score, key_part.astype(jnp.bfloat16)), queries_slope),
                (dot_tn(grad_score, queries.astype(jnp.bfloat16)), keys_slope),
            ),
            1,
        ):
            held = grad_part.astype(jnp.bfloat16).astype(jnp.float32)
            at = part * width + start
            grads[0, :, at : at + HEAD_WIDTH] = (held * side).astype(jnp.bfloat16)


def store_slot(slot, value, columns, near, far):
    count = near.shape[0]

    @pl.when(slot < count)
    def _():
        near[jnp.minimum(slot, count - 1), :, columns] = value

    @pl.when(slot >= count)
    def _():
        far[jnp.maximum(slot - count, 0), :, columns] = value


def terms_kernel(place, normed_t, grads, keep, recv, *refs):
    outs, held, sems = refs[:8], refs[8:16], refs[16]
    step = pl.program_id(0)
    rows, width = held[0].shape[1], grads.shape[1]
    depth = normed_t.shape[0]
    half = keep.shape[0] // rows

    def copies(turn):
        return [
            pltpu.make_async_copy(held[at], outs[at], sems.at[at])
            for at in (2 * turn, 2 * turn + 1)
        ]

    for turn in range(4):

        @pl.when(step == turn)
        def _(turn=turn):
            near, far = held[2 * turn : 2 * turn + 2]
            for chunk in range(0, depth, BLK):
                term = dot_nn(normed_t[chunk : chunk + BLK, :], grads[...]).astype(jnp.bfloat16)
                for block in range(BLK // rows):
                    slot = relative_slot((chunk // rows + block) ^ place[0], turn)
                    value = term[block * rows : (block + 1) * rows]
                    store_slot(slot, value, slice(0, width), near, far)
            share = near.shape[2] - width
            if share:
                cut = slice((turn - 1) * share, turn * share)
                for side, outer in ((place[1], keep), (1 - place[1], recv)):
                    for block in range(half):
                        value = outer[block * rows : (block + 1) * rows, cut]
                        slot = relative_slot((side * half + block) ^ place[0], turn)
                        store_slot(slot, value, slice(width, width + share), near, far)
            for copy in copies(turn):
                copy.start()

    @pl.when(step == 3)
    def _():
        for turn in range(4):
            for copy in copies(turn):
                copy.wait()


def rows_of(*dims):
    return pl.BlockSpec((1, *dims), lambda i, *_: (i,) + (0,) * len(dims))


def whole(*dims):
    return pl.BlockSpec(dims, lambda i, *_: (0,) * len(dims))


def call(kernel, name, grid, prefetch, in_specs, out, inputs, scratch=()):
    moved = sum(v.size * v.dtype.itemsize for v in inputs)
    return pl.pallas_call(
        kernel,
        grid_spec=pltpu.PrefetchScalarGridSpec(
            num_scalar_prefetch=len(prefetch),
            grid=grid,
            in_specs=in_specs,
            out_specs=[spec for spec, _, _ in out],
            scratch_shapes=list(scratch),
        ),
        out_shape=[jax.ShapeDtypeStruct(shape, dtype) for _, shape, dtype in out],
        compiler_params=pltpu.CompilerParams(vmem_limit_bytes=20 * 1024 * 1024),
        cost_estimate=pl.CostEstimate(flops=1, bytes_accessed=1, transcendentals=0),
        name=name,
    )(*prefetch, *inputs)


def column_block(value, width, at):
    return pl.BlockSpec((*value.shape[:-1], width), lambda i, *_: (0,) * (value.ndim - 1) + (at,))


def attention_forward(place, lengths, normed, held_a, held_b):
    count, rows, depth = normed.shape
    width = held_a[3].shape[2]
    heads = width // HEAD_WIDTH
    held = (*held_a, *held_b)
    return call(
        forward_kernel,
        "attention_forward",
        (count,),
        (place, lengths),
        [rows_of(rows, depth)] + [whole(*part.shape) for part in held],
        [
            (rows_of(rows, 3 * width), (count, rows, 3 * width), jnp.float32),
            (rows_of(heads, rows, rows), (count, heads, rows, rows), jnp.float32),
            (rows_of(rows, width), (count, rows, width), jnp.float32),
            (whole(depth, width), (depth, width), jnp.bfloat16),
        ],
        (normed, *held),
        [pltpu.VMEM((depth, 3 * width), jnp.bfloat16)],
    )


def gating_forward(place, normed, held_b, masked, keep, recv, mixed):
    count, rows, depth = normed.shape
    width = mixed.shape[2]
    low, high = held_b[:3], held_b[4]
    return call(
        gating_kernel,
        "gating_forward",
        (count,),
        (place,),
        [
            rows_of(rows, depth),
            *(column_block(part, width, 1) for part in low),
            column_block(high, width, 0),
            rows_of(rows, depth),
            whole(*keep.shape),
            whole(*recv.shape),
            rows_of(rows, width),
        ],
        [
            (rows_of(rows, width), (count, rows, width), jnp.float32),
            (rows_of(rows, width), (count, rows, width), jnp.bfloat16),
            (rows_of(rows, 128), (count, rows, 128), jnp.float32),
        ],
        (normed, *low, high, masked, keep, recv, mixed),
        [pltpu.VMEM((depth, width), jnp.bfloat16)],
    )


def stats_specs(count, rows):
    return [
        rows_of(rows, 128),
        pl.BlockSpec((1, rows, 128), lambda i, *_: ((i + count // 2) % count, 0, 0)),
    ]


def outer_term(place, gating, mixed, stats, stats_other, masked):
    count, rows, width = mixed.shape
    block = rows_of(rows, width)
    shape = (2, width, width)
    return call(
        outer_kernel,
        "outer_term",
        (count,),
        (place,),
        [block, block, *stats_specs(count, rows), rows_of(rows, 2 * width)],
        [(whole(*shape), shape, jnp.bfloat16)],
        (gating, mixed, stats, stats_other, masked),
        [pltpu.VMEM(shape, jnp.float32)],
    )[0]


def attention_back(lengths, gating, projected, scores, mixed, grad_gated, stats, stats_other):
    count, rows, width = mixed.shape
    heads = width // HEAD_WIDTH
    block = rows_of(rows, width)
    return call(
        backward_kernel,
        "attention_back",
        (count,),
        (lengths,),
        [
            block,
            rows_of(rows, 3 * width),
            rows_of(heads, rows, rows),
            block,
            block,
            *stats_specs(count, rows),
        ],
        [(rows_of(rows, 4 * width), (count, rows, 4 * width), jnp.bfloat16)],
        (gating, projected, scores, mixed, grad_gated, stats, stats_other),
    )[0]


def terms(place, owned, normed_t, grads, keep, recv):
    depth, rows = normed_t.shape
    width = grads.shape[1] // 4
    shapes = []
    for turn in range(4):
        columns = width + (keep.shape[1] // 2 if turn in (1, 2) else 0)
        shapes += [(depth // owned // 2, owned, columns)] * 2
    anywhere = pl.BlockSpec(memory_space=pl.ANY)
    outs = call(
        terms_kernel,
        "terms",
        (4,),
        (place,),
        [
            whole(depth, rows),
            pl.BlockSpec((rows, width), lambda i, *_: (0, i)),
            whole(*keep.shape),
            whole(*recv.shape),
        ],
        [(anywhere, shape, jnp.bfloat16) for shape in shapes],
        (normed_t, grads, keep, recv),
        [pltpu.VMEM(shape, jnp.bfloat16) for shape in shapes] + [pltpu.SemaphoreType.DMA((8,))],
    )
    return [outs[2 * turn : 2 * turn + 2] for turn in range(4)]


def sum_squares(values):
    values = values.astype(jnp.float32)
    return jnp.sum(values * values)


def update_kernel(place, squares, mine, other, *refs):
    half = mine.shape[1] // 5
    model_width = 2 * half
    first = place[1] == 0
    owners = squares.shape[0] // 8
    total = sum(squares[8 * i : 8 * i + 1, 0:1] for i in range(owners))
    clip = jnp.minimum(1.0, jnp.sqrt(5.0 * model_width * model_width / (total + norm_eps)))
    for parts, (weight, moment, square, new_weight, new_moment, new_square) in (
        (range(4), (refs[0], refs[1], refs[2], refs[6], refs[7], refs[8])),
        (range(4, 5), (refs[3], refs[4], refs[5], refs[9], refs[10], refs[11])),
    ):
        update_sq = weight_sq = 0.0
        for part in parts:
            at = slice(part * half, (part + 1) * half)
            both = (mine[:, at].astype(jnp.float32), other[:, at].astype(jnp.float32))
            for core in (0, 1):
                grad = jnp.where(first, both[core], both[1 - core]) * clip
                start = (part - parts[0]) * model_width + core * half
                col = slice(start, start + half)
                held = beta_first * moment[:, col] + (1.0 - beta_first) * grad
                held_sq = beta_second * square[:, col] + (1.0 - beta_second) * grad * grad
                new_moment[:, col] = held
                new_square[:, col] = held_sq
                update = (held * (1.0 / (1.0 - beta_first**step_number))) / (
                    jnp.sqrt(held_sq * (1.0 / (1.0 - beta_second**step_number))) + update_eps
                )
                new_weight[:, col] = update
                update_sq += jnp.sum(update * update, axis=1, keepdims=True)
                held = weight[:, col].astype(jnp.float32)
                weight_sq += jnp.sum(held * held, axis=1, keepdims=True)
        ratio = learn_rate * jnp.sqrt(weight_sq) / (jnp.sqrt(update_sq) + ratio_eps)
        new_weight[...] = weight[...].astype(jnp.float32) - ratio * new_weight[...]


def update_rows(place, squares, mine, other, *state):
    rows = 16
    count = mine.shape[0] // rows

    def block(value):
        return pl.BlockSpec((rows, value.shape[1]), lambda i, *_: (i, 0))

    return call(
        update_kernel,
        "update_rows",
        (count,),
        (place,),
        [whole(*squares.shape)] + [block(v) for v in (mine, other, *state)],
        [(block(v), v.shape, jnp.float32) for v in state],
        (squares, mine, other, *state),
    )


def swap_cores(values):
    return lax.ppermute(values, "c", SWAP)


def over_link(values, axis, mask):
    return lax.ppermute(values, axis, [(i, i ^ mask) for i in range(4)])


def direct_round(blocks_of, groups):
    got = [[None] * 4, [None] * 4]
    for mask in (1, 3, 2):
        for group, axis in enumerate(("x", "y")):
            got[group][mask] = over_link(blocks_of(groups[group], mask), axis, mask)
    return got


def gather_groups(groups, width, prepare):
    got = direct_round(lambda group, mask: group, groups)
    got[0][1], beside = prepare(got[0][1])
    for group, mine in zip(got, groups):
        group[0] = mine
    got = lax.optimization_barrier(got)
    held = [jnp.stack(group) for group in got]
    one = [over_link(part, axis, 1) for part, axis in zip(held, ("y", "x"))]
    three = [over_link(part, axis, 3) for part, axis in zip(held, ("y", "x"))]
    one, three, beside = lax.optimization_barrier((one, three, beside))
    low = [over_link(part[:, :, :width], axis, 3) for part, axis in zip(one, ("y", "x"))]
    high = [over_link(part[:, :, width:], axis, 1) for part, axis in zip(three, ("y", "x"))]
    low, high = lax.optimization_barrier((low, high))
    return list(zip(held, one, three, low, high)), beside


def add_blocks(*blocks):
    return sum(block.astype(jnp.float32) for block in blocks).astype(jnp.bfloat16)


def scatter_parts(pairs):
    for step in (1, 0):
        got = [over_link(far, *STEPS[turn][step]) for turn, (_, far) in enumerate(pairs)]
        mine, got = lax.optimization_barrier(([near for near, _ in pairs], got))
        held = [add_blocks(*pair) for pair in zip(mine, got)]
        if step:
            pairs = [jnp.split(part, 2, axis=0) for part in held]
    groups = [jnp.concatenate([held[0], held[2]], axis=2), jnp.concatenate([held[1], held[3]], axis=2)]
    got = direct_round(lambda group, mask: group[mask], groups)
    return [add_blocks(group[0], *blocks[1:]) for group, blocks in zip(groups, got)]


def exchange(blocks, axes):
    return lax.all_to_all(blocks, axes, 0, 0, tiled=True)


def per_device(
    tokens,
    cotangent,
    lengths,
    norm_gain,
    weight_in,
    weight_out,
    moment_in,
    square_in,
    moment_out,
    square_out,
):
    slots, rows, model_width = tokens.shape
    half = model_width // 2
    quarter = half // 2
    core = lax.axis_index("c")
    own = lax.axis_index(OWN)
    owners = lax.axis_size(OWN)
    planes = lax.axis_size("z")
    owned = weight_in.shape[0]
    place = jnp.stack([own, core]).astype(jnp.int32)

    mine = [
        lax.dynamic_slice_in_dim(weight_in, part * model_width + core * half, half, axis=1)
        for part in range(4)
    ]
    mine_out = lax.dynamic_slice_in_dim(weight_out, core * half, half, axis=1)
    def prepare(got):
        got, token_rows, cot_rows = lax.optimization_barrier((got, tokens, cotangent))
        normed = (rms_scale(token_rows.astype(jnp.float32)) * norm_gain).astype(jnp.bfloat16)
        row_index = jnp.arange(rows, dtype=jnp.int32)
        live = row_index[None, :] < lengths[:, None]
        masked = jnp.where(live[:, :, None], cot_rows, jnp.zeros_like(cot_rows))
        normed = jnp.concatenate([normed, swap_cores(normed)], axis=0)
        masked = jnp.concatenate([masked, swap_cores(masked)], axis=0)
        all_lengths = jnp.concatenate([lengths, swap_cores(lengths)], axis=0)
        return got, (normed, masked, all_lengths, normed.reshape(-1, model_width).T)

    (held_a, held_b), (normed, masked, all_lengths, normed_t) = gather_groups(
        [
            jnp.concatenate([mine[2], mine[1], mine_out[:, :quarter]], axis=1),
            jnp.concatenate([mine[3], mine[0], mine_out[:, quarter:]], axis=1),
        ],
        half,
        prepare,
    )

    projected, scores, mixed, outer_cols = attention_forward(
        place, all_lengths, normed, held_a, held_b
    )
    outer_cols = outer_cols.reshape(2, half, half)
    keep = lax.dynamic_index_in_dim(outer_cols, core, axis=0, keepdims=False)
    recv = swap_cores(lax.dynamic_index_in_dim(outer_cols, 1 - core, axis=0, keepdims=False))
    gating, grad_gated, stats = gating_forward(place, normed, held_b, masked, keep, recv, mixed)
    stats_other = swap_cores(stats)
    outer = outer_term(place, gating, mixed, stats, stats_other, masked)
    outer_recv = swap_cores(outer[1])
    grads = attention_back(
        all_lengths, gating, projected, scores, mixed, grad_gated, stats, stats_other
    )
    term_g, term_v, term_q, term_k = terms(
        place, owned, normed_t, grads.reshape(-1, 4 * half), outer[0], outer_recv
    )
    part_gq, part_vk = scatter_parts([term_g, term_v, term_q, term_k])
    wide = half + quarter
    part = jnp.concatenate(
        [
            part_gq[:, :half],
            part_vk[:, :half],
            part_gq[:, half : 2 * half],
            part_vk[:, wide:],
            part_vk[:, half:wide],
            part_gq[:, 2 * half :],
        ],
        axis=1,
    )

    piece = jnp.sum(
        exchange(part, "z").reshape(planes, owned // planes, -1).astype(jnp.float32), axis=0
    ).astype(jnp.bfloat16)
    shard = exchange(
        jnp.broadcast_to(piece[None], (planes, *piece.shape)).reshape(owned, -1), "z"
    )
    other = swap_cores(shard)
    squares = exchange(
        jnp.broadcast_to(sum_squares(shard), (2 * owners * 8, 128)), ("c", *OWN)
    )
    return update_rows(
        place,
        squares,
        shard,
        other,
        weight_in,
        moment_in,
        square_in,
        weight_out,
        moment_out,
        square_out,
    )


def solution(mesh):
    fine = Mesh(mesh.devices.reshape(8, 2, 4, 4), ("z", "c", "x", "y"))
    histories = ("z", "c", "x", "y")
    placed = (
        P(histories, None, None),
        P(histories, None, None),
        P(histories),
        P(),
        P(OWN, None),
        P(OWN, None),
        P(OWN, None),
        P(OWN, None),
        P(OWN, None),
        P(OWN, None),
    )
    return jax.shard_map(
        per_device,
        mesh=fine,
        in_specs=placed,
        out_specs=(P(OWN, None),) * 6,
        check_vma=False,
    )
```

time: 198 us -> 205 us (1.035)
  waiting for transfers between devices: 42.4 us -> 53.5 us
  local copies, waits for them, and re-layouts: 14.8 us -> 11.5 us
    ppermute x28, waiting for transfers between devices: 40 us -> 50.4 us  [over_link(): return lax.ppermute(values, axis, [(i, i ^ mask) for i in range(4)])]
    slice x0 -> x4, local copies, waits for them, and re-layouts: none -> 5.88 us  [the longest x2 3.34 us: gather_groups(): part[:, :, :width]]
    unnamed x35 -> x29, local copies, waits for them, and re-layouts: 5.05 us -> 0.1 us
    concatenate x4 -> x0, local copies, waits for them, and re-layouts: 4.73 us -> none  [gather_parts(): held = [jnp.concatenate(pair, axis=0) for pair in zip(held, got)]]
    pallas_call x12 -> x6, Pallas kernels: 39.1 us -> 38.5 us  [call(): pl.pallas_call(kernel, grid_spec=pltpu.PrefetchScalarGridSpec(num_scalar_...]
  transfers between devices with their start and end apart: 35 -> 35, of which waited for: 15 -> 18; matrix products, arithmetic and copies ran while one was open for 8% -> 8% of each run, Pallas kernels for 11% -> 3%
where the time goes in v2:
time: 205 us; the launch traced here: 204 us
  waiting for transfers between devices  53.5 us (26%)
  starting transfers between devices  46.3 us (23%)
  blocking collectives  42.7 us (21%)
  Pallas kernels  38.5 us (19%)
  local copies, waits for them, and re-layouts  11.5 us (6%)
  other arithmetic  10.6 us (5%)
    ppermute x28, waiting for transfers between devices, over_link(): return lax.ppermute(values, axis, [(i, i ^ mask) for i in range(4)])  50.4 us
    all_to_all x3, blocking collectives, exchange(): return lax.all_to_all(blocks, axes, 0, 0, tiled=True)  42.7 us
    pallas_call x6, Pallas kernels, call(): pl.pallas_call(kernel, grid_spec=pltpu.PrefetchScalarGridSpec(num_scalar_...  38.5 us
    ppermute x28, starting transfers between devices, over_link(): return lax.ppermute(values, axis, [(i, i ^ mask) for i in range(4)])  30.8 us
    ppermute x7, starting transfers between devices, swap_cores(): return lax.ppermute(values, 'c', SWAP)  15.5 us
  transfers between devices with their start and end apart: 35, of which 18 were waited for; matrix products, arithmetic and copies ran while one was open for 8% of the time, Pallas kernels for 3%

profile of v2, /device:TPU:1, one launch (start us, length us, event | category | flops | bytes accessed | tf_op | source)
XLA Modules:
  0.0 204.4 jit_solution(16075059521808120164)
XLA Ops:
  2.6 3.4 %collective-permute-start.2 = (bf16[64,1280]{1,0:T(8,128)(2,1)S(1)}, bf16[64,1280]{1,0:T(8,128)(2,1)S(1)}, u32[]{:S(2)}, u32[]{:S(2)}) collective-permute-start(bf16[64,1280]{1,0:T(8,128)(2,1)S(1)} %pad_maximum_fusion.6), channel_id=1, source_target_pairs={{0,12},{4,8},{8,4},{12,0},{1,13},{5,9},{9,5},{13,1},{2,14},{6,10},... | collective-permute-start | bytes 491528 | tf_op jit(solution)/shard_map/ppermute | solution.py:515
  6.7 2.9 %collective-permute-start.5 = (bf16[64,1280]{1,0:T(8,128)(2,1)S(1)}, bf16[64,1280]{1,0:T(8,128)(2,1)S(1)}, u32[]{:S(2)}, u32[]{:S(2)}) collective-permute-start(bf16[64,1280]{1,0:T(8,128)(2,1)S(1)} %pad_maximum_fusion.7), channel_id=1, source_target_pairs={{0,3},{1,2},{2,1},{3,0},{4,7},{5,6},{6,5},{7,4},{8,11},{9,10},{10,... | collective-permute-start | bytes 491528 | tf_op jit(solution)/shard_map/ppermute | solution.py:515
  14.5 2.8 %collective-permute-start.10 = (bf16[2,256,1024]{2,1,0:T(8,128)(2,1)S(1)}, bf16[2,256,1024]{2,1,0:T(8,128)(2,1)S(1)}, u32[]{:S(2)}, u32[]{:S(2)}) collective-permute-start(bf16[2,256,1024]{2,1,0:T(8,128)(2,1)S(1)} %fusion.2), channel_id=1, source_target_pairs={{0,16},{16,0},{1,17},{17,1},{2,18},{18,2},{3,19},{19,3},{4,20},{20... | collective-permute-start | bytes 3145736 | tf_op jit(solution)/shard_map/ppermute | solution.py:511
  20.5 2.8 %collective-permute-done.3 = bf16[64,1280]{1,0:T(8,128)(2,1)S(1)} collective-permute-done((bf16[64,1280]{1,0:T(8,128)(2,1)S(1)}, bf16[64,1280]{1,0:T(8,128)(2,1)S(1)}, u32[]{:S(2)}, u32[]{:S(2)}) %collective-permute-start.3) | collective-permute-done | bytes 163872 | tf_op jit(solution)/shard_map/ppermute | solution.py:515
  26.9 2.7 %collective-permute-start.8 = (bf16[4,64,1280]{2,1,0:T(8,128)(2,1)}, bf16[4,64,1280]{2,1,0:T(8,128)(2,1)}, u32[]{:S(2)}, u32[]{:S(2)}) collective-permute-start(bf16[4,64,1280]{2,1,0:T(8,128)(2,1)} %pad_maximum_fusion.2.a0), channel_id=1, source_target_pairs={{0,3},{1,2},{2,1},{3,0},{4,7},{5,6},{6,5},{7,4},{8,11},{9,10},{10,... | collective-permute-start | bytes 1966088 | tf_op jit(solution)/shard_map/ppermute | solution.py:515
  32.5 3.1 %pad_maximum_fusion.1.masked = bf16[4,256,1024]{2,1,0:T(8,128)(2,1)} fusion(bf16[2,256,1024]{2,1,0:T(8,128)(2,1)} %collective-permute-done.11, bf16[2,256,1024]{2,1,0:T(8,128)(2,1)} %broadcast_select_fusion), kind=kLoop, calls=%fused_computation.6 | loop fusion | flops 1048576 | bytes 4194304 | tf_op jit(solution)/shard_map/concatenate | solution.py:596
  35.6 4.7 %collective-permute-done.9.b2 = bf16[4,64,1280]{2,1,0:T(8,128)(2,1)S(1)} collective-permute-done((bf16[4,64,1280]{2,1,0:T(8,128)(2,1)S(1)}, bf16[4,64,1280]{2,1,0:T(8,128)(2,1)S(1)}, u32[]{:S(2)}, u32[]{:S(2)}) %collective-permute-start.9) | collective-permute-done | bytes 655392 | tf_op jit(solution)/shard_map/ppermute | solution.py:515
  53.7 5.2 %collective-permute-done.14.b_low = bf16[4,64,512]{2,1,0:T(8,128)(2,1)} collective-permute-done((bf16[4,64,512]{2,1,0:T(8,128)(2,1)}, bf16[4,64,512]{2,1,0:T(8,128)(2,1)}, u32[]{:S(2)}, u32[]{:S(2)}) %collective-permute-start.14) | collective-permute-done | bytes 262176 | tf_op jit(solution)/shard_map/ppermute | solution.py:515
  59.1 9.0 %attention_forward.1 = (f32[4,256,1536]{2,1,0:T(8,128)S(1)}, f32[4,2,256,256]{3,2,1,0:T(8,128)S(1)}, f32[4,256,512]{2,1,0:T(8,128)S(1)}, bf16[1024,512]{1,0:T(8,128)(2,1)S(1)}) custom-call(s32[2]{0:T(128)S(1)} %pad_add_fusion.place, s32[4]{0:T(128)S(1)} %pad_add_fusion.1.lengths, bf16[4,256,1024]{2,1,0:T(8,128)(2,1)S(1)} %pad_maximum_fusion.normed, ...), custom_call_target="tpu_custom_call" | custom-call | flops 1 | bytes 1 | tf_op jit(solution)/shard_map/attention_forward/pallas_call | solution.py:312
  68.2 4.5 %collective-permute-start.17 = (bf16[512,512]{1,0:T(8,128)(2,1)S(1)}, bf16[512,512]{1,0:T(8,128)(2,1)S(1)}, u32[]{:S(2)}, u32[]{:S(2)}) collective-permute-start(bf16[512,512]{1,0:T(8,128)(2,1)S(1)} %get-tuple-element.116), channel_id=1, source_target_pairs={{0,16},{16,0},{1,17},{17,1},{2,18},{18,2},{3,19},{19,3},{4,20},{20... | collective-permute-start | bytes 1572872 | tf_op jit(solution)/shard_map/ppermute | solution.py:511
  74.2 5.0 %gating_forward.1 = (f32[4,256,512]{2,1,0:T(8,128)S(1)}, bf16[4,256,512]{2,1,0:T(8,128)(2,1)S(1)}, f32[4,256,128]{2,1,0:T(8,128)S(1)}) custom-call(s32[2]{0:T(128)S(1)} %pad_add_fusion.place, bf16[4,256,1024]{2,1,0:T(8,128)(2,1)S(1)} %pad_maximum_fusion.normed, bf16[4,64,1280]{2,1,0:T(8,128)(2,1)S(1)} %pad_maximum_fusion.3.b0, ...), custom_call_target="tpu_custom_call" | custom-call | flops 1 | bytes 1 | tf_op jit(solution)/shard_map/gating_forward/pallas_call | solution.py:312
  81.2 4.6 %outer_term.1 = bf16[2,512,512]{2,1,0:T(8,128)(2,1)S(1)} custom-call(s32[2]{0:T(128)S(1)} %pad_add_fusion.place, f32[4,256,512]{2,1,0:T(8,128)S(1)} %get-tuple-element.85.gating_in.projected, f32[4,256,512]{2,1,0:T(8,128)S(1)} %get-tuple-element.84.mixed, f32[4,256,128]{2,1,0:T(8,128)S(1)} %get-tuple-element.89.stats, ...), custom_call_target="tpu_custom_call" | custom-call | flops 1 | bytes 1 | tf_op jit(solution)/shard_map/outer_term/pallas_call | solution.py:312
  86.3 6.0 %attention_back.1 = bf16[4,256,2048]{2,1,0:T(8,128)(2,1)S(1)} custom-call(s32[4]{0:T(128)S(1)} %pad_add_fusion.1.lengths, f32[4,256,512]{2,1,0:T(8,128)S(1)} %get-tuple-element.85.gating_in.projected, f32[4,256,1536]{2,1,0:T(8,128)S(1)} %get-tuple-element.86.projected, f32[4,2,256,256]{3,2,1,0:T(8,128)S(1)} %get-tuple-element.87.scores, ...), custom_call_target="tpu_custom_call" | custom-call | flops 1 | bytes 1 | tf_op jit(solution)/shard_map/attention_back/pallas_call | solution.py:312
  92.4 10.2 %terms.1 = (bf16[8,64,512]{2,1,0:T(8,128)(2,1)S(1)}, bf16[8,64,512]{2,1,0:T(8,128)(2,1)S(1)}, bf16[8,64,768]{2,1,0:T(8,128)(2,1)S(1)}, bf16[8,64,768]{2,1,0:T(8,...) custom-call(s32[2]{0:T(128)S(1)} %pad_add_fusion.place, ...), custom_call_target="tpu_custom_call" | custom-call | flops 1 | bytes 1 | tf_op jit(solution)/shard_map/terms/pallas_call | solution.py:312
  106.6 12.7 %collective-permute-done.20 = bf16[8,64,512]{2,1,0:T(8,128)(2,1)S(1)} collective-permute-done((bf16[8,64,512]{2,1,0:T(8,128)(2,1)S(1)}, bf16[8,64,512]{2,1,0:T(8,128)(2,1)S(1)}, u32[]{:S(2)}, u32[]{:S(2)}) %collective-permute-start.20) | collective-permute-done | bytes 524320 | tf_op jit(solution)/shard_map/ppermute | solution.py:515
  119.3 3.5 %collective-permute-done.21 = bf16[8,64,768]{2,1,0:T(8,128)(2,1)S(1)} collective-permute-done((bf16[8,64,768]{2,1,0:T(8,128)(2,1)S(1)}, bf16[8,64,768]{2,1,0:T(8,128)(2,1)S(1)}, u32[]{:S(2)}, u32[]{:S(2)}) %collective-permute-start.21) | collective-permute-done | bytes 786464 | tf_op jit(solution)/shard_map/ppermute | solution.py:515
  127.8 4.1 %collective-permute-done.27 = bf16[4,64,512]{2,1,0:T(8,128)(2,1)S(1)} collective-permute-done((bf16[4,64,512]{2,1,0:T(8,128)(2,1)S(1)}, bf16[4,64,512]{2,1,0:T(8,128)(2,1)S(1)}, u32[]{:S(2)}, u32[]{:S(2)}) %collective-permute-start.27) | collective-permute-done | bytes 262176 | tf_op jit(solution)/shard_map/ppermute | solution.py:515
  134.1 2.9 %collective-permute-done.26 = bf16[4,64,768]{2,1,0:T(8,128)(2,1)S(1)} collective-permute-done((bf16[4,64,768]{2,1,0:T(8,128)(2,1)S(1)}, bf16[4,64,768]{2,1,0:T(8,128)(2,1)S(1)}, u32[]{:S(2)}, u32[]{:S(2)}) %collective-permute-start.26) | collective-permute-done | bytes 393248 | tf_op jit(solution)/shard_map/ppermute | solution.py:515
  145.3 3.0 %collective-permute-done.33 = bf16[64,1280]{1,0:T(8,128)(2,1)S(1)} collective-permute-done((bf16[64,1280]{1,0:T(8,128)(2,1)S(1)}, bf16[64,1280]{1,0:T(8,128)(2,1)S(1)}, u32[]{:S(2)}, u32[]{:S(2)}) %collective-permute-start.33) | collective-permute-done | bytes 163872 | tf_op jit(solution)/shard_map/ppermute | solution.py:515
  148.5 18.3 %all_to_all.25 = bf16[8,8,2560]{2,1,0:T(8,128)(2,1)} all-to-all(bf16[8,8,2560]{2,1,0:T(8,128)(2,1)S(1)} %bitcast.56), channel_id=1, replica_groups=mesh['z'=8,'c'=2,'x'=4,'y'=4] {'z'}, dimensions={0} | all-to-all | bytes 655360 | tf_op jit(solution)/shard_map/all_to_all | solution.py:559
  167.8 12.4 %all_to_all.26 = bf16[8,8,2560]{2,1,0:T(8,128)(2,1)S(1)} all-to-all(bf16[8,8,2560]{2,1,0:T(8,128)(2,1)S(1)} %broadcast_in_dim.16), channel_id=1, replica_groups=mesh['z'=8,'c'=2,'x'=4,'y'=4] {'z'}, dimensions={0} | all-to-all | bytes 655360 | tf_op jit(solution)/shard_map/all_to_all | solution.py:559
  180.2 6.8 %collective-permute-start.34 = (bf16[64,2560]{1,0:T(8,128)(2,1)S(1)}, bf16[64,2560]{1,0:T(8,128)(2,1)S(1)}, u32[]{:S(2)}, u32[]{:S(2)}) collective-permute-start(bf16[64,2560]{1,0:T(8,128)(2,1)S(1)} %bitcast.50), channel_id=1, source_target_pairs={{0,16},{16,0},{1,17},{17,1},{2,18},{18,2},{3,19},{19,3},{4,20},{20... | collective-permute-start | bytes 983048 | tf_op jit(solution)/shard_map/ppermute | solution.py:511
  188.4 12.0 %all_to_all.27 = f32[32,8,128]{2,1,0:T(8,128)S(1)} all-to-all(f32[32,8,128]{2,1,0:T(8,128)S(1)} %broadcast_in_dim.28), channel_id=1, replica_groups=mesh['z'=8,'c'=2,'x'=4,'y'=4] {'c','x','y'}, dimensions={0} | all-to-all | bytes 262144 | tf_op jit(solution)/shard_map/all_to_all | solution.py:559
  200.5 3.7 %update_rows.1 = (f32[64,4096]{1,0:T(8,128)}, f32[64,4096]{1,0:T(8,128)}, f32[64,4096]{1,0:T(8,128)}, f32[64,1024]{1,0:T(8,128)}, f32[64,1024]{1,0:T(8,128)}, /*index=5*/f32[64,1024]{1,0:T(8,128)}) custom-call(s32[2]{0:T(128)S(1)} %pad_add_fusion.place, f32[256,128]{1,0:T(8,128)S(1)} %bitcast.53, bf16[64,2560]{1,0:T(8,128)(2,1)S(1)} %bitcast.51, ...), custom_call_target="tpu_custom_call" | custom-call | flops 1 | bytes 1 | tf_op jit(solution)/shard_map/update_rows/pallas_call | solution.py:312
  (125 shorter events, 56.6 us)
Async XLA Ops:
  2.6 14.8 %collective-permute-start.2 = (bf16[64,1280]{1,0:T(8,128)(2,1)S(1)}, bf16[64,1280]{1,0:T(8,128)(2,1)S(1)}, u32[]{:S(2)}, u32[]{:S(2)}) collective-permute-start(bf16[64,1280]{1,0:T(8,128)(2,1)S(1)} %pad_maximum_fusion.6), channel_id=1, source_target_pairs={{0,12},{4,8},{8,4},{12,0},{1,13},{5,9},{9,5},{13,1},{2,14},{6,10},... | collective-permute-start | bytes 491528 | tf_op jit(solution)/shard_map/ppermute | solution.py:515
  6.0 13.9 %collective-permute-start.1 = (bf16[64,1280]{1,0:T(8,128)(2,1)S(1)}, bf16[64,1280]{1,0:T(8,128)(2,1)S(1)}, u32[]{:S(2)}, u32[]{:S(2)}) collective-permute-start(bf16[64,1280]{1,0:T(8,128)(2,1)S(1)} %pad_maximum_fusion.6), channel_id=1, source_target_pairs={{0,8},{4,12},{8,0},{12,4},{1,9},{5,13},{9,1},{13,5},{2,10},{6,14},... | collective-permute-start | bytes 491528 | tf_op jit(solution)/shard_map/ppermute | solution.py:515
  6.7 13.6 %collective-permute-start.5 = (bf16[64,1280]{1,0:T(8,128)(2,1)S(1)}, bf16[64,1280]{1,0:T(8,128)(2,1)S(1)}, u32[]{:S(2)}, u32[]{:S(2)}) collective-permute-start(bf16[64,1280]{1,0:T(8,128)(2,1)S(1)} %pad_maximum_fusion.7), channel_id=1, source_target_pairs={{0,3},{1,2},{2,1},{3,0},{4,7},{5,6},{6,5},{7,4},{8,11},{9,10},{10,... | collective-permute-start | bytes 491528 | tf_op jit(solution)/shard_map/ppermute | solution.py:515
  9.6 10.8 %collective-permute-start.4 = (bf16[64,1280]{1,0:T(8,128)(2,1)S(1)}, bf16[64,1280]{1,0:T(8,128)(2,1)S(1)}, u32[]{:S(2)}, u32[]{:S(2)}) collective-permute-start(bf16[64,1280]{1,0:T(8,128)(2,1)S(1)} %pad_maximum_fusion.7), channel_id=1, source_target_pairs={{0,2},{1,3},{2,0},{3,1},{4,6},{5,7},{6,4},{7,5},{8,10},{9,11},{10,... | collective-permute-start | bytes 491528 | tf_op jit(solution)/shard_map/ppermute | solution.py:515
  14.5 15.1 %collective-permute-start.10 = (bf16[2,256,1024]{2,1,0:T(8,128)(2,1)S(1)}, bf16[2,256,1024]{2,1,0:T(8,128)(2,1)S(1)}, u32[]{:S(2)}, u32[]{:S(2)}) collective-permute-start(bf16[2,256,1024]{2,1,0:T(8,128)(2,1)S(1)} %fusion.2), channel_id=1, source_target_pairs={{0,16},{16,0},{1,17},{17,1},{2,18},{18,2},{3,19},{19,3},{4,20},{20... | collective-permute-start | bytes 3145736 | tf_op jit(solution)/shard_map/ppermute | solution.py:511
  20.0 12.6 %collective-permute-start.11 = (bf16[2,256,1024]{2,1,0:T(8,128)(2,1)}, bf16[2,256,1024]{2,1,0:T(8,128)(2,1)}, u32[]{:S(2)}, u32[]{:S(2)}) collective-permute-start(bf16[2,256,1024]{2,1,0:T(8,128)(2,1)} %broadcast_select_fusion), channel_id=1, source_target_pairs={{0,16},{16,0},{1,17},{17,1},{2,18},{18,2},{3,19},{19,3},{4,20},{20... | collective-permute-start | bytes 3145736 | tf_op jit(solution)/shard_map/ppermute | solution.py:511
  23.4 16.9 %collective-permute-start.9 = (bf16[4,64,1280]{2,1,0:T(8,128)(2,1)S(1)}, bf16[4,64,1280]{2,1,0:T(8,128)(2,1)S(1)}, u32[]{:S(2)}, u32[]{:S(2)}) collective-permute-start(bf16[4,64,1280]{2,1,0:T(8,128)(2,1)S(1)} %pad_maximum_fusion.3.b0), channel_id=1, source_target_pairs={{0,12},{4,8},{8,4},{12,0},{1,13},{5,9},{9,5},{13,1},{2,14},{6,10},... | collective-permute-start | bytes 1966088 | tf_op jit(solution)/shard_map/ppermute | solution.py:515
  26.0 15.2 %collective-permute-start.7 = (bf16[4,64,1280]{2,1,0:T(8,128)(2,1)S(1)}, bf16[4,64,1280]{2,1,0:T(8,128)(2,1)}, u32[]{:S(2)}, u32[]{:S(2)}) collective-permute-start(bf16[4,64,1280]{2,1,0:T(8,128)(2,1)S(1)} %pad_maximum_fusion.3.b0), channel_id=1, source_target_pairs={{0,4},{4,0},{8,12},{12,8},{1,5},{5,1},{9,13},{13,9},{2,6},{6,2},{1... | collective-permute-start | bytes 1966088 | tf_op jit(solution)/shard_map/ppermute | solution.py:515
  26.9 16.6 %collective-permute-start.8 = (bf16[4,64,1280]{2,1,0:T(8,128)(2,1)}, bf16[4,64,1280]{2,1,0:T(8,128)(2,1)}, u32[]{:S(2)}, u32[]{:S(2)}) collective-permute-start(bf16[4,64,1280]{2,1,0:T(8,128)(2,1)} %pad_maximum_fusion.2.a0), channel_id=1, source_target_pairs={{0,3},{1,2},{2,1},{3,0},{4,7},{5,6},{6,5},{7,4},{8,11},{9,10},{10,... | collective-permute-start | bytes 1966088 | tf_op jit(solution)/shard_map/ppermute | solution.py:515
  29.7 15.0 %collective-permute-start.6 = (bf16[4,64,1280]{2,1,0:T(8,128)(2,1)}, bf16[4,64,1280]{2,1,0:T(8,128)(2,1)}, u32[]{:S(2)}, u32[]{:S(2)}) collective-permute-start(bf16[4,64,1280]{2,1,0:T(8,128)(2,1)} %pad_maximum_fusion.2.a0), channel_id=1, source_target_pairs={{0,1},{1,0},{2,3},{3,2},{4,5},{5,4},{6,7},{7,6},{8,9},{9,8},{10,11... | collective-permute-start | bytes 1966088 | tf_op jit(solution)/shard_map/ppermute | solution.py:515
  47.2 11.9 %collective-permute-start.16 = (bf16[4,64,768]{2,1,0:T(8,128)(2,1)}, bf16[4,64,768]{2,1,0:T(8,128)(2,1)}, u32[]{:S(2)}, u32[]{:S(2)}) collective-permute-start(bf16[4,64,768]{2,1,0:T(8,128)(2,1)} %slice.71), channel_id=1, source_target_pairs={{0,4},{4,0},{8,12},{12,8},{1,5},{5,1},{9,13},{13,9},{2,6},{6,2},{1... | collective-permute-start | bytes 1179656 | tf_op jit(solution)/shard_map/ppermute | solution.py:515
  48.6 10.5 %collective-permute-start.15 = (bf16[4,64,768]{2,1,0:T(8,128)(2,1)}, bf16[4,64,768]{2,1,0:T(8,128)(2,1)}, u32[]{:S(2)}, u32[]{:S(2)}) collective-permute-start(bf16[4,64,768]{2,1,0:T(8,128)(2,1)} %slice.70), channel_id=1, source_target_pairs={{0,1},{1,0},{2,3},{3,2},{4,5},{5,4},{6,7},{7,6},{8,9},{9,8},{10,11... | collective-permute-start | bytes 1179656 | tf_op jit(solution)/shard_map/ppermute | solution.py:515
  52.3 6.7 %collective-permute-start.13 = (bf16[4,64,512]{2,1,0:T(8,128)(2,1)}, bf16[4,64,512]{2,1,0:T(8,128)(2,1)}, u32[]{:S(2)}, u32[]{:S(2)}) collective-permute-start(bf16[4,64,512]{2,1,0:T(8,128)(2,1)} %slice.68), channel_id=1, source_target_pairs={{0,3},{1,2},{2,1},{3,0},{4,7},{5,6},{6,5},{7,4},{8,11},{9,10},{10,... | collective-permute-start | bytes 786440 | tf_op jit(solution)/shard_map/ppermute | solution.py:515
  102.6 20.3 %collective-permute-start.21 = (bf16[8,64,768]{2,1,0:T(8,128)(2,1)S(1)}, bf16[8,64,768]{2,1,0:T(8,128)(2,1)S(1)}, u32[]{:S(2)}, u32[]{:S(2)}) collective-permute-start(bf16[8,64,768]{2,1,0:T(8,128)(2,1)S(1)} %get-tuple-element.95), channel_id=1, source_target_pairs={{0,12},{4,8},{8,4},{12,0},{1,13},{5,9},{9,5},{13,1},{2,14},{6,10},... | collective-permute-start | bytes 2359304 | tf_op jit(solution)/shard_map/ppermute | solution.py:515
  105.1 18.7 %collective-permute-start.22 = (bf16[8,64,768]{2,1,0:T(8,128)(2,1)S(1)}, bf16[8,64,768]{2,1,0:T(8,128)(2,1)S(1)}, u32[]{:S(2)}, u32[]{:S(2)}) collective-permute-start(bf16[8,64,768]{2,1,0:T(8,128)(2,1)S(1)} %get-tuple-element.96), channel_id=1, source_target_pairs={{0,1},{1,0},{2,3},{3,2},{4,5},{5,4},{6,7},{7,6},{8,9},{9,8},{10,11... | collective-permute-start | bytes 2359304 | tf_op jit(solution)/shard_map/ppermute | solution.py:515
  105.4 13.9 %collective-permute-start.20 = (bf16[8,64,512]{2,1,0:T(8,128)(2,1)S(1)}, bf16[8,64,512]{2,1,0:T(8,128)(2,1)S(1)}, u32[]{:S(2)}, u32[]{:S(2)}) collective-permute-start(bf16[8,64,512]{2,1,0:T(8,128)(2,1)S(1)} %get-tuple-element.94), channel_id=1, source_target_pairs={{0,3},{1,2},{2,1},{3,0},{4,7},{5,6},{6,5},{7,4},{8,11},{9,10},{10,... | collective-permute-start | bytes 1572872 | tf_op jit(solution)/shard_map/ppermute | solution.py:515
  106.6 12.7 %collective-permute-start.23 = (bf16[8,64,512]{2,1,0:T(8,128)(2,1)S(1)}, bf16[8,64,512]{2,1,0:T(8,128)(2,1)S(1)}, u32[]{:S(2)}, u32[]{:S(2)}) collective-permute-start(bf16[8,64,512]{2,1,0:T(8,128)(2,1)S(1)} %get-tuple-element.97), channel_id=1, source_target_pairs={{0,4},{4,0},{8,12},{12,8},{1,5},{5,1},{9,13},{13,9},{2,6},{6,2},{1... | collective-permute-start | bytes 1572872 | tf_op jit(solution)/shard_map/ppermute | solution.py:515
  124.2 7.8 %collective-permute-start.27 = (bf16[4,64,512]{2,1,0:T(8,128)(2,1)S(1)}, bf16[4,64,512]{2,1,0:T(8,128)(2,1)S(1)}, u32[]{:S(2)}, u32[]{:S(2)}) collective-permute-start(bf16[4,64,512]{2,1,0:T(8,128)(2,1)S(1)} %get-tuple-element.128), channel_id=1, source_target_pairs={{0,12},{4,8},{8,4},{12,0},{1,13},{5,9},{9,5},{13,1},{2,14},{6,10},... | collective-permute-start | bytes 786440 | tf_op jit(solution)/shard_map/ppermute | solution.py:515
  126.3 10.6 %collective-permute-start.26 = (bf16[4,64,768]{2,1,0:T(8,128)(2,1)S(1)}, bf16[4,64,768]{2,1,0:T(8,128)(2,1)S(1)}, u32[]{:S(2)}, u32[]{:S(2)}) collective-permute-start(bf16[4,64,768]{2,1,0:T(8,128)(2,1)S(1)} %get-tuple-element.118), channel_id=1, source_target_pairs={{0,3},{1,2},{2,1},{3,0},{4,7},{5,6},{6,5},{7,4},{8,11},{9,10},{10,... | collective-permute-start | bytes 1179656 | tf_op jit(solution)/shard_map/ppermute | solution.py:515
  127.3 9.6 %collective-permute-start.25 = (bf16[4,64,768]{2,1,0:T(8,128)(2,1)S(1)}, bf16[4,64,768]{2,1,0:T(8,128)(2,1)S(1)}, u32[]{:S(2)}, u32[]{:S(2)}) collective-permute-start(bf16[4,64,768]{2,1,0:T(8,128)(2,1)S(1)} %get-tuple-element.120), channel_id=1, source_target_pairs={{0,4},{4,0},{8,12},{12,8},{1,5},{5,1},{9,13},{13,9},{2,6},{6,2},{1... | collective-permute-start | bytes 1179656 | tf_op jit(solution)/shard_map/ppermute | solution.py:515
  137.3 7.8 %collective-permute-start.30 = (bf16[64,1280]{1,0:T(8,128)(2,1)S(1)}, bf16[64,1280]{1,0:T(8,128)(2,1)S(1)}, u32[]{:S(2)}, u32[]{:S(2)}) collective-permute-start(bf16[64,1280]{1,0:T(8,128)(2,1)S(1)} %get-tuple-element.126), channel_id=1, source_target_pairs={{0,12},{4,8},{8,4},{12,0},{1,13},{5,9},{9,5},{13,1},{2,14},{6,10},... | collective-permute-start | bytes 491528 | tf_op jit(solution)/shard_map/ppermute | solution.py:515
  138.2 6.9 %collective-permute-start.29 = (bf16[64,1280]{1,0:T(8,128)(2,1)S(1)}, bf16[64,1280]{1,0:T(8,128)(2,1)S(1)}, u32[]{:S(2)}, u32[]{:S(2)}) collective-permute-start(bf16[64,1280]{1,0:T(8,128)(2,1)S(1)} %get-tuple-element.127), channel_id=1, source_target_pairs={{0,8},{4,12},{8,0},{12,4},{1,9},{5,13},{9,1},{13,5},{2,10},{6,14},... | collective-permute-start | bytes 491528 | tf_op jit(solution)/shard_map/ppermute | solution.py:515
  140.8 7.5 %collective-permute-start.33 = (bf16[64,1280]{1,0:T(8,128)(2,1)S(1)}, bf16[64,1280]{1,0:T(8,128)(2,1)S(1)}, u32[]{:S(2)}, u32[]{:S(2)}) collective-permute-start(bf16[64,1280]{1,0:T(8,128)(2,1)S(1)} %get-tuple-element.123), channel_id=1, source_target_pairs={{0,3},{1,2},{2,1},{3,0},{4,7},{5,6},{6,5},{7,4},{8,11},{9,10},{10,... | collective-permute-start | bytes 491528 | tf_op jit(solution)/shard_map/ppermute | solution.py:515
  180.2 20.2 %collective-permute-start.34 = (bf16[64,2560]{1,0:T(8,128)(2,1)S(1)}, bf16[64,2560]{1,0:T(8,128)(2,1)S(1)}, u32[]{:S(2)}, u32[]{:S(2)}) collective-permute-start(bf16[64,2560]{1,0:T(8,128)(2,1)S(1)} %bitcast.50), channel_id=1, source_target_pairs={{0,16},{16,0},{1,17},{17,1},{2,18},{18,2},{3,19},{19,3},{4,20},{20... | collective-permute-start | bytes 983048 | tf_op jit(solution)/shard_map/ppermute | solution.py:511
  (23 other events, 466.0 us)

commit v3 on v2

v3 whole, which is shorter than its diff:
```python
import functools

import jax
import jax.numpy as jnp
from jax import lax
from jax.experimental import pallas as pl
from jax.experimental.pallas import tpu as pltpu
from jax.sharding import Mesh
from jax.sharding import PartitionSpec as P

BLK = 256
HEAD_WIDTH = 256

norm_eps = 1e-06
beta_first = 0.9
beta_second = 0.95
learn_rate = 0.01
step_number = 10.0
update_eps = 1e-08
ratio_eps = 1e-06

OWN = ("x", "y")
SWAP = ((0, 1), (1, 0))

ROUNDS = (
    (("x", 1), ("x", 3), ("y", 1), ("y", 3)),
    (("y", 1), ("y", 3), ("x", 1), ("x", 3)),
    (("x", 3), ("x", 1), ("y", 3), ("y", 1)),
    (("y", 3), ("y", 1), ("x", 3), ("x", 1)),
)


def rms_scale(values):
    return values * lax.rsqrt(jnp.mean(values * values, axis=-1, keepdims=True) + norm_eps)


def sigmoid(values):
    return 1.0 / (1.0 + jnp.exp(-values))


def allowed_mask(length):
    row = lax.broadcasted_iota(jnp.int32, (BLK, BLK), 0)
    col = lax.broadcasted_iota(jnp.int32, (BLK, BLK), 1)
    return ((col <= row) & (row < length)).astype(jnp.float32) * (1.0 / BLK)


def dot_nt(left, right):
    return lax.dot_general(
        left, right, (((1,), (1,)), ((), ())), preferred_element_type=jnp.float32
    )


def dot_tn(left, right):
    return lax.dot_general(
        left, right, (((0,), (0,)), ((), ())), preferred_element_type=jnp.float32
    )


def dot_nn(left, right):
    return jnp.dot(left, right, preferred_element_type=jnp.float32)


def silu_slope(values):
    sig = sigmoid(values)
    act = values * sig
    return act, sig + act * (1.0 - sig)


def link_bits(place, turn):
    high, odd = place >> 1, (place >> 1) ^ (place & 1)
    return odd + 2 * high if turn < 2 else high + 2 * odd


def gather_slot(mask, turn):
    one, two = (mask >> 2, mask & 3) if turn % 2 == 0 else (mask & 3, mask >> 2)
    return link_bits(one, turn) + 4 * link_bits(two, turn)


def scatter_slot(mask, turn):
    one, two = (mask >> 2, mask & 3) if turn % 2 == 0 else (mask & 3, mask >> 2)
    return one + 4 * link_bits(two, turn)


def place_rows(turn, own, near, far, store):
    count, rows, _ = near.shape
    for mask in range(2 * count):
        slot = gather_slot(mask, turn)
        block = near[slot] if slot < count else far[slot - count]
        store(pl.ds(pl.multiple_of((own ^ mask) * rows, rows), rows), block)


def forward_kernel(
    place,
    lengths,
    normed,
    q_near,
    q_far,
    k_near,
    k_far,
    v_near,
    v_far,
    g_near,
    g_far,
    projected,
    scores,
    mixed,
    outer,
    weight,
):
    count, rows, width = mixed.shape
    share = outer.shape[1] // 4

    @pl.when(pl.program_id(0) == 0)
    def _():
        for turn, near, far, column in (
            (0, q_near, q_far, 0),
            (1, k_near, k_far, 2 * width),
            (2, v_near, v_far, width),
            (3, g_near, g_far, None),
        ):

            def store(at, block, turn=turn, column=column):
                if column is not None:
                    weight[at, column : column + width] = block[:, :width]
                outer[at, turn * share : (turn + 1) * share] = block[:, block.shape[1] - share :]

            place_rows(turn, place[0], near, far, store)

    projected[...] = dot_nn(normed[...].reshape(count * rows, -1), weight[...]).reshape(
        projected.shape
    )
    for item in range(count):
        proj = projected[item]
        held = (proj * sigmoid(proj)).astype(jnp.bfloat16)
        allowed = allowed_mask(lengths[pl.program_id(0) * count + item])
        for start in range(0, width, HEAD_WIDTH):
            queries, values, key_part = (
                held[:, part * width + start : part * width + start + HEAD_WIDTH]
                for part in range(3)
            )
            score = dot_nt(queries, key_part) * HEAD_WIDTH ** (-0.5)
            scores[item, start // HEAD_WIDTH] = score
            attention = (score * sigmoid(score) * allowed).astype(jnp.bfloat16)
            mixed[item, :, start : start + HEAD_WIDTH] = dot_nn(attention, values)


def gating_kernel(
    place,
    normed,
    near,
    far,
    masked,
    keep,
    recv,
    mixed,
    gating_out,
    grad_gated,
    stats,
    weight,
):
    count, rows, width = mixed.shape

    @pl.when(pl.program_id(0) == 0)
    def _():
        def store(at, block):
            weight[at, :] = block

        place_rows(3, place[0], near, far, store)

    proj = dot_nn(normed[...].reshape(count * rows, -1), weight[...])
    gating_out[...] = proj.reshape(gating_out.shape)
    core = place[1]
    mine = masked[:, :, pl.ds(pl.multiple_of(core * width, width), width)]
    others = masked[:, :, pl.ds(pl.multiple_of((1 - core) * width, width), width)]
    grad = (
        dot_nt(mine.reshape(count * rows, width), keep[...])
        + dot_nt(others.reshape(count * rows, width), recv[...])
    ).astype(jnp.bfloat16)
    grad_gated[...] = grad.reshape(grad_gated.shape)
    mix = mixed[...].reshape(count * rows, width)
    square = jnp.sum(mix * mix, axis=1, keepdims=True)
    cross = jnp.sum(
        grad.astype(jnp.float32) * (proj * sigmoid(proj)) * mix, axis=1, keepdims=True
    )
    lane = lax.broadcasted_iota(jnp.int32, (count * rows, 128), 1)
    stats[...] = jnp.where(lane == 0, square, cross).reshape(stats.shape)


def norm_scale(model_width, stats, stats_other):
    total = (stats[...] + stats_other[...]).reshape(-1, stats.shape[2])
    inv = lax.rsqrt(total[:, 0:1] / model_width + norm_eps)
    return inv, inv * inv * inv * (total[:, 1:2] / model_width)


def outer_kernel(place, projected, mixed, stats, stats_other, masked, term, total):
    width = mixed.shape[2]
    inv, _ = norm_scale(2 * width, stats, stats_other)
    proj = projected[...].reshape(-1, width)
    gated = (mixed[...].reshape(-1, width) * inv * (proj * sigmoid(proj))).astype(jnp.bfloat16)
    step = pl.program_id(0)
    for side in range(2):
        column = (place[1] + side) % 2
        part = masked[:, :, pl.ds(pl.multiple_of(column * width, width), width)]
        value = dot_tn(gated, part.reshape(-1, width))

        @pl.when(step == 0)
        def _():
            total[side] = value

        @pl.when(step > 0)
        def _():
            total[side] += value

    @pl.when(step == pl.num_programs(0) - 1)
    def _():
        term[...] = total[...].astype(jnp.bfloat16)


def backward_kernel(
    lengths, gating_in, projected, scores, mixed, grad_gated, stats, stats_other, grads
):
    width = mixed.shape[2]
    inv, back = norm_scale(2 * width, stats, stats_other)
    gating, slope = silu_slope(gating_in[0])
    mix = mixed[0]
    grad = grad_gated[0].astype(jnp.float32)
    grads[0, :, :width] = (grad * (mix * inv) * slope).astype(jnp.bfloat16)
    grad_mixed = (inv * (grad * gating) - mix * back).astype(jnp.bfloat16)
    allowed = allowed_mask(lengths[pl.program_id(0)])
    for start in range(0, width, HEAD_WIDTH):
        (queries, queries_slope), (values, values_slope), (key_part, keys_slope) = (
            silu_slope(projected[0, :, part * width + start : part * width + start + HEAD_WIDTH])
            for part in range(3)
        )
        act, slope = silu_slope(scores[0, start // HEAD_WIDTH])
        attention = (act * allowed).astype(jnp.bfloat16)
        grad_head = grad_mixed[:, start : start + HEAD_WIDTH]
        grad_att = dot_nt(grad_head, values.astype(jnp.bfloat16)).astype(jnp.bfloat16)
        grad_score = (
            grad_att.astype(jnp.float32) * allowed * slope * HEAD_WIDTH ** (-0.5)
        ).astype(jnp.bfloat16)
        for part, (grad_part, side) in enumerate(
            (
                (dot_tn(attention, grad_head), values_slope),
                (dot_nn(grad_score, key_part.astype(jnp.bfloat16)), queries_slope),
                (dot_tn(grad_score, queries.astype(jnp.bfloat16)), keys_slope),
            ),
            1,
        ):
            held = grad_part.astype(jnp.bfloat16).astype(jnp.float32)
            at = part * width + start
            grads[0, :, at : at + HEAD_WIDTH] = (held * side).astype(jnp.bfloat16)


def terms_kernel(place, normed_t, grads, keep, recv, *refs):
    outs, held, sems = refs[:8], refs[8:12], refs[12]
    step = pl.program_id(0)
    slots, rows, _ = held[0].shape
    width = grads.shape[1]
    half = keep.shape[0] // rows

    def copies(turn):
        return [
            pltpu.make_async_copy(
                held[turn].at[pl.ds(side * (slots // 2), slots // 2)],
                outs[2 * turn + side],
                sems.at[2 * turn + side],
            )
            for side in range(2)
        ]

    for turn in range(4):

        @pl.when(step == turn)
        def _(turn=turn):
            term = dot_nn(normed_t[...], grads[...]).astype(jnp.bfloat16)
            for block in range(slots):
                slot = scatter_slot(block ^ place[0], turn)
                held[turn][slot, :, :width] = term[block * rows : (block + 1) * rows]
            share = held[turn].shape[2] - width
            cut = slice(turn * share, (turn + 1) * share)
            for side, outer in ((place[1], keep), (1 - place[1], recv)):
                for block in range(half):
                    slot = scatter_slot((side * half + block) ^ place[0], turn)
                    held[turn][slot, :, width:] = outer[block * rows : (block + 1) * rows, cut]
            for copy in copies(turn):
                copy.start()

    @pl.when(step == 3)
    def _():
        for turn in range(4):
            for copy in copies(turn):
                copy.wait()


def rows_of(*dims, some=1):
    return pl.BlockSpec((some, *dims), lambda i, *_: (i,) + (0,) * len(dims))


def whole(*dims):
    return pl.BlockSpec(
        dims, lambda i, *_: (0,) * len(dims), pipeline_mode=pl.Buffered(buffer_count=1)
    )


def columns_of(value, width, at):
    return pl.BlockSpec(
        (*value.shape[:-1], width),
        lambda i, *_: (0,) * (value.ndim - 1) + (at,),
        pipeline_mode=pl.Buffered(buffer_count=1),
    )


def call(kernel, name, grid, prefetch, in_specs, out, inputs, scratch=(), room=18):
    moved = sum(v.size * v.dtype.itemsize for v in inputs)
    return pl.pallas_call(
        kernel,
        grid_spec=pltpu.PrefetchScalarGridSpec(
            num_scalar_prefetch=len(prefetch),
            grid=grid,
            in_specs=in_specs,
            out_specs=[spec for spec, _, _ in out],
            scratch_shapes=list(scratch),
        ),
        out_shape=[jax.ShapeDtypeStruct(shape, dtype) for _, shape, dtype in out],
        compiler_params=pltpu.CompilerParams(vmem_limit_bytes=room * 1024 * 1024),
        cost_estimate=pl.CostEstimate(flops=1, bytes_accessed=1, transcendentals=0),
        name=name,
    )(*prefetch, *inputs)


def attention_forward(place, lengths, normed, queries, keys_in, values, gating):
    count, rows, depth = normed.shape
    width = depth // 2
    heads = width // HEAD_WIDTH
    held = (*queries, *keys_in, *values)
    return call(
        forward_kernel,
        "attention_forward",
        (count // 2,),
        (place, lengths),
        [rows_of(rows, depth, some=2)]
        + [whole(*part.shape) for part in held]
        + [columns_of(part, width // 4, 4) for part in gating],
        [
            (rows_of(rows, 3 * width, some=2), (count, rows, 3 * width), jnp.float32),
            (rows_of(heads, rows, rows, some=2), (count, heads, rows, rows), jnp.float32),
            (rows_of(rows, width, some=2), (count, rows, width), jnp.float32),
            (whole(depth, width), (depth, width), jnp.bfloat16),
        ],
        (normed, *held, *gating),
        [pltpu.VMEM((depth, 3 * width), jnp.bfloat16)],
        room=28,
    )


def gating_forward(place, normed, gating, masked, keep, recv, mixed):
    count, rows, depth = normed.shape
    width = mixed.shape[2]
    return call(
        gating_kernel,
        "gating_forward",
        (count // 2,),
        (place,),
        [
            rows_of(rows, depth, some=2),
            *(columns_of(part, width, 0) for part in gating),
            rows_of(rows, depth, some=2),
            whole(*keep.shape),
            whole(*recv.shape),
            rows_of(rows, width, some=2),
        ],
        [
            (rows_of(rows, width, some=2), (count, rows, width), jnp.float32),
            (rows_of(rows, width, some=2), (count, rows, width), jnp.bfloat16),
            (rows_of(rows, 128, some=2), (count, rows, 128), jnp.float32),
        ],
        (normed, *gating, masked, keep, recv, mixed),
        [pltpu.VMEM((depth, width), jnp.bfloat16)],
        room=18,
    )


def stats_specs(count, rows, some=1):
    steps = count // some
    return [
        rows_of(rows, 128, some=some),
        pl.BlockSpec((some, rows, 128), lambda i, *_: ((i + steps // 2) % steps, 0, 0)),
    ]


def outer_term(place, gating, mixed, stats, stats_other, masked):
    count, rows, width = mixed.shape
    block = rows_of(rows, width, some=2)
    shape = (2, width, width)
    return call(
        outer_kernel,
        "outer_term",
        (count // 2,),
        (place,),
        [block, block, *stats_specs(count, rows, 2), rows_of(rows, 2 * width, some=2)],
        [(whole(*shape), shape, jnp.bfloat16)],
        (gating, mixed, stats, stats_other, masked),
        [pltpu.VMEM(shape, jnp.float32)],
    )[0]


def attention_back(lengths, gating, projected, scores, mixed, grad_gated, stats, stats_other):
    count, rows, width = mixed.shape
    heads = width // HEAD_WIDTH
    block = rows_of(rows, width)
    return call(
        backward_kernel,
        "attention_back",
        (count,),
        (lengths,),
        [
            block,
            rows_of(rows, 3 * width),
            rows_of(heads, rows, rows),
            block,
            block,
            *stats_specs(count, rows),
        ],
        [(rows_of(rows, 4 * width), (count, rows, 4 * width), jnp.bfloat16)],
        (gating, projected, scores, mixed, grad_gated, stats, stats_other),
    )[0]


def terms(place, owned, normed_t, grads, keep, recv):
    depth, rows = normed_t.shape
    width = grads.shape[1] // 4
    columns = width + keep.shape[1] // 4
    shapes = [(depth // owned // 2, owned, columns)] * 8
    anywhere = pl.BlockSpec(memory_space=pl.ANY)
    outs = call(
        terms_kernel,
        "terms",
        (4,),
        (place,),
        [
            whole(depth, rows),
            pl.BlockSpec((rows, width), lambda i, *_: (0, i)),
            whole(*keep.shape),
            whole(*recv.shape),
        ],
        [(anywhere, shape, jnp.bfloat16) for shape in shapes],
        (normed_t, grads, keep, recv),
        [pltpu.VMEM((2 * half, *rest), jnp.bfloat16) for half, *rest in shapes[::2]]
        + [pltpu.SemaphoreType.DMA((8,))],
    )
    return [outs[2 * turn : 2 * turn + 2] for turn in range(4)]


def sum_squares(values):
    values = values.astype(jnp.float32)
    return jnp.sum(values * values)


def update_kernel(place, squares, mine, other, *refs):
    half = mine.shape[1] // 5
    model_width = 2 * half
    first = place[1] == 0
    owners = squares.shape[0] // 8
    total = sum(squares[8 * i : 8 * i + 1, 0:1] for i in range(owners))
    clip = jnp.minimum(1.0, jnp.sqrt(5.0 * model_width * model_width / (total + norm_eps)))
    for parts, (weight, moment, square, new_weight, new_moment, new_square) in (
        (range(4), (refs[0], refs[1], refs[2], refs[6], refs[7], refs[8])),
        (range(4, 5), (refs[3], refs[4], refs[5], refs[9], refs[10], refs[11])),
    ):
        update_sq = weight_sq = 0.0
        for part in parts:
            at = slice(part * half, (part + 1) * half)
            both = (mine[:, at].astype(jnp.float32), other[:, at].astype(jnp.float32))
            for core in (0, 1):
                grad = jnp.where(first, both[core], both[1 - core]) * clip
                start = (part - parts[0]) * model_width + core * half
                col = slice(start, start + half)
                held = beta_first * moment[:, col] + (1.0 - beta_first) * grad
                held_sq = beta_second * square[:, col] + (1.0 - beta_second) * grad * grad
                new_moment[:, col] = held
                new_square[:, col] = held_sq
                update = (held * (1.0 / (1.0 - beta_first**step_number))) / (
                    jnp.sqrt(held_sq * (1.0 / (1.0 - beta_second**step_number))) + update_eps
                )
                new_weight[:, col] = update
                update_sq += jnp.sum(update * update, axis=1, keepdims=True)
                held = weight[:, col].astype(jnp.float32)
                weight_sq += jnp.sum(held * held, axis=1, keepdims=True)
        ratio = learn_rate * jnp.sqrt(weight_sq) / (jnp.sqrt(update_sq) + ratio_eps)
        new_weight[...] = weight[...].astype(jnp.float32) - ratio * new_weight[...]


def update_rows(place, squares, mine, other, *state):
    rows = 16
    count = mine.shape[0] // rows

    def block(value):
        return pl.BlockSpec((rows, value.shape[1]), lambda i, *_: (i, 0))

    return call(
        update_kernel,
        "update_rows",
        (count,),
        (place,),
        [whole(*squares.shape)] + [block(v) for v in (mine, other, *state)],
        [(block(v), v.shape, jnp.float32) for v in state],
        (squares, mine, other, *state),
    )


def swap_cores(values):
    return lax.ppermute(values, "c", SWAP)


def over_link(values, axis, mask):
    return lax.ppermute(values, axis, [(i, i ^ mask) for i in range(4)])


def direct_round(blocks_of, groups):
    got = [[None] * 4, [None] * 4]
    for mask in (1, 3, 2):
        for group, axis in enumerate(("x", "y")):
            got[group][mask] = over_link(blocks_of(groups[group], mask), axis, mask)
    return got


def gather_parts(parts, prepare, join):
    held = [part[None] for part in parts]
    for step in range(3):
        got = [over_link(part, *ROUNDS[turn][step]) for turn, part in enumerate(held)]
        held = [jnp.concatenate(pair, axis=0) for pair in zip(held, got)]
        if step == 1:
            held, beside = lax.optimization_barrier((held, beside))
        else:
            held = lax.optimization_barrier(held)
        if step == 0:
            held[0], beside = prepare(held[0])
    far = [over_link(part, *ROUNDS[turn][3]) for turn, part in enumerate(held)]
    far, beside = lax.optimization_barrier((far, join(beside)))
    return list(zip(held, far)), beside


def add_blocks(*blocks):
    return sum(block.astype(jnp.float32) for block in blocks).astype(jnp.bfloat16)


def scatter_parts(pairs):
    for step in (1, 0):
        got = [over_link(far, *ROUNDS[turn][2 + step]) for turn, (_, far) in enumerate(pairs)]
        mine, got = lax.optimization_barrier(([near for near, _ in pairs], got))
        held = [add_blocks(*pair) for pair in zip(mine, got)]
        if step:
            pairs = [jnp.split(part, 2, axis=0) for part in held]
    groups = [jnp.concatenate([held[0], held[2]], axis=2), jnp.concatenate([held[1], held[3]], axis=2)]
    got = direct_round(lambda group, mask: group[mask], groups)
    return [add_blocks(group[0], *blocks[1:]) for group, blocks in zip(groups, got)]


def exchange(blocks, axes):
    return lax.all_to_all(blocks, axes, 0, 0, tiled=True)


def per_device(
    tokens,
    cotangent,
    lengths,
    norm_gain,
    weight_in,
    weight_out,
    moment_in,
    square_in,
    moment_out,
    square_out,
):
    slots, rows, model_width = tokens.shape
    half = model_width // 2
    share = half // 4
    core = lax.axis_index("c")
    own = lax.axis_index(OWN)
    owners = lax.axis_size(OWN)
    planes = lax.axis_size("z")
    owned = weight_in.shape[0]
    place = jnp.stack([own, core]).astype(jnp.int32)

    mine = [
        lax.dynamic_slice_in_dim(weight_in, part * model_width + core * half, half, axis=1)
        for part in range(4)
    ]
    mine_out = lax.dynamic_slice_in_dim(weight_out, core * half, half, axis=1)
    def prepare(got):
        got, token_rows, cot_rows, lengths_other = lax.optimization_barrier(
            (got, tokens, cotangent, swap_cores(lengths))
        )
        normed = (rms_scale(token_rows.astype(jnp.float32)) * norm_gain).astype(jnp.bfloat16)
        row_index = jnp.arange(rows, dtype=jnp.int32)
        live = row_index[None, :] < lengths[:, None]
        masked = jnp.where(live[:, :, None], cot_rows, jnp.zeros_like(cot_rows))
        mine = jnp.concatenate([normed, masked], axis=0)
        return got, (mine, swap_cores(mine), lengths_other)

    def join(made):
        mine, other, lengths_other = made
        normed, masked = (
            jnp.concatenate([side[at : at + slots] for side in (mine, other)], axis=0)
            for at in (0, slots)
        )
        all_lengths = jnp.concatenate([lengths, lengths_other], axis=0)
        return normed, masked, all_lengths, normed.reshape(-1, model_width).T

    (queries, keys_in, values, gating), (normed, masked, all_lengths, normed_t) = gather_parts(
        [
            jnp.concatenate([mine[part], mine_out[:, at * share : (at + 1) * share]], axis=1)
            for at, part in enumerate((2, 3, 1, 0))
        ],
        prepare,
        join,
    )

    projected, scores, mixed, outer_cols = attention_forward(
        place, all_lengths, normed, queries, keys_in, values, gating
    )
    outer_cols = outer_cols.reshape(2, half, half)
    keep = lax.dynamic_index_in_dim(outer_cols, core, axis=0, keepdims=False)
    recv = swap_cores(lax.dynamic_index_in_dim(outer_cols, 1 - core, axis=0, keepdims=False))
    gating, grad_gated, stats = gating_forward(place, normed, gating, masked, keep, recv, mixed)
    stats_other = swap_cores(stats)
    outer = outer_term(place, gating, mixed, stats, stats_other, masked)
    outer_recv = swap_cores(outer[1])
    grads = attention_back(
        all_lengths, gating, projected, scores, mixed, grad_gated, stats, stats_other
    )
    term_g, term_v, term_q, term_k = terms(
        place, owned, normed_t, grads.reshape(-1, 4 * half), outer[0], outer_recv
    )
    part_gq, part_vk = scatter_parts([term_g, term_v, term_q, term_k])
    wide = half + share
    sides = (part_gq, part_vk)
    part = jnp.concatenate(
        [side[:, at : at + half] for at in (0, wide) for side in sides]
        + [side[:, at : at + share] for at in (half, wide + half) for side in sides],
        axis=1,
    )

    piece = jnp.sum(
        exchange(part, "z").reshape(planes, owned // planes, -1).astype(jnp.float32), axis=0
    ).astype(jnp.bfloat16)
    shard = exchange(
        jnp.broadcast_to(piece[None], (planes, *piece.shape)).reshape(owned, -1), "z"
    )
    other = swap_cores(shard)
    squares = exchange(
        jnp.broadcast_to(sum_squares(shard), (2 * owners * 8, 128)), ("c", *OWN)
    )
    return update_rows(
        place,
        squares,
        shard,
        other,
        weight_in,
        moment_in,
        square_in,
        weight_out,
        moment_out,
        square_out,
    )


def solution(mesh):
    fine = Mesh(mesh.devices.reshape(8, 2, 4, 4), ("z", "c", "x", "y"))
    histories = ("z", "c", "x", "y")
    placed = (
        P(histories, None, None),
        P(histories, None, None),
        P(histories),
        P(),
        P(OWN, None),
        P(OWN, None),
        P(OWN, None),
        P(OWN, None),
        P(OWN, None),
        P(OWN, None),
    )
    return jax.shard_map(
        per_device,
        mesh=fine,
        in_specs=placed,
        out_specs=(P(OWN, None),) * 6,
        check_vma=False,
    )
```

time: 205 us -> 193 us (0.941)
  waiting for transfers between devices: 53.5 us -> 46.1 us
  Pallas kernels: 38.5 us -> 33.7 us
  starting transfers between devices: 46.3 us -> 49 us
  local copies, waits for them, and re-layouts: 11.5 us -> 8.93 us
    ppermute x28 -> x30, waiting for transfers between devices: 50.4 us -> 42.9 us  [over_link(): return lax.ppermute(values, axis, [(i, i ^ mask) for i in range(4)])]
    pallas_call x6, Pallas kernels: 38.5 us -> 33.7 us  [call(): pl.pallas_call(kernel, grid_spec=pltpu.PrefetchScalarGridSpec(num_scalar_...]
    concatenate x5 -> x16, other arithmetic: 3.35 us -> 7.3 us  [the longest x12 5.14 us: gather_parts(): held = [jnp.concatenate(pair, axis=0) for pair in zip(held, got)]]
    slice x5 -> x2, local copies, waits for them, and re-layouts: 6.74 us -> 2.84 us  [the longest x1 1.91 us: join(): side[at:at + slots]]
    ppermute x7 -> x6, starting transfers between devices: 15.5 us -> 17.1 us  [swap_cores(): return lax.ppermute(values, 'c', SWAP)]
    ppermute x28 -> x30, starting transfers between devices: 30.8 us -> 31.8 us  [over_link(): return lax.ppermute(values, axis, [(i, i ^ mask) for i in range(4)])]
  transfers between devices with their start and end apart: 35 -> 36, of which waited for: 18 -> 18; matrix products, arithmetic and copies ran while one was open for 8% -> 7% of each run, Pallas kernels for 3% -> 3%
where the time goes in v3:
time: 193 us
  starting transfers between devices  49 us (25%)
  waiting for transfers between devices  46.1 us (24%)
  blocking collectives  41.8 us (22%)
  Pallas kernels  33.7 us (17%)
  other arithmetic  12 us (6%)
  local copies, waits for them, and re-layouts  8.93 us (5%)
    ppermute x30, waiting for transfers between devices, over_link(): return lax.ppermute(values, axis, [(i, i ^ mask) for i in range(4)])  42.9 us
    all_to_all x3, blocking collectives, exchange(): return lax.all_to_all(blocks, axes, 0, 0, tiled=True)  41.8 us
    pallas_call x6, Pallas kernels, call(): pl.pallas_call(kernel, grid_spec=pltpu.PrefetchScalarGridSpec(num_scalar_...  33.7 us
    ppermute x30, starting transfers between devices, over_link(): return lax.ppermute(values, axis, [(i, i ^ mask) for i in range(4)])  31.8 us
    ppermute x6, starting transfers between devices, swap_cores(): return lax.ppermute(values, 'c', SWAP)  17.1 us
    concatenate x12, other arithmetic, gather_parts(): held = [jnp.concatenate(pair, axis=0) for pair in zip(held, got)]  5.14 us
  transfers between devices with their start and end apart: 36, of which 18 were waited for; matrix products, arithmetic and copies ran while one was open for 7% of the time, Pallas kernels for 3%

profile of v3, /device:TPU:1, one launch (start us, length us, event | category | flops | bytes accessed | tf_op | source)
XLA Modules:
  0.0 192.7 jit_solution(13794355106471617161)
XLA Ops:
  2.6 2.1 %collective-permute-start = (bf16[1,64,640]{2,1,0:T(8,128)(2,1)S(1)}, bf16[1,64,640]{2,1,0:T(8,128)(2,1)S(1)}, u32[]{:S(2)}, u32[]{:S(2)}) collective-permute-start(bf16[1,64,640]{2,1,0:T(8,128)(2,1)S(1)} %maximum_bitcast_fusion), channel_id=1, source_target_pairs={{0,4},{4,0},{8,12},{12,8},{1,5},{5,1},{9,13},{13,9},{2,6},{6,2},{1... | collective-permute-start | bytes 245768 | tf_op jit(solution)/shard_map/ppermute | solution.py:517
  8.0 2.0 %collective-permute-start.3 = (bf16[1,64,640]{2,1,0:T(8,128)(2,1)S(1)}, bf16[1,64,640]{2,1,0:T(8,128)(2,1)S(1)}, u32[]{:S(2)}, u32[]{:S(2)}) collective-permute-start(bf16[1,64,640]{2,1,0:T(8,128)(2,1)S(1)} %maximum_bitcast_fusion.3), channel_id=1, source_target_pairs={{0,3},{1,2},{2,1},{3,0},{4,7},{5,6},{6,5},{7,4},{8,11},{9,10},{10,... | collective-permute-start | bytes 245768 | tf_op jit(solution)/shard_map/ppermute | solution.py:517
  13.7 2.6 %collective-permute-start.9 = (bf16[4,256,1024]{2,1,0:T(8,128)(2,1)S(1)}, bf16[4,256,1024]{2,1,0:T(8,128)(2,1)S(1)}, u32[]{:S(2)}, u32[]{:S(2)}) collective-permute-start(bf16[4,256,1024]{2,1,0:T(8,128)(2,1)S(1)} %pad_maximum_fusion), channel_id=1, source_target_pairs={{0,16},{16,0},{1,17},{17,1},{2,18},{18,2},{3,19},{19,3},{4,20},{20... | collective-permute-start | bytes 6291464 | tf_op jit(solution)/shard_map/ppermute | solution.py:513
  19.1 4.2 %collective-permute-done.5 = bf16[2,64,640]{2,1,0:T(8,128)(2,1)S(1)} collective-permute-done((bf16[2,64,640]{2,1,0:T(8,128)(2,1)S(1)}, bf16[2,64,640]{2,1,0:T(8,128)(2,1)S(1)}, u32[]{:S(2)}, u32[]{:S(2)}) %collective-permute-start.5) | collective-permute-done | bytes 163872 | tf_op jit(solution)/shard_map/ppermute | solution.py:517
  29.8 3.7 %collective-permute-done.10 = bf16[4,64,640]{2,1,0:T(8,128)(2,1)} collective-permute-done((bf16[4,64,640]{2,1,0:T(8,128)(2,1)S(1)}, bf16[4,64,640]{2,1,0:T(8,128)(2,1)}, u32[]{:S(2)}, u32[]{:S(2)}) %collective-permute-start.10) | collective-permute-done | bytes 327712 | tf_op jit(solution)/shard_map/ppermute | solution.py:517
  35.4 2.0 %pad_maximum_fusion.4.k_near = bf16[8,64,640]{2,1,0:T(8,128)(2,1)} fusion(bf16[4,64,640]{2,1,0:T(8,128)(2,1)} %collective-permute-done.11, bf16[4,64,640]{2,1,0:T(8,128)(2,1)S(1)} %pad_maximum_fusion.8), kind=kLoop, calls=%fused_computation.26 | loop fusion | flops 327680 | bytes 1310720 | tf_op jit(solution)/shard_map/concatenate | solution.py:532
  38.4 2.0 %collective-permute-start.14 = (bf16[8,64,640]{2,1,0:T(8,128)(2,1)}, bf16[8,64,640]{2,1,0:T(8,128)(2,1)}, u32[]{:S(2)}, u32[]{:S(2)}) collective-permute-start(bf16[8,64,640]{2,1,0:T(8,128)(2,1)} %pad_maximum_fusion.3.q_near), channel_id=1, source_target_pairs={{0,3},{1,2},{2,1},{3,0},{4,7},{5,6},{6,5},{7,4},{8,11},{9,10},{10,... | collective-permute-start | bytes 1966088 | tf_op jit(solution)/shard_map/ppermute | solution.py:517
  44.3 2.6 %copy.17 = bf16[1024,1024]{0,1:T(8,128)(2,1)} copy(bf16[1024,1024]{1,0:T(8,128)(2,1)S(1)} %bitcast.47) | data formatting | bytes 4194304 | tf_op jit(solution)/shard_map/reshape | solution.py:609
  48.7 5.1 %collective-permute-done.14.q_far = bf16[8,64,640]{2,1,0:T(8,128)(2,1)} collective-permute-done((bf16[8,64,640]{2,1,0:T(8,128)(2,1)}, bf16[8,64,640]{2,1,0:T(8,128)(2,1)}, u32[]{:S(2)}, u32[]{:S(2)}) %collective-permute-start.14) | collective-permute-done | bytes 655392 | tf_op jit(solution)/shard_map/ppermute | solution.py:517
  53.8 1.9 %collective-permute-done.15.k_far = bf16[8,64,640]{2,1,0:T(8,128)(2,1)} collective-permute-done((bf16[8,64,640]{2,1,0:T(8,128)(2,1)}, bf16[8,64,640]{2,1,0:T(8,128)(2,1)}, u32[]{:S(2)}, u32[]{:S(2)}) %collective-permute-start.15) | collective-permute-done | bytes 655392 | tf_op jit(solution)/shard_map/ppermute | solution.py:517
  56.1 8.4 %attention_forward.1 = (f32[4,256,1536]{2,1,0:T(8,128)S(1)}, f32[4,2,256,256]{3,2,1,0:T(8,128)S(1)}, f32[4,256,512]{2,1,0:T(8,128)S(1)}, bf16[1024,512]{1,0:T(8,128)(2,1)S(1)}) custom-call(s32[2]{0:T(128)S(1)} %pad_add_fusion.place, s32[4]{0:T(128)S(1)} %pad_add_fusion.1.lengths, bf16[4,256,1024]{2,1,0:T(8,128)(2,1)S(1)} %pad_maximum_fusion.1.normed, ...), custom_call_target="tpu_custom_call" | custom-call | flops 1 | bytes 1 | tf_op jit(solution)/shard_map/attention_forward/pallas_call | solution.py:316
  64.6 3.7 %collective-permute-start.18 = (bf16[512,512]{1,0:T(8,128)(2,1)S(1)}, bf16[512,512]{1,0:T(8,128)(2,1)S(1)}, u32[]{:S(2)}, u32[]{:S(2)}) collective-permute-start(bf16[512,512]{1,0:T(8,128)(2,1)S(1)} %get-tuple-element.128), channel_id=1, source_target_pairs={{0,16},{16,0},{1,17},{17,1},{2,18},{18,2},{3,19},{19,3},{4,20},{20... | collective-permute-start | bytes 1572872 | tf_op jit(solution)/shard_map/ppermute | solution.py:513
  69.8 3.7 %gating_forward.1 = (f32[4,256,512]{2,1,0:T(8,128)S(1)}, bf16[4,256,512]{2,1,0:T(8,128)(2,1)S(1)}, f32[4,256,128]{2,1,0:T(8,128)S(1)}) custom-call(s32[2]{0:T(128)S(1)} %pad_add_fusion.place, bf16[4,256,1024]{2,1,0:T(8,128)(2,1)S(1)} %pad_maximum_fusion.1.normed, bf16[8,64,640]{2,1,0:T(8,128)(2,1)S(1)} %pad_maximum_fusion.6.g_near.near, ...), custom_call_target="tpu_custom_call" | custom-call | flops 1 | bytes 1 | tf_op jit(solution)/shard_map/gating_forward/pallas_call | solution.py:316
  75.5 3.4 %outer_term.1 = bf16[2,512,512]{2,1,0:T(8,128)(2,1)S(1)} custom-call(s32[2]{0:T(128)S(1)} %pad_add_fusion.place, f32[4,256,512]{2,1,0:T(8,128)S(1)} %get-tuple-element.93.gating_in.projected, f32[4,256,512]{2,1,0:T(8,128)S(1)} %get-tuple-element.92.mixed, f32[4,256,128]{2,1,0:T(8,128)S(1)} %get-tuple-element.97.stats, ...), custom_call_target="tpu_custom_call" | custom-call | flops 1 | bytes 1 | tf_op jit(solution)/shard_map/outer_term/pallas_call | solution.py:316
  79.7 6.2 %attention_back.1 = bf16[4,256,2048]{2,1,0:T(8,128)(2,1)S(1)} custom-call(s32[4]{0:T(128)S(1)} %pad_add_fusion.1.lengths, f32[4,256,512]{2,1,0:T(8,128)S(1)} %get-tuple-element.93.gating_in.projected, f32[4,256,1536]{2,1,0:T(8,128)S(1)} %get-tuple-element.94.projected, f32[4,2,256,256]{3,2,1,0:T(8,128)S(1)} %get-tuple-element.95.scores, ...), custom_call_target="tpu_custom_call" | custom-call | flops 1 | bytes 1 | tf_op jit(solution)/shard_map/attention_back/pallas_call | solution.py:316
  86.0 8.2 %terms.1 = (bf16[8,64,640]{2,1,0:T(8,128)(2,1)S(1)}, bf16[8,64,640]{2,1,0:T(8,128)(2,1)S(1)}, bf16[8,64,640]{2,1,0:T(8,128)(2,1)S(1)}, bf16[8,64,640]{2,1,0:T(8,...) custom-call(s32[2]{0:T(128)S(1)} %pad_add_fusion.place, ...), custom_call_target="tpu_custom_call" | custom-call | flops 1 | bytes 1 | tf_op jit(solution)/shard_map/terms/pallas_call | solution.py:316
  96.5 15.2 %collective-permute-done.21 = bf16[8,64,640]{2,1,0:T(8,128)(2,1)S(1)} collective-permute-done((bf16[8,64,640]{2,1,0:T(8,128)(2,1)S(1)}, bf16[8,64,640]{2,1,0:T(8,128)(2,1)S(1)}, u32[]{:S(2)}, u32[]{:S(2)}) %collective-permute-start.21) | collective-permute-done | bytes 655392 | tf_op jit(solution)/shard_map/ppermute | solution.py:517
  117.7 3.2 %collective-permute-done.25 = bf16[4,64,640]{2,1,0:T(8,128)(2,1)S(1)} collective-permute-done((bf16[4,64,640]{2,1,0:T(8,128)(2,1)S(1)}, bf16[4,64,640]{2,1,0:T(8,128)(2,1)S(1)}, u32[]{:S(2)}, u32[]{:S(2)}) %collective-permute-start.25) | collective-permute-done | bytes 327712 | tf_op jit(solution)/shard_map/ppermute | solution.py:517
  132.8 3.0 %collective-permute-done.34 = bf16[64,1280]{1,0:T(8,128)(2,1)S(1)} collective-permute-done((bf16[64,1280]{1,0:T(8,128)(2,1)S(1)}, bf16[64,1280]{1,0:T(8,128)(2,1)S(1)}, u32[]{:S(2)}, u32[]{:S(2)}) %collective-permute-start.34) | collective-permute-done | bytes 163872 | tf_op jit(solution)/shard_map/ppermute | solution.py:517
  136.6 18.1 %all_to_all.25 = bf16[8,8,2560]{2,1,0:T(8,128)(2,1)} all-to-all(bf16[8,8,2560]{2,1,0:T(8,128)(2,1)S(1)} %bitcast.54), channel_id=1, replica_groups=mesh['z'=8,'c'=2,'x'=4,'y'=4] {'z'}, dimensions={0} | all-to-all | bytes 655360 | tf_op jit(solution)/shard_map/all_to_all | solution.py:561
  155.8 12.4 %all_to_all.26 = bf16[8,8,2560]{2,1,0:T(8,128)(2,1)S(1)} all-to-all(bf16[8,8,2560]{2,1,0:T(8,128)(2,1)S(1)} %broadcast_in_dim.43), channel_id=1, replica_groups=mesh['z'=8,'c'=2,'x'=4,'y'=4] {'z'}, dimensions={0} | all-to-all | bytes 655360 | tf_op jit(solution)/shard_map/all_to_all | solution.py:561
  168.2 7.9 %collective-permute-start.35 = (bf16[64,2560]{1,0:T(8,128)(2,1)S(1)}, bf16[64,2560]{1,0:T(8,128)(2,1)S(1)}, u32[]{:S(2)}, u32[]{:S(2)}) collective-permute-start(bf16[64,2560]{1,0:T(8,128)(2,1)S(1)} %bitcast.50), channel_id=1, source_target_pairs={{0,16},{16,0},{1,17},{17,1},{2,18},{18,2},{3,19},{19,3},{4,20},{20... | collective-permute-start | bytes 983048 | tf_op jit(solution)/shard_map/ppermute | solution.py:513
  177.6 11.2 %all_to_all.27 = f32[32,8,128]{2,1,0:T(8,128)S(1)} all-to-all(f32[32,8,128]{2,1,0:T(8,128)S(1)} %broadcast_in_dim.44), channel_id=1, replica_groups=mesh['z'=8,'c'=2,'x'=4,'y'=4] {'c','x','y'}, dimensions={0} | all-to-all | bytes 262144 | tf_op jit(solution)/shard_map/all_to_all | solution.py:561
  188.9 3.7 %update_rows.1 = (f32[64,4096]{1,0:T(8,128)}, f32[64,4096]{1,0:T(8,128)}, f32[64,4096]{1,0:T(8,128)}, f32[64,1024]{1,0:T(8,128)}, f32[64,1024]{1,0:T(8,128)}, /*index=5*/f32[64,1024]{1,0:T(8,128)}) custom-call(s32[2]{0:T(128)S(1)} %pad_add_fusion.place, f32[256,128]{1,0:T(8,128)S(1)} %bitcast.53, bf16[64,2560]{1,0:T(8,128)(2,1)S(1)} %bitcast.51, ...), custom_call_target="tpu_custom_call" | custom-call | flops 1 | bytes 1 | tf_op jit(solution)/shard_map/update_rows/pallas_call | solution.py:316
  (143 shorter events, 54.6 us)
Async XLA Ops:
  2.6 10.0 %collective-permute-start = (bf16[1,64,640]{2,1,0:T(8,128)(2,1)S(1)}, bf16[1,64,640]{2,1,0:T(8,128)(2,1)S(1)}, u32[]{:S(2)}, u32[]{:S(2)}) collective-permute-start(bf16[1,64,640]{2,1,0:T(8,128)(2,1)S(1)} %maximum_bitcast_fusion), channel_id=1, source_target_pairs={{0,4},{4,0},{8,12},{12,8},{1,5},{5,1},{9,13},{13,9},{2,6},{6,2},{1... | collective-permute-start | bytes 245768 | tf_op jit(solution)/shard_map/ppermute | solution.py:517
  4.7 7.9 %collective-permute-start.1 = (bf16[1,64,640]{2,1,0:T(8,128)(2,1)S(1)}, bf16[1,64,640]{2,1,0:T(8,128)(2,1)S(1)}, u32[]{:S(2)}, u32[]{:S(2)}) collective-permute-start(bf16[1,64,640]{2,1,0:T(8,128)(2,1)S(1)} %maximum_bitcast_fusion.1), channel_id=1, source_target_pairs={{0,1},{1,0},{2,3},{3,2},{4,5},{5,4},{6,7},{7,6},{8,9},{9,8},{10,11... | collective-permute-start | bytes 245768 | tf_op jit(solution)/shard_map/ppermute | solution.py:517
  13.7 10.6 %collective-permute-start.9 = (bf16[4,256,1024]{2,1,0:T(8,128)(2,1)S(1)}, bf16[4,256,1024]{2,1,0:T(8,128)(2,1)S(1)}, u32[]{:S(2)}, u32[]{:S(2)}) collective-permute-start(bf16[4,256,1024]{2,1,0:T(8,128)(2,1)S(1)} %pad_maximum_fusion), channel_id=1, source_target_pairs={{0,16},{16,0},{1,17},{17,1},{2,18},{18,2},{3,19},{19,3},{4,20},{20... | collective-permute-start | bytes 6291464 | tf_op jit(solution)/shard_map/ppermute | solution.py:513
  16.4 7.0 %collective-permute-start.5 = (bf16[2,64,640]{2,1,0:T(8,128)(2,1)S(1)}, bf16[2,64,640]{2,1,0:T(8,128)(2,1)S(1)}, u32[]{:S(2)}, u32[]{:S(2)}) collective-permute-start(bf16[2,64,640]{2,1,0:T(8,128)(2,1)S(1)} %pad_maximum_fusion.13), channel_id=1, source_target_pairs={{0,12},{4,8},{8,4},{12,0},{1,13},{5,9},{9,5},{13,1},{2,14},{6,10},... | collective-permute-start | bytes 491528 | tf_op jit(solution)/shard_map/ppermute | solution.py:517
  25.7 7.8 %collective-permute-start.10 = (bf16[4,64,640]{2,1,0:T(8,128)(2,1)S(1)}, bf16[4,64,640]{2,1,0:T(8,128)(2,1)}, u32[]{:S(2)}, u32[]{:S(2)}) collective-permute-start(bf16[4,64,640]{2,1,0:T(8,128)(2,1)S(1)} %pad_maximum_fusion.7), channel_id=1, source_target_pairs={{0,1},{1,0},{2,3},{3,2},{4,5},{5,4},{6,7},{7,6},{8,9},{9,8},{10,11... | collective-permute-start | bytes 983048 | tf_op jit(solution)/shard_map/ppermute | solution.py:517
  26.0 9.4 %collective-permute-start.11 = (bf16[4,64,640]{2,1,0:T(8,128)(2,1)S(1)}, bf16[4,64,640]{2,1,0:T(8,128)(2,1)}, u32[]{:S(2)}, u32[]{:S(2)}) collective-permute-start(bf16[4,64,640]{2,1,0:T(8,128)(2,1)S(1)} %pad_maximum_fusion.8), channel_id=1, source_target_pairs={{0,4},{4,0},{8,12},{12,8},{1,5},{5,1},{9,13},{13,9},{2,6},{6,2},{1... | collective-permute-start | bytes 983048 | tf_op jit(solution)/shard_map/ppermute | solution.py:517
  27.1 10.3 %collective-permute-start.12 = (bf16[4,64,640]{2,1,0:T(8,128)(2,1)S(1)}, bf16[4,64,640]{2,1,0:T(8,128)(2,1)S(1)}, u32[]{:S(2)}, u32[]{:S(2)}) collective-permute-start(bf16[4,64,640]{2,1,0:T(8,128)(2,1)S(1)} %pad_maximum_fusion.9), channel_id=1, source_target_pairs={{0,3},{1,2},{2,1},{3,0},{4,7},{5,6},{6,5},{7,4},{8,11},{9,10},{10,... | collective-permute-start | bytes 983048 | tf_op jit(solution)/shard_map/ppermute | solution.py:517
  28.0 10.4 %collective-permute-start.13 = (bf16[4,64,640]{2,1,0:T(8,128)(2,1)S(1)}, bf16[4,64,640]{2,1,0:T(8,128)(2,1)S(1)}, u32[]{:S(2)}, u32[]{:S(2)}) collective-permute-start(bf16[4,64,640]{2,1,0:T(8,128)(2,1)S(1)} %pad_maximum_fusion.10), channel_id=1, source_target_pairs={{0,12},{4,8},{8,4},{12,0},{1,13},{5,9},{9,5},{13,1},{2,14},{6,10},... | collective-permute-start | bytes 983048 | tf_op jit(solution)/shard_map/ppermute | solution.py:517
  38.4 15.4 %collective-permute-start.14 = (bf16[8,64,640]{2,1,0:T(8,128)(2,1)}, bf16[8,64,640]{2,1,0:T(8,128)(2,1)}, u32[]{:S(2)}, u32[]{:S(2)}) collective-permute-start(bf16[8,64,640]{2,1,0:T(8,128)(2,1)} %pad_maximum_fusion.3.q_near), channel_id=1, source_target_pairs={{0,3},{1,2},{2,1},{3,0},{4,7},{5,6},{6,5},{7,4},{8,11},{9,10},{10,... | collective-permute-start | bytes 1966088 | tf_op jit(solution)/shard_map/ppermute | solution.py:517
  40.4 15.4 %collective-permute-start.15 = (bf16[8,64,640]{2,1,0:T(8,128)(2,1)}, bf16[8,64,640]{2,1,0:T(8,128)(2,1)}, u32[]{:S(2)}, u32[]{:S(2)}) collective-permute-start(bf16[8,64,640]{2,1,0:T(8,128)(2,1)} %pad_maximum_fusion.4.k_near), channel_id=1, source_target_pairs={{0,12},{4,8},{8,4},{12,0},{1,13},{5,9},{9,5},{13,1},{2,14},{6,10},... | collective-permute-start | bytes 1966088 | tf_op jit(solution)/shard_map/ppermute | solution.py:517
  42.2 13.9 %collective-permute-start.16 = (bf16[8,64,640]{2,1,0:T(8,128)(2,1)}, bf16[8,64,640]{2,1,0:T(8,128)(2,1)}, u32[]{:S(2)}, u32[]{:S(2)}) collective-permute-start(bf16[8,64,640]{2,1,0:T(8,128)(2,1)} %pad_maximum_fusion.5.v_near), channel_id=1, source_target_pairs={{0,1},{1,0},{2,3},{3,2},{4,5},{5,4},{6,7},{7,6},{8,9},{9,8},{10,11... | collective-permute-start | bytes 1966088 | tf_op jit(solution)/shard_map/ppermute | solution.py:517
  42.2 13.9 %collective-permute-start.17 = (bf16[8,64,640]{2,1,0:T(8,128)(2,1)S(1)}, bf16[8,64,640]{2,1,0:T(8,128)(2,1)S(1)}, u32[]{:S(2)}, u32[]{:S(2)}) collective-permute-start(bf16[8,64,640]{2,1,0:T(8,128)(2,1)S(1)} %pad_maximum_fusion.6.g_near.near), channel_id=1, source_target_pairs={{0,4},{4,0},{8,12},{12,8},{1,5},{5,1},{9,13},{13,9},{2,6},{6,2},{1... | collective-permute-start | bytes 1966088 | tf_op jit(solution)/shard_map/ppermute | solution.py:517
  79.0 6.9 %collective-permute-start.20 = (bf16[512,512]{1,0:T(8,128)(2,1)S(1)}, bf16[512,512]{1,0:T(8,128)(2,1)S(1)}, u32[]{:S(2)}, u32[]{:S(2)}) collective-permute-start(bf16[512,512]{1,0:T(8,128)(2,1)S(1)} %get-tuple-element.126), channel_id=1, source_target_pairs={{0,16},{16,0},{1,17},{17,1},{2,18},{18,2},{3,19},{19,3},{4,20},{20... | collective-permute-start | bytes 1572872 | tf_op jit(solution)/shard_map/ppermute | solution.py:513
  94.2 17.5 %collective-permute-start.21 = (bf16[8,64,640]{2,1,0:T(8,128)(2,1)S(1)}, bf16[8,64,640]{2,1,0:T(8,128)(2,1)S(1)}, u32[]{:S(2)}, u32[]{:S(2)}) collective-permute-start(bf16[8,64,640]{2,1,0:T(8,128)(2,1)S(1)} %get-tuple-element.102), channel_id=1, source_target_pairs={{0,3},{1,2},{2,1},{3,0},{4,7},{5,6},{6,5},{7,4},{8,11},{9,10},{10,... | collective-permute-start | bytes 1966088 | tf_op jit(solution)/shard_map/ppermute | solution.py:517
  95.1 17.1 %collective-permute-start.22 = (bf16[8,64,640]{2,1,0:T(8,128)(2,1)S(1)}, bf16[8,64,640]{2,1,0:T(8,128)(2,1)S(1)}, u32[]{:S(2)}, u32[]{:S(2)}) collective-permute-start(bf16[8,64,640]{2,1,0:T(8,128)(2,1)S(1)} %get-tuple-element.103), channel_id=1, source_target_pairs={{0,12},{4,8},{8,4},{12,0},{1,13},{5,9},{9,5},{13,1},{2,14},{6,10},... | collective-permute-start | bytes 1966088 | tf_op jit(solution)/shard_map/ppermute | solution.py:517
  96.3 15.9 %collective-permute-start.23 = (bf16[8,64,640]{2,1,0:T(8,128)(2,1)S(1)}, bf16[8,64,640]{2,1,0:T(8,128)(2,1)S(1)}, u32[]{:S(2)}, u32[]{:S(2)}) collective-permute-start(bf16[8,64,640]{2,1,0:T(8,128)(2,1)S(1)} %get-tuple-element.104), channel_id=1, source_target_pairs={{0,1},{1,0},{2,3},{3,2},{4,5},{5,4},{6,7},{7,6},{8,9},{9,8},{10,11... | collective-permute-start | bytes 1966088 | tf_op jit(solution)/shard_map/ppermute | solution.py:517
  96.5 15.7 %collective-permute-start.24 = (bf16[8,64,640]{2,1,0:T(8,128)(2,1)S(1)}, bf16[8,64,640]{2,1,0:T(8,128)(2,1)S(1)}, u32[]{:S(2)}, u32[]{:S(2)}) collective-permute-start(bf16[8,64,640]{2,1,0:T(8,128)(2,1)S(1)} %get-tuple-element.105), channel_id=1, source_target_pairs={{0,4},{4,0},{8,12},{12,8},{1,5},{5,1},{9,13},{13,9},{2,6},{6,2},{1... | collective-permute-start | bytes 1966088 | tf_op jit(solution)/shard_map/ppermute | solution.py:517
  113.1 7.8 %collective-permute-start.25 = (bf16[4,64,640]{2,1,0:T(8,128)(2,1)S(1)}, bf16[4,64,640]{2,1,0:T(8,128)(2,1)S(1)}, u32[]{:S(2)}, u32[]{:S(2)}) collective-permute-start(bf16[4,64,640]{2,1,0:T(8,128)(2,1)S(1)} %get-tuple-element.142), channel_id=1, source_target_pairs={{0,1},{1,0},{2,3},{3,2},{4,5},{5,4},{6,7},{7,6},{8,9},{9,8},{10,11... | collective-permute-start | bytes 983048 | tf_op jit(solution)/shard_map/ppermute | solution.py:517
  114.0 7.0 %collective-permute-start.26 = (bf16[4,64,640]{2,1,0:T(8,128)(2,1)S(1)}, bf16[4,64,640]{2,1,0:T(8,128)(2,1)S(1)}, u32[]{:S(2)}, u32[]{:S(2)}) collective-permute-start(bf16[4,64,640]{2,1,0:T(8,128)(2,1)S(1)} %get-tuple-element.140), channel_id=1, source_target_pairs={{0,4},{4,0},{8,12},{12,8},{1,5},{5,1},{9,13},{13,9},{2,6},{6,2},{1... | collective-permute-start | bytes 983048 | tf_op jit(solution)/shard_map/ppermute | solution.py:517
  114.4 8.3 %collective-permute-start.27 = (bf16[4,64,640]{2,1,0:T(8,128)(2,1)S(1)}, bf16[4,64,640]{2,1,0:T(8,128)(2,1)S(1)}, u32[]{:S(2)}, u32[]{:S(2)}) collective-permute-start(bf16[4,64,640]{2,1,0:T(8,128)(2,1)S(1)} %get-tuple-element.138), channel_id=1, source_target_pairs={{0,3},{1,2},{2,1},{3,0},{4,7},{5,6},{6,5},{7,4},{8,11},{9,10},{10,... | collective-permute-start | bytes 983048 | tf_op jit(solution)/shard_map/ppermute | solution.py:517
  116.3 8.0 %collective-permute-start.28 = (bf16[4,64,640]{2,1,0:T(8,128)(2,1)S(1)}, bf16[4,64,640]{2,1,0:T(8,128)(2,1)S(1)}, u32[]{:S(2)}, u32[]{:S(2)}) collective-permute-start(bf16[4,64,640]{2,1,0:T(8,128)(2,1)S(1)} %get-tuple-element.136), channel_id=1, source_target_pairs={{0,12},{4,8},{8,4},{12,0},{1,13},{5,9},{9,5},{13,1},{2,14},{6,10},... | collective-permute-start | bytes 983048 | tf_op jit(solution)/shard_map/ppermute | solution.py:517
  128.1 7.8 %collective-permute-start.34 = (bf16[64,1280]{1,0:T(8,128)(2,1)S(1)}, bf16[64,1280]{1,0:T(8,128)(2,1)S(1)}, u32[]{:S(2)}, u32[]{:S(2)}) collective-permute-start(bf16[64,1280]{1,0:T(8,128)(2,1)S(1)} %get-tuple-element.131), channel_id=1, source_target_pairs={{0,3},{1,2},{2,1},{3,0},{4,7},{5,6},{6,5},{7,4},{8,11},{9,10},{10,... | collective-permute-start | bytes 491528 | tf_op jit(solution)/shard_map/ppermute | solution.py:517
  129.2 6.7 %collective-permute-start.33 = (bf16[64,1280]{1,0:T(8,128)(2,1)S(1)}, bf16[64,1280]{1,0:T(8,128)(2,1)S(1)}, u32[]{:S(2)}, u32[]{:S(2)}) collective-permute-start(bf16[64,1280]{1,0:T(8,128)(2,1)S(1)} %get-tuple-element.132), channel_id=1, source_target_pairs={{0,2},{1,3},{2,0},{3,1},{4,6},{5,7},{6,4},{7,5},{8,10},{9,11},{10,... | collective-permute-start | bytes 491528 | tf_op jit(solution)/shard_map/ppermute | solution.py:517
  168.2 20.6 %collective-permute-start.35 = (bf16[64,2560]{1,0:T(8,128)(2,1)S(1)}, bf16[64,2560]{1,0:T(8,128)(2,1)S(1)}, u32[]{:S(2)}, u32[]{:S(2)}) collective-permute-start(bf16[64,2560]{1,0:T(8,128)(2,1)S(1)} %bitcast.50), channel_id=1, source_target_pairs={{0,16},{16,0},{1,17},{17,1},{2,18},{18,2},{3,19},{19,3},{4,20},{20... | collective-permute-start | bytes 983048 | tf_op jit(solution)/shard_map/ppermute | solution.py:513
  (25 other events, 440.9 us)

commit v4 on v3

--- a/solution.py
+++ b/solution.py
@@ -22,12 +22,7 @@
 OWN = ("x", "y")
 SWAP = ((0, 1), (1, 0))
 
-ROUNDS = (
-    (("x", 1), ("x", 3), ("y", 1), ("y", 3)),
-    (("y", 1), ("y", 3), ("x", 1), ("x", 3)),
-    (("x", 3), ("x", 1), ("y", 3), ("y", 1)),
-    (("y", 3), ("y", 1), ("x", 3), ("x", 1)),
-)
+ROUNDS = (((0, 1), (0, 3), (1, 1), (1, 3)), ((0, 3), (0, 1), (1, 3), (1, 1)))
 
 
 def rms_scale(values):
@@ -35,7 +30,7 @@
 
 
 def sigmoid(values):
-    return 1.0 / (1.0 + jnp.exp(-values))
+    return 0.5 + 0.5 * jnp.tanh(0.5 * values)
 
 
 def allowed_mask(length):
@@ -66,65 +61,53 @@
     return act, sig + act * (1.0 - sig)
 
 
-def link_bits(place, turn):
-    high, odd = place >> 1, (place >> 1) ^ (place & 1)
-    return odd + 2 * high if turn < 2 else high + 2 * odd
-
-
-def gather_slot(mask, turn):
-    one, two = (mask >> 2, mask & 3) if turn % 2 == 0 else (mask & 3, mask >> 2)
-    return link_bits(one, turn) + 4 * link_bits(two, turn)
-
-
-def scatter_slot(mask, turn):
-    one, two = (mask >> 2, mask & 3) if turn % 2 == 0 else (mask & 3, mask >> 2)
-    return one + 4 * link_bits(two, turn)
-
-
-def place_rows(turn, own, near, far, store):
-    count, rows, _ = near.shape
-    for mask in range(2 * count):
-        slot = gather_slot(mask, turn)
-        block = near[slot] if slot < count else far[slot - count]
-        store(pl.ds(pl.multiple_of((own ^ mask) * rows, rows), rows), block)
+def scatter_slot(mask, part, core):
+    x, y = mask >> 2, mask & 3
+    one, two = jnp.where(core == 0, x, y), jnp.where(core == 0, y, x)
+    high, odd = two >> 1, (two >> 1) ^ (two & 1)
+    return one + 4 * (odd + 2 * high if part == 0 else high + 2 * odd)
+
+
+def gather_mask(slot, part, core):
+    links = (1, 3) if part == 0 else (3, 1)
+    one, two = (
+        (links[0] if bits & 1 else 0) ^ (links[1] if bits & 2 else 0)
+        for bits in (slot & 3, slot >> 2)
+    )
+    return jnp.where(core == 0, 4 * one + two, 4 * two + one)
+
+
+def place_rows(part, place, held, store):
+    count, rows, _ = held[0].shape
+    for slot in range(4 * count):
+        block = held[slot // count][slot % count]
+        owner = place[0] ^ gather_mask(slot, part, place[1])
+        store(pl.ds(pl.multiple_of(owner * rows, rows), rows), block)
 
 
 def forward_kernel(
     place,
     lengths,
     normed,
-    q_near,
-    q_far,
-    k_near,
-    k_far,
-    v_near,
-    v_far,
-    g_near,
-    g_far,
-    projected,
-    scores,
-    mixed,
-    outer,
-    weight,
+    *refs,
 ):
+    projected, scores, mixed, outer, weight = refs[8:]
     count, rows, width = mixed.shape
-    share = outer.shape[1] // 4
+    share = outer.shape[1] // 2
 
     @pl.when(pl.program_id(0) == 0)
     def _():
-        for turn, near, far, column in (
-            (0, q_near, q_far, 0),
-            (1, k_near, k_far, 2 * width),
-            (2, v_near, v_far, width),
-            (3, g_near, g_far, None),
-        ):
-
-            def store(at, block, turn=turn, column=column):
-                if column is not None:
-                    weight[at, column : column + width] = block[:, :width]
-                outer[at, turn * share : (turn + 1) * share] = block[:, block.shape[1] - share :]
-
-            place_rows(turn, place[0], near, far, store)
+        def store_0(at, block):
+            weight[at, :width] = block[:, :width]
+            weight[at, 2 * width :] = block[:, width : 2 * width]
+            outer[at, :share] = block[:, 2 * width :]
+
+        def store_1(at, block):
+            weight[at, width : 2 * width] = block[:, :width]
+            outer[at, share:] = block[:, 2 * width :]
+
+        place_rows(0, place, refs[:4], store_0)
+        place_rows(1, place, refs[4:8], store_1)
 
     projected[...] = dot_nn(normed[...].reshape(count * rows, -1), weight[...]).reshape(
         projected.shape
@@ -147,8 +130,10 @@
 def gating_kernel(
     place,
     normed,
-    near,
-    far,
+    held_0,
+    held_1,
+    held_2,
+    held_3,
     masked,
     keep,
     recv,
@@ -165,7 +150,7 @@
         def store(at, block):
             weight[at, :] = block
 
-        place_rows(3, place[0], near, far, store)
+        place_rows(1, place, (held_0, held_1, held_2, held_3), store)
 
     proj = dot_nn(normed[...].reshape(count * rows, -1), weight[...])
     gating_out[...] = proj.reshape(gating_out.shape)
@@ -253,36 +238,42 @@
 
 
 def terms_kernel(place, normed_t, grads, keep, recv, *refs):
-    outs, held, sems = refs[:8], refs[8:12], refs[12]
+    outs, held, sems = refs[:8], refs[8:10], refs[10]
     step = pl.program_id(0)
     slots, rows, _ = held[0].shape
     width = grads.shape[1]
     half = keep.shape[0] // rows
+    core = place[1]
 
     def copies(turn):
+        part, columns = turn // 2, (slice(width, None) if turn % 2 else slice(0, width))
+        span = pl.ds(columns.start, (held[0].shape[2] if turn % 2 else width) - columns.start)
         return [
             pltpu.make_async_copy(
-                held[turn].at[pl.ds(side * (slots // 2), slots // 2)],
-                outs[2 * turn + side],
-                sems.at[2 * turn + side],
+                held[part].at[pl.ds(group * (slots // 4), slots // 4), :, span],
+                outs[4 * part + group].at[:, :, span],
+                sems.at[4 * turn + group],
             )
-            for side in range(2)
+            for group in range(4)
         ]
 
     for turn in range(4):
 
         @pl.when(step == turn)
         def _(turn=turn):
+            part, start = turn // 2, (turn % 2) * width
             term = dot_nn(normed_t[...], grads[...]).astype(jnp.bfloat16)
             for block in range(slots):
-                slot = scatter_slot(block ^ place[0], turn)
-                held[turn][slot, :, :width] = term[block * rows : (block + 1) * rows]
-            share = held[turn].shape[2] - width
-            cut = slice(turn * share, (turn + 1) * share)
-            for side, outer in ((place[1], keep), (1 - place[1], recv)):
-                for block in range(half):
-                    slot = scatter_slot((side * half + block) ^ place[0], turn)
-                    held[turn][slot, :, width:] = outer[block * rows : (block + 1) * rows, cut]
+                slot = scatter_slot(block ^ place[0], part, core)
+                held[part][slot, :, start : start + width] = term[block * rows : (block + 1) * rows]
+            if turn % 2:
+                share = held[part].shape[2] - 2 * width
+                cut = slice(part * share, (part + 1) * share)
+                for side, outer in ((core, keep), (1 - core, recv)):
+                    for block in range(half):
+                        slot = scatter_slot((side * half + block) ^ place[0], part, core)
+                        value = outer[block * rows : (block + 1) * rows, cut]
+                        held[part][slot, :, 2 * width :] = value
             for copy in copies(turn):
                 copy.start()
 
@@ -297,9 +288,9 @@
     return pl.BlockSpec((some, *dims), lambda i, *_: (i,) + (0,) * len(dims))
 
 
-def whole(*dims):
+def whole(*dims, buffers=1):
     return pl.BlockSpec(
-        dims, lambda i, *_: (0,) * len(dims), pipeline_mode=pl.Buffered(buffer_count=1)
+        dims, lambda i, *_: (0,) * len(dims), pipeline_mode=pl.Buffered(buffer_count=buffers)
     )
 
 
@@ -329,26 +320,24 @@
     )(*prefetch, *inputs)
 
 
-def attention_forward(place, lengths, normed, queries, keys_in, values, gating):
+def attention_forward(place, lengths, normed, held):
     count, rows, depth = normed.shape
     width = depth // 2
     heads = width // HEAD_WIDTH
-    held = (*queries, *keys_in, *values)
     return call(
         forward_kernel,
         "attention_forward",
         (count // 2,),
         (place, lengths),
         [rows_of(rows, depth, some=2)]
-        + [whole(*part.shape) for part in held]
-        + [columns_of(part, width // 4, 4) for part in gating],
+        + [whole(*part.shape) for part in held],
         [
             (rows_of(rows, 3 * width, some=2), (count, rows, 3 * width), jnp.float32),
             (rows_of(heads, rows, rows, some=2), (count, heads, rows, rows), jnp.float32),
             (rows_of(rows, width, some=2), (count, rows, width), jnp.float32),
             (whole(depth, width), (depth, width), jnp.bfloat16),
         ],
-        (normed, *held, *gating),
+        (normed, *held),
         [pltpu.VMEM((depth, 3 * width), jnp.bfloat16)],
         room=28,
     )
@@ -364,7 +353,7 @@
         (place,),
         [
             rows_of(rows, depth, some=2),
-            *(columns_of(part, width, 0) for part in gating),
+            *(columns_of(part, width, 1) for part in gating),
             rows_of(rows, depth, some=2),
             whole(*keep.shape),
             whole(*recv.shape),
@@ -430,8 +419,7 @@
 def terms(place, owned, normed_t, grads, keep, recv):
     depth, rows = normed_t.shape
     width = grads.shape[1] // 4
-    columns = width + keep.shape[1] // 4
-    shapes = [(depth // owned // 2, owned, columns)] * 8
+    shapes = [(depth // owned // 4, owned, 2 * width + keep.shape[1] // 2)] * 8
     anywhere = pl.BlockSpec(memory_space=pl.ANY)
     outs = call(
         terms_kernel,
@@ -439,17 +427,17 @@
         (4,),
         (place,),
         [
-            whole(depth, rows),
+            whole(depth, rows, buffers=2),
             pl.BlockSpec((rows, width), lambda i, *_: (0, i)),
-            whole(*keep.shape),
-            whole(*recv.shape),
+            whole(*keep.shape, buffers=2),
+            whole(*recv.shape, buffers=2),
         ],
         [(anywhere, shape, jnp.bfloat16) for shape in shapes],
         (normed_t, grads, keep, recv),
-        [pltpu.VMEM((2 * half, *rest), jnp.bfloat16) for half, *rest in shapes[::2]]
-        + [pltpu.SemaphoreType.DMA((8,))],
-    )
-    return [outs[2 * turn : 2 * turn + 2] for turn in range(4)]
+        [pltpu.VMEM((4 * count, *rest), jnp.bfloat16) for count, *rest in shapes[::4]]
+        + [pltpu.SemaphoreType.DMA((16,))],
+    )
+    return [outs[:4], outs[4:]]
 
 
 def sum_squares(values):
@@ -514,47 +502,46 @@
 
 
 def over_link(values, axis, mask):
-    return lax.ppermute(values, axis, [(i, i ^ mask) for i in range(4)])
-
-
-def direct_round(blocks_of, groups):
-    got = [[None] * 4, [None] * 4]
-    for mask in (1, 3, 2):
-        for group, axis in enumerate(("x", "y")):
-            got[group][mask] = over_link(blocks_of(groups[group], mask), axis, mask)
-    return got
+    pairs = []
+    for core in range(2):
+        shift = mask << 2 if axis == core else mask
+        pairs += [(16 * core + own, 16 * core + (own ^ shift)) for own in range(16)]
+    return lax.ppermute(values, ("c", *OWN), pairs)
 
 
 def gather_parts(parts, prepare, join):
     held = [part[None] for part in parts]
-    for step in range(3):
+    for step in range(2):
         got = [over_link(part, *ROUNDS[turn][step]) for turn, part in enumerate(held)]
         held = [jnp.concatenate(pair, axis=0) for pair in zip(held, got)]
-        if step == 1:
+        if step == 0:
+            held = lax.optimization_barrier(held)
+            held[0], beside = prepare(held[0])
+        else:
             held, beside = lax.optimization_barrier((held, beside))
-        else:
-            held = lax.optimization_barrier(held)
-        if step == 0:
-            held[0], beside = prepare(held[0])
-    far = [over_link(part, *ROUNDS[turn][3]) for turn, part in enumerate(held)]
-    far, beside = lax.optimization_barrier((far, join(beside)))
-    return list(zip(held, far)), beside
+    first = [over_link(part, *ROUNDS[turn][2]) for turn, part in enumerate(held)]
+    second = [over_link(part, *ROUNDS[turn][3]) for turn, part in enumerate(held)]
+    first, second = lax.optimization_barrier((first, second))
+    both = [over_link(part, *ROUNDS[turn][3]) for turn, part in enumerate(first)]
+    both, beside = lax.optimization_barrier((both, join(beside)))
+    return list(zip(held, first, second, both)), beside
 
 
 def add_blocks(*blocks):
     return sum(block.astype(jnp.float32) for block in blocks).astype(jnp.bfloat16)
 
 
-def scatter_parts(pairs):
-    for step in (1, 0):
-        got = [over_link(far, *ROUNDS[turn][2 + step]) for turn, (_, far) in enumerate(pairs)]
-        mine, got = lax.optimization_barrier(([near for near, _ in pairs], got))
-        held = [add_blocks(*pair) for pair in zip(mine, got)]
-        if step:
-            pairs = [jnp.split(part, 2, axis=0) for part in held]
-    groups = [jnp.concatenate([held[0], held[2]], axis=2), jnp.concatenate([held[1], held[3]], axis=2)]
-    got = direct_round(lambda group, mask: group[mask], groups)
-    return [add_blocks(group[0], *blocks[1:]) for group, blocks in zip(groups, got)]
+def scatter_parts(parts):
+    mine, first, second, both = zip(*parts)
+    both = [over_link(part, *ROUNDS[turn][3]) for turn, part in enumerate(both)]
+    second = [over_link(part, *ROUNDS[turn][3]) for turn, part in enumerate(second)]
+    first, both, second = lax.optimization_barrier((first, both, second))
+    first = [add_blocks(*pair) for pair in zip(first, both)]
+    first = [over_link(part, *ROUNDS[turn][2]) for turn, part in enumerate(first)]
+    mine, first, second = lax.optimization_barrier((mine, first, second))
+    held = [add_blocks(*blocks) for blocks in zip(mine, first, second)]
+    held = jnp.concatenate(held, axis=2)
+    return add_blocks(held[0], *(over_link(held[mask], 0, mask) for mask in (1, 3, 2)))
 
 
 def exchange(blocks, axes):
@@ -608,37 +595,35 @@
         all_lengths = jnp.concatenate([lengths, lengths_other], axis=0)
         return normed, masked, all_lengths, normed.reshape(-1, model_width).T
 
-    (queries, keys_in, values, gating), (normed, masked, all_lengths, normed_t) = gather_parts(
+    parts, (normed, masked, all_lengths, normed_t) = gather_parts(
         [
-            jnp.concatenate([mine[part], mine_out[:, at * share : (at + 1) * share]], axis=1)
-            for at, part in enumerate((2, 3, 1, 0))
+            jnp.concatenate([mine[2], mine[3], mine_out[:, : half // 2]], axis=1),
+            jnp.concatenate([mine[1], mine[0], mine_out[:, half // 2 :]], axis=1),
         ],
         prepare,
         join,
     )
 
     projected, scores, mixed, outer_cols = attention_forward(
-        place, all_lengths, normed, queries, keys_in, values, gating
+        place, all_lengths, normed, (*parts[0], *parts[1])
     )
     outer_cols = outer_cols.reshape(2, half, half)
     keep = lax.dynamic_index_in_dim(outer_cols, core, axis=0, keepdims=False)
     recv = swap_cores(lax.dynamic_index_in_dim(outer_cols, 1 - core, axis=0, keepdims=False))
-    gating, grad_gated, stats = gating_forward(place, normed, gating, masked, keep, recv, mixed)
+    gating, grad_gated, stats = gating_forward(place, normed, parts[1], masked, keep, recv, mixed)
     stats_other = swap_cores(stats)
     outer = outer_term(place, gating, mixed, stats, stats_other, masked)
     outer_recv = swap_cores(outer[1])
     grads = attention_back(
         all_lengths, gating, projected, scores, mixed, grad_gated, stats, stats_other
     )
-    term_g, term_v, term_q, term_k = terms(
-        place, owned, normed_t, grads.reshape(-1, 4 * half), outer[0], outer_recv
-    )
-    part_gq, part_vk = scatter_parts([term_g, term_v, term_q, term_k])
-    wide = half + share
-    sides = (part_gq, part_vk)
+    part = scatter_parts(
+        terms(place, owned, normed_t, grads.reshape(-1, 4 * half), outer[0], outer_recv)
+    )
+    wide = part.shape[1] // 2
     part = jnp.concatenate(
-        [side[:, at : at + half] for at in (0, wide) for side in sides]
-        + [side[:, at : at + share] for at in (half, wide + half) for side in sides],
+        [part[:, : 2 * half], part[:, wide : wide + 2 * half]]
+        + [part[:, at + 2 * half : at + wide] for at in (0, wide)],
         axis=1,
     )
 

time: 193 us -> 188 us (0.974)
  waiting for transfers between devices: 46.1 us -> 62.3 us
  starting transfers between devices: 49 us -> 33.6 us
  other arithmetic: 12 us -> 6.85 us
  Pallas kernels: 33.7 us -> 31.7 us
    ppermute x30 -> x19, waiting for transfers between devices: 42.9 us -> 59.2 us  [over_link(): return lax.ppermute(values, ('c', *OWN), pairs)]
    ppermute x30 -> x19, starting transfers between devices: 31.8 us -> 19 us  [over_link(): return lax.ppermute(values, ('c', *OWN), pairs)]
    concatenate x12 -> x4, other arithmetic: 5.14 us -> 0.18 us  [gather_parts(): held = [jnp.concatenate(pair, axis=0) for pair in zip(held, got)]]
    ppermute x6, starting transfers between devices: 17.1 us -> 14.7 us  [swap_cores(): return lax.ppermute(values, 'c', SWAP)]
    slice x1, local copies, waits for them, and re-layouts: 1.91 us -> 3.93 us  [join(): side[at:at + slots]]
    pallas_call x6, Pallas kernels: 33.7 us -> 31.7 us  [call(): pl.pallas_call(kernel, grid_spec=pltpu.PrefetchScalarGridSpec(num_scalar_...]
  transfers between devices with their start and end apart: 36 -> 25, of which waited for: 18 -> 17; matrix products, arithmetic and copies ran while one was open for 7% -> 7% of each run, Pallas kernels for 3% -> 3%
where the time goes in v4:
time: 188 us
  waiting for transfers between devices  62.3 us (33%)
  blocking collectives  43.1 us (23%)
  starting transfers between devices  33.6 us (18%)
  Pallas kernels  31.7 us (17%)
  local copies, waits for them, and re-layouts  9.2 us (5%)
  other arithmetic  6.85 us (4%)
    ppermute x19, waiting for transfers between devices, over_link(): return lax.ppermute(values, ('c', *OWN), pairs)  59.2 us
    all_to_all x3, blocking collectives, exchange(): return lax.all_to_all(blocks, axes, 0, 0, tiled=True)  43.1 us
    pallas_call x6, Pallas kernels, call(): pl.pallas_call(kernel, grid_spec=pltpu.PrefetchScalarGridSpec(num_scalar_...  31.7 us
    ppermute x19, starting transfers between devices, over_link(): return lax.ppermute(values, ('c', *OWN), pairs)  19 us
    ppermute x6, starting transfers between devices, swap_cores(): return lax.ppermute(values, 'c', SWAP)  14.7 us
    slice x1, local copies, waits for them, and re-layouts, join(): side[at:at + slots]  3.93 us
  transfers between devices with their start and end apart: 25, of which 17 were waited for; matrix products, arithmetic and copies ran while one was open for 7% of the time, Pallas kernels for 3%

profile of v4, /device:TPU:1, one launch (start us, length us, event | category | flops | bytes accessed | tf_op | source)
XLA Modules:
  0.0 188.1 jit_solution(15929055719264243910)
XLA Ops:
  0.7 3.3 %collective-permute-start.2 = (s32[2]{0:T(128)}, s32[2]{0:T(128)S(1)}, u32[]{:S(2)}, u32[]{:S(2)}) collective-permute-start(s32[2]{0:T(128)} %param.12), channel_id=1, source_target_pairs={{0,16},{16,0},{1,17},{17,1},{2,18},{18,2},{3,19},{19,3},{4,20},{20... | collective-permute-start | bytes 32 | tf_op jit(solution)/shard_map/ppermute | solution.py:501
  13.7 2.5 %collective-permute-start.3 = (bf16[2,64,1280]{2,1,0:T(8,128)(2,1)S(1)}, bf16[2,64,1280]{2,1,0:T(8,128)(2,1)S(1)}, u32[]{:S(2)}, u32[]{:S(2)}) collective-permute-start(bf16[2,64,1280]{2,1,0:T(8,128)(2,1)S(1)} %pad_maximum_fusion.6), channel_id=1, source_target_pairs={{0,12},{1,13},{2,14},{3,15},{4,8},{5,9},{6,10},{7,11},{8,4},{9,5},... | collective-permute-start | bytes 983048 | tf_op jit(solution)/shard_map/ppermute | solution.py:509
  16.2 5.0 %collective-permute-done.3 = bf16[2,64,1280]{2,1,0:T(8,128)(2,1)S(1)} collective-permute-done((bf16[2,64,1280]{2,1,0:T(8,128)(2,1)S(1)}, bf16[2,64,1280]{2,1,0:T(8,128)(2,1)S(1)}, u32[]{:S(2)}, u32[]{:S(2)}) %collective-permute-start.3) | collective-permute-done | bytes 327712 | tf_op jit(solution)/shard_map/ppermute | solution.py:509
  26.7 6.7 %collective-permute-done.8.refs_2_ = bf16[4,64,1280]{2,1,0:T(8,128)(2,1)S(1)} collective-permute-done((bf16[4,64,1280]{2,1,0:T(8,128)(2,1)S(1)}, bf16[4,64,1280]{2,1,0:T(8,128)(2,1)S(1)}, u32[]{:S(2)}, u32[]{:S(2)}) %collective-permute-start.8) | collective-permute-done | bytes 655392 | tf_op jit(solution)/shard_map/ppermute | solution.py:509
  33.9 7.0 %collective-permute-done.9.refs_6_.held_2 = bf16[4,64,1280]{2,1,0:T(8,128)(2,1)S(1)} collective-permute-done((bf16[4,64,1280]{2,1,0:T(8,128)(2,1)S(1)}, bf16[4,64,1280]{2,1,0:T(8,128)(2,1)S(1)}, u32[]{:S(2)}, u32[]{:S(2)}) %collective-permute-start.9) | collective-permute-done | bytes 655392 | tf_op jit(solution)/shard_map/ppermute | solution.py:509
  42.1 3.9 %fusion.13 = (bf16[2,256,1024]{2,1,0:T(8,128)(2,1)}, bf16[2,256,1024]{2,1,0:T(8,128)(2,1)S(1)}, bf16[2,256,1024]{2,1,0:T(8,128)(2,1)S(1)}, bf16[2,256,1024]{2,1,0:T(8,128)(2,1)}) fusion(bf16[4,256,1024]{2,1,0:T(8,128)(2,1)} %copy-done.11, bf16[4,256,1024]{2,1,0:T(8,128)(2,1)} %copy-done.13), kind=kLoop, calls=%fused_computation.53 | loop fusion | bytes 8388608 | tf_op jit(solution)/shard_map/slice | solution.py:592
  46.3 2.6 %copy.17 = bf16[1024,1024]{0,1:T(8,128)(2,1)} copy(bf16[1024,1024]{1,0:T(8,128)(2,1)S(1)} %bitcast.33) | data formatting | bytes 4194304 | tf_op jit(solution)/shard_map/reshape | solution.py:596
  52.2 7.5 %attention_forward.1 = (f32[4,256,1536]{2,1,0:T(8,128)S(1)}, f32[4,2,256,256]{3,2,1,0:T(8,128)S(1)}, f32[4,256,512]{2,1,0:T(8,128)S(1)}, bf16[1024,512]{1,0:T(8,128)(2,1)S(1)}) custom-call(s32[2]{0:T(128)S(1)} %pad_add_fusion.place, s32[4]{0:T(128)S(1)} %pad_add_fusion.1.lengths, bf16[4,256,1024]{2,1,0:T(8,128)(2,1)S(1)} %pad_maximum_fusion.1.normed, ...), custom_call_target="tpu_custom_call" | custom-call | flops 1 | bytes 1 | tf_op jit(solution)/shard_map/attention_forward/pallas_call | solution.py:307
  59.8 3.8 %collective-permute-start.12 = (bf16[512,512]{1,0:T(8,128)(2,1)S(1)}, bf16[512,512]{1,0:T(8,128)(2,1)S(1)}, u32[]{:S(2)}, u32[]{:S(2)}) collective-permute-start(bf16[512,512]{1,0:T(8,128)(2,1)S(1)} %get-tuple-element.111), channel_id=1, source_target_pairs={{0,16},{16,0},{1,17},{17,1},{2,18},{18,2},{3,19},{19,3},{4,20},{20... | collective-permute-start | bytes 1572872 | tf_op jit(solution)/shard_map/ppermute | solution.py:501
  65.1 4.6 %gating_forward.1 = (f32[4,256,512]{2,1,0:T(8,128)S(1)}, bf16[4,256,512]{2,1,0:T(8,128)(2,1)S(1)}, f32[4,256,128]{2,1,0:T(8,128)S(1)}) custom-call(s32[2]{0:T(128)S(1)} %pad_add_fusion.place, bf16[4,256,1024]{2,1,0:T(8,128)(2,1)S(1)} %pad_maximum_fusion.1.normed, bf16[4,64,1280]{2,1,0:T(8,128)(2,1)S(1)} %pad_maximum_fusion.4.refs_4_.held_0, ...), custom_call_target="tpu_custom_call" | custom-call | flops 1 | bytes 1 | tf_op jit(solution)/shard_map/gating_forward/pallas_call | solution.py:307
  71.7 3.3 %outer_term.1 = bf16[2,512,512]{2,1,0:T(8,128)(2,1)S(1)} custom-call(s32[2]{0:T(128)S(1)} %pad_add_fusion.place, f32[4,256,512]{2,1,0:T(8,128)S(1)} %get-tuple-element.77.gating_in.projected, f32[4,256,512]{2,1,0:T(8,128)S(1)} %get-tuple-element.76.mixed, f32[4,256,128]{2,1,0:T(8,128)S(1)} %get-tuple-element.81.stats, ...), custom_call_target="tpu_custom_call" | custom-call | flops 1 | bytes 1 | tf_op jit(solution)/shard_map/outer_term/pallas_call | solution.py:307
  75.6 5.9 %attention_back.1 = bf16[4,256,2048]{2,1,0:T(8,128)(2,1)S(1)} custom-call(s32[4]{0:T(128)S(1)} %pad_add_fusion.1.lengths, f32[4,256,512]{2,1,0:T(8,128)S(1)} %get-tuple-element.77.gating_in.projected, f32[4,256,1536]{2,1,0:T(8,128)S(1)} %get-tuple-element.78.projected, f32[4,2,256,256]{3,2,1,0:T(8,128)S(1)} %get-tuple-element.79.scores, ...), custom_call_target="tpu_custom_call" | custom-call | flops 1 | bytes 1 | tf_op jit(solution)/shard_map/attention_back/pallas_call | solution.py:307
  81.5 6.7 %terms.1 = (bf16[4,64,1280]{2,1,0:T(8,128)(2,1)S(1)}, bf16[4,64,1280]{2,1,0:T(8,128)(2,1)S(1)}, bf16[4,64,1280]{2,1,0:T(8,128)(2,1)S(1)}, bf16[4,64,1280]{2,1,0:...) custom-call(s32[2]{0:T(128)S(1)} %pad_add_fusion.place, ...), custom_call_target="tpu_custom_call" | custom-call | flops 1 | bytes 1 | tf_op jit(solution)/shard_map/terms/pallas_call | solution.py:307
  91.8 7.4 %collective-permute-done.15 = bf16[4,64,1280]{2,1,0:T(8,128)(2,1)S(1)} collective-permute-done((bf16[4,64,1280]{2,1,0:T(8,128)(2,1)S(1)}, bf16[4,64,1280]{2,1,0:T(8,128)(2,1)S(1)}, u32[]{:S(2)}, u32[]{:S(2)}) %collective-permute-start.15) | collective-permute-done | bytes 655392 | tf_op jit(solution)/shard_map/ppermute | solution.py:509
  99.2 7.0 %collective-permute-done.17 = bf16[4,64,1280]{2,1,0:T(8,128)(2,1)S(1)} collective-permute-done((bf16[4,64,1280]{2,1,0:T(8,128)(2,1)S(1)}, bf16[4,64,1280]{2,1,0:T(8,128)(2,1)S(1)}, u32[]{:S(2)}, u32[]{:S(2)}) %collective-permute-start.17) | collective-permute-done | bytes 655392 | tf_op jit(solution)/shard_map/ppermute | solution.py:509
  108.4 9.0 %collective-permute-done.20 = bf16[4,64,1280]{2,1,0:T(8,128)(2,1)S(1)} collective-permute-done((bf16[4,64,1280]{2,1,0:T(8,128)(2,1)S(1)}, bf16[4,64,1280]{2,1,0:T(8,128)(2,1)S(1)}, u32[]{:S(2)}, u32[]{:S(2)}) %collective-permute-start.20) | collective-permute-done | bytes 655392 | tf_op jit(solution)/shard_map/ppermute | solution.py:509
  118.8 2.8 %collective-permute-start.23 = (bf16[64,2560]{1,0:T(8,128)(2,1)S(1)}, bf16[64,2560]{1,0:T(8,128)(2,1)S(1)}, u32[]{:S(2)}, u32[]{:S(2)}) collective-permute-start(bf16[64,2560]{1,0:T(8,128)(2,1)S(1)} %get-tuple-element.107), channel_id=1, source_target_pairs={{0,8},{1,9},{2,10},{3,11},{4,12},{5,13},{6,14},{7,15},{8,0},{9,1},... | collective-permute-start | bytes 983048 | tf_op jit(solution)/shard_map/ppermute | solution.py:509
  125.0 4.9 %collective-permute-done.23 = bf16[64,2560]{1,0:T(8,128)(2,1)S(1)} collective-permute-done((bf16[64,2560]{1,0:T(8,128)(2,1)S(1)}, bf16[64,2560]{1,0:T(8,128)(2,1)S(1)}, u32[]{:S(2)}, u32[]{:S(2)}) %collective-permute-start.23) | collective-permute-done | bytes 327712 | tf_op jit(solution)/shard_map/ppermute | solution.py:509
  129.9 2.6 %collective-permute-done.22 = bf16[64,2560]{1,0:T(8,128)(2,1)S(1)} collective-permute-done((bf16[64,2560]{1,0:T(8,128)(2,1)S(1)}, bf16[64,2560]{1,0:T(8,128)(2,1)S(1)}, u32[]{:S(2)}, u32[]{:S(2)}) %collective-permute-start.22) | collective-permute-done | bytes 327712 | tf_op jit(solution)/shard_map/ppermute | solution.py:509
  132.9 18.4 %all_to_all.25 = bf16[8,8,2560]{2,1,0:T(8,128)(2,1)} all-to-all(bf16[8,8,2560]{2,1,0:T(8,128)(2,1)S(1)} %maximum_bitcast_fusion), channel_id=1, replica_groups=mesh['z'=8,'c'=2,'x'=4,'y'=4] {'z'}, dimensions={0} | all-to-all | bytes 655360 | tf_op jit(solution)/shard_map/all_to_all | solution.py:548
  152.4 12.5 %all_to_all.26 = bf16[8,8,2560]{2,1,0:T(8,128)(2,1)S(1)} all-to-all(bf16[8,8,2560]{2,1,0:T(8,128)(2,1)S(1)} %broadcast_in_dim.35), channel_id=1, replica_groups=mesh['z'=8,'c'=2,'x'=4,'y'=4] {'z'}, dimensions={0} | all-to-all | bytes 655360 | tf_op jit(solution)/shard_map/all_to_all | solution.py:548
  164.9 5.6 %collective-permute-start.24 = (bf16[64,2560]{1,0:T(8,128)(2,1)S(1)}, bf16[64,2560]{1,0:T(8,128)(2,1)S(1)}, u32[]{:S(2)}, u32[]{:S(2)}) collective-permute-start(bf16[64,2560]{1,0:T(8,128)(2,1)S(1)} %bitcast.36), channel_id=1, source_target_pairs={{0,16},{16,0},{1,17},{17,1},{2,18},{18,2},{3,19},{19,3},{4,20},{20... | collective-permute-start | bytes 983048 | tf_op jit(solution)/shard_map/ppermute | solution.py:501
  172.0 12.2 %all_to_all.27 = f32[32,8,128]{2,1,0:T(8,128)S(1)} all-to-all(f32[32,8,128]{2,1,0:T(8,128)S(1)} %broadcast_in_dim.36), channel_id=1, replica_groups=mesh['z'=8,'c'=2,'x'=4,'y'=4] {'c','x','y'}, dimensions={0} | all-to-all | bytes 262144 | tf_op jit(solution)/shard_map/all_to_all | solution.py:548
  184.2 3.7 %update_rows.1 = (f32[64,4096]{1,0:T(8,128)}, f32[64,4096]{1,0:T(8,128)}, f32[64,4096]{1,0:T(8,128)}, f32[64,1024]{1,0:T(8,128)}, f32[64,1024]{1,0:T(8,128)}, /*index=5*/f32[64,1024]{1,0:T(8,128)}) custom-call(s32[2]{0:T(128)S(1)} %pad_add_fusion.place, f32[256,128]{1,0:T(8,128)S(1)} %bitcast.39, bf16[64,2560]{1,0:T(8,128)(2,1)S(1)} %bitcast.37, ...), custom_call_target="tpu_custom_call" | custom-call | flops 1 | bytes 1 | tf_op jit(solution)/shard_map/update_rows/pallas_call | solution.py:307
  (104 shorter events, 37.8 us)
Async XLA Ops:
  0.7 11.0 %collective-permute-start.2 = (s32[2]{0:T(128)}, s32[2]{0:T(128)S(1)}, u32[]{:S(2)}, u32[]{:S(2)}) collective-permute-start(s32[2]{0:T(128)} %param.12), channel_id=1, source_target_pairs={{0,16},{16,0},{1,17},{17,1},{2,18},{18,2},{3,19},{19,3},{4,20},{20... | collective-permute-start | bytes 32 | tf_op jit(solution)/shard_map/ppermute | solution.py:501
  5.7 4.6 %collective-permute-start = (bf16[1,64,1280]{2,1,0:T(8,128)(2,1)S(1)}, bf16[1,64,1280]{2,1,0:T(8,128)(2,1)S(1)}, u32[]{:S(2)}, u32[]{:S(2)}) collective-permute-start(bf16[1,64,1280]{2,1,0:T(8,128)(2,1)S(1)} %maximum_bitcast_fusion.1), channel_id=1, source_target_pairs={{0,4},{1,5},{2,6},{3,7},{4,0},{5,1},{6,2},{7,3},{8,12},{9,13},{10,... | collective-permute-start | bytes 491528 | tf_op jit(solution)/shard_map/ppermute | solution.py:509
  5.9 5.8 %collective-permute-start.1 = (bf16[1,64,1280]{2,1,0:T(8,128)(2,1)S(1)}, bf16[1,64,1280]{2,1,0:T(8,128)(2,1)S(1)}, u32[]{:S(2)}, u32[]{:S(2)}) collective-permute-start(bf16[1,64,1280]{2,1,0:T(8,128)(2,1)S(1)} %maximum_bitcast_fusion.2), channel_id=1, source_target_pairs={{0,12},{1,13},{2,14},{3,15},{4,8},{5,9},{6,10},{7,11},{8,4},{9,5},... | collective-permute-start | bytes 491528 | tf_op jit(solution)/shard_map/ppermute | solution.py:509
  12.6 9.7 %collective-permute-start.5 = (bf16[4,256,1024]{2,1,0:T(8,128)(2,1)S(1)}, bf16[4,256,1024]{2,1,0:T(8,128)(2,1)S(1)}, u32[]{:S(2)}, u32[]{:S(2)}) collective-permute-start(bf16[4,256,1024]{2,1,0:T(8,128)(2,1)S(1)} %pad_maximum_fusion), channel_id=1, source_target_pairs={{0,16},{16,0},{1,17},{17,1},{2,18},{18,2},{3,19},{19,3},{4,20},{20... | collective-permute-start | bytes 6291464 | tf_op jit(solution)/shard_map/ppermute | solution.py:501
  13.7 7.4 %collective-permute-start.3 = (bf16[2,64,1280]{2,1,0:T(8,128)(2,1)S(1)}, bf16[2,64,1280]{2,1,0:T(8,128)(2,1)S(1)}, u32[]{:S(2)}, u32[]{:S(2)}) collective-permute-start(bf16[2,64,1280]{2,1,0:T(8,128)(2,1)S(1)} %pad_maximum_fusion.6), channel_id=1, source_target_pairs={{0,12},{1,13},{2,14},{3,15},{4,8},{5,9},{6,10},{7,11},{8,4},{9,5},... | collective-permute-start | bytes 983048 | tf_op jit(solution)/shard_map/ppermute | solution.py:509
  16.2 6.1 %collective-permute-start.4 = (bf16[2,64,1280]{2,1,0:T(8,128)(2,1)S(1)}, bf16[2,64,1280]{2,1,0:T(8,128)(2,1)S(1)}, u32[]{:S(2)}, u32[]{:S(2)}) collective-permute-start(bf16[2,64,1280]{2,1,0:T(8,128)(2,1)S(1)} %pad_maximum_fusion.7), channel_id=1, source_target_pairs={{0,4},{1,5},{2,6},{3,7},{4,0},{5,1},{6,2},{7,3},{8,12},{9,13},{10,... | collective-permute-start | bytes 983048 | tf_op jit(solution)/shard_map/ppermute | solution.py:509
  22.4 11.0 %collective-permute-start.8 = (bf16[4,64,1280]{2,1,0:T(8,128)(2,1)S(1)}, bf16[4,64,1280]{2,1,0:T(8,128)(2,1)S(1)}, u32[]{:S(2)}, u32[]{:S(2)}) collective-permute-start(bf16[4,64,1280]{2,1,0:T(8,128)(2,1)S(1)} %pad_maximum_fusion.3.refs_0_), channel_id=1, source_target_pairs={{0,3},{1,2},{2,1},{3,0},{4,7},{5,6},{6,5},{7,4},{8,11},{9,10},{10,... | collective-permute-start | bytes 1966088 | tf_op jit(solution)/shard_map/ppermute | solution.py:509
  24.1 9.8 %collective-permute-start.6 = (bf16[4,64,1280]{2,1,0:T(8,128)(2,1)S(1)}, bf16[4,64,1280]{2,1,0:T(8,128)(2,1)}, u32[]{:S(2)}, u32[]{:S(2)}) collective-permute-start(bf16[4,64,1280]{2,1,0:T(8,128)(2,1)S(1)} %pad_maximum_fusion.3.refs_0_), channel_id=1, source_target_pairs={{0,1},{1,0},{2,3},{3,2},{4,5},{5,4},{6,7},{7,6},{8,9},{9,8},{10,11... | collective-permute-start | bytes 1966088 | tf_op jit(solution)/shard_map/ppermute | solution.py:509
  24.1 16.9 %collective-permute-start.9 = (bf16[4,64,1280]{2,1,0:T(8,128)(2,1)S(1)}, bf16[4,64,1280]{2,1,0:T(8,128)(2,1)S(1)}, u32[]{:S(2)}, u32[]{:S(2)}) collective-permute-start(bf16[4,64,1280]{2,1,0:T(8,128)(2,1)S(1)} %pad_maximum_fusion.4.refs_4_.held_0), channel_id=1, source_target_pairs={{0,1},{1,0},{2,3},{3,2},{4,5},{5,4},{6,7},{7,6},{8,9},{9,8},{10,11... | collective-permute-start | bytes 1966088 | tf_op jit(solution)/shard_map/ppermute | solution.py:509
  25.5 15.4 %collective-permute-start.7 = (bf16[4,64,1280]{2,1,0:T(8,128)(2,1)S(1)}, bf16[4,64,1280]{2,1,0:T(8,128)(2,1)}, u32[]{:S(2)}, u32[]{:S(2)}) collective-permute-start(bf16[4,64,1280]{2,1,0:T(8,128)(2,1)S(1)} %pad_maximum_fusion.4.refs_4_.held_0), channel_id=1, source_target_pairs={{0,3},{1,2},{2,1},{3,0},{4,7},{5,6},{6,5},{7,4},{8,11},{9,10},{10,... | collective-permute-start | bytes 1966088 | tf_op jit(solution)/shard_map/ppermute | solution.py:509
  40.9 11.3 %collective-permute-start.10 = (bf16[4,64,1280]{2,1,0:T(8,128)(2,1)}, bf16[4,64,1280]{2,1,0:T(8,128)(2,1)}, u32[]{:S(2)}, u32[]{:S(2)}) collective-permute-start(bf16[4,64,1280]{2,1,0:T(8,128)(2,1)} %collective-permute-done.6.refs_1_), channel_id=1, source_target_pairs={{0,3},{1,2},{2,1},{3,0},{4,7},{5,6},{6,5},{7,4},{8,11},{9,10},{10,... | collective-permute-start | bytes 1966088 | tf_op jit(solution)/shard_map/ppermute | solution.py:509
  42.1 10.1 %collective-permute-start.11 = (bf16[4,64,1280]{2,1,0:T(8,128)(2,1)}, bf16[4,64,1280]{2,1,0:T(8,128)(2,1)}, u32[]{:S(2)}, u32[]{:S(2)}) collective-permute-start(bf16[4,64,1280]{2,1,0:T(8,128)(2,1)} %collective-permute-done.7.refs_5_.held_1), channel_id=1, source_target_pairs={{0,1},{1,0},{2,3},{3,2},{4,5},{5,4},{6,7},{7,6},{8,9},{9,8},{10,11... | collective-permute-start | bytes 1966088 | tf_op jit(solution)/shard_map/ppermute | solution.py:509
  59.8 5.3 %collective-permute-start.12 = (bf16[512,512]{1,0:T(8,128)(2,1)S(1)}, bf16[512,512]{1,0:T(8,128)(2,1)S(1)}, u32[]{:S(2)}, u32[]{:S(2)}) collective-permute-start(bf16[512,512]{1,0:T(8,128)(2,1)S(1)} %get-tuple-element.111), channel_id=1, source_target_pairs={{0,16},{16,0},{1,17},{17,1},{2,18},{18,2},{3,19},{19,3},{4,20},{20... | collective-permute-start | bytes 1572872 | tf_op jit(solution)/shard_map/ppermute | solution.py:501
  75.1 6.4 %collective-permute-start.14 = (bf16[512,512]{1,0:T(8,128)(2,1)S(1)}, bf16[512,512]{1,0:T(8,128)(2,1)S(1)}, u32[]{:S(2)}, u32[]{:S(2)}) collective-permute-start(bf16[512,512]{1,0:T(8,128)(2,1)S(1)} %get-tuple-element.109), channel_id=1, source_target_pairs={{0,16},{16,0},{1,17},{17,1},{2,18},{18,2},{3,19},{19,3},{4,20},{20... | collective-permute-start | bytes 1572872 | tf_op jit(solution)/shard_map/ppermute | solution.py:501
  88.2 11.0 %collective-permute-start.15 = (bf16[4,64,1280]{2,1,0:T(8,128)(2,1)S(1)}, bf16[4,64,1280]{2,1,0:T(8,128)(2,1)S(1)}, u32[]{:S(2)}, u32[]{:S(2)}) collective-permute-start(bf16[4,64,1280]{2,1,0:T(8,128)(2,1)S(1)} %get-tuple-element.86), channel_id=1, source_target_pairs={{0,3},{1,2},{2,1},{3,0},{4,7},{5,6},{6,5},{7,4},{8,11},{9,10},{10,... | collective-permute-start | bytes 1966088 | tf_op jit(solution)/shard_map/ppermute | solution.py:509
  89.3 9.9 %collective-permute-start.16 = (bf16[4,64,1280]{2,1,0:T(8,128)(2,1)S(1)}, bf16[4,64,1280]{2,1,0:T(8,128)(2,1)S(1)}, u32[]{:S(2)}, u32[]{:S(2)}) collective-permute-start(bf16[4,64,1280]{2,1,0:T(8,128)(2,1)S(1)} %get-tuple-element.87), channel_id=1, source_target_pairs={{0,1},{1,0},{2,3},{3,2},{4,5},{5,4},{6,7},{7,6},{8,9},{9,8},{10,11... | collective-permute-start | bytes 1966088 | tf_op jit(solution)/shard_map/ppermute | solution.py:509
  89.3 16.9 %collective-permute-start.17 = (bf16[4,64,1280]{2,1,0:T(8,128)(2,1)S(1)}, bf16[4,64,1280]{2,1,0:T(8,128)(2,1)S(1)}, u32[]{:S(2)}, u32[]{:S(2)}) collective-permute-start(bf16[4,64,1280]{2,1,0:T(8,128)(2,1)S(1)} %get-tuple-element.88), channel_id=1, source_target_pairs={{0,3},{1,2},{2,1},{3,0},{4,7},{5,6},{6,5},{7,4},{8,11},{9,10},{10,... | collective-permute-start | bytes 1966088 | tf_op jit(solution)/shard_map/ppermute | solution.py:509
  91.0 15.3 %collective-permute-start.18 = (bf16[4,64,1280]{2,1,0:T(8,128)(2,1)S(1)}, bf16[4,64,1280]{2,1,0:T(8,128)(2,1)S(1)}, u32[]{:S(2)}, u32[]{:S(2)}) collective-permute-start(bf16[4,64,1280]{2,1,0:T(8,128)(2,1)S(1)} %get-tuple-element.89), channel_id=1, source_target_pairs={{0,1},{1,0},{2,3},{3,2},{4,5},{5,4},{6,7},{7,6},{8,9},{9,8},{10,11... | collective-permute-start | bytes 1966088 | tf_op jit(solution)/shard_map/ppermute | solution.py:509
  106.4 11.0 %collective-permute-start.20 = (bf16[4,64,1280]{2,1,0:T(8,128)(2,1)S(1)}, bf16[4,64,1280]{2,1,0:T(8,128)(2,1)S(1)}, u32[]{:S(2)}, u32[]{:S(2)}) collective-permute-start(bf16[4,64,1280]{2,1,0:T(8,128)(2,1)S(1)} %add_convert_fusion.2), channel_id=1, source_target_pairs={{0,3},{1,2},{2,1},{3,0},{4,7},{5,6},{6,5},{7,4},{8,11},{9,10},{10,... | collective-permute-start | bytes 1966088 | tf_op jit(solution)/shard_map/ppermute | solution.py:509
  108.1 10.0 %collective-permute-start.19 = (bf16[4,64,1280]{2,1,0:T(8,128)(2,1)S(1)}, bf16[4,64,1280]{2,1,0:T(8,128)(2,1)S(1)}, u32[]{:S(2)}, u32[]{:S(2)}) collective-permute-start(bf16[4,64,1280]{2,1,0:T(8,128)(2,1)S(1)} %add_convert_fusion.3), channel_id=1, source_target_pairs={{0,1},{1,0},{2,3},{3,2},{4,5},{5,4},{6,7},{7,6},{8,9},{9,8},{10,11... | collective-permute-start | bytes 1966088 | tf_op jit(solution)/shard_map/ppermute | solution.py:509
  118.7 6.3 %collective-permute-start.21 = (bf16[64,2560]{1,0:T(8,128)(2,1)S(1)}, bf16[64,2560]{1,0:T(8,128)(2,1)S(1)}, u32[]{:S(2)}, u32[]{:S(2)}) collective-permute-start(bf16[64,2560]{1,0:T(8,128)(2,1)S(1)} %get-tuple-element.106), channel_id=1, source_target_pairs={{0,4},{1,5},{2,6},{3,7},{4,0},{5,1},{6,2},{7,3},{8,12},{9,13},{10,... | collective-permute-start | bytes 983048 | tf_op jit(solution)/shard_map/ppermute | solution.py:509
  118.8 11.1 %collective-permute-start.23 = (bf16[64,2560]{1,0:T(8,128)(2,1)S(1)}, bf16[64,2560]{1,0:T(8,128)(2,1)S(1)}, u32[]{:S(2)}, u32[]{:S(2)}) collective-permute-start(bf16[64,2560]{1,0:T(8,128)(2,1)S(1)} %get-tuple-element.107), channel_id=1, source_target_pairs={{0,8},{1,9},{2,10},{3,11},{4,12},{5,13},{6,14},{7,15},{8,0},{9,1},... | collective-permute-start | bytes 983048 | tf_op jit(solution)/shard_map/ppermute | solution.py:509
  121.6 10.9 %collective-permute-start.22 = (bf16[64,2560]{1,0:T(8,128)(2,1)S(1)}, bf16[64,2560]{1,0:T(8,128)(2,1)S(1)}, u32[]{:S(2)}, u32[]{:S(2)}) collective-permute-start(bf16[64,2560]{1,0:T(8,128)(2,1)S(1)} %get-tuple-element.108), channel_id=1, source_target_pairs={{0,12},{1,13},{2,14},{3,15},{4,8},{5,9},{6,10},{7,11},{8,4},{9,5},... | collective-permute-start | bytes 983048 | tf_op jit(solution)/shard_map/ppermute | solution.py:509
  164.9 19.3 %collective-permute-start.24 = (bf16[64,2560]{1,0:T(8,128)(2,1)S(1)}, bf16[64,2560]{1,0:T(8,128)(2,1)S(1)}, u32[]{:S(2)}, u32[]{:S(2)}) collective-permute-start(bf16[64,2560]{1,0:T(8,128)(2,1)S(1)} %bitcast.36), channel_id=1, source_target_pairs={{0,16},{16,0},{1,17},{17,1},{2,18},{18,2},{3,19},{19,3},{4,20},{20... | collective-permute-start | bytes 983048 | tf_op jit(solution)/shard_map/ppermute | solution.py:501
  (18 other events, 404.2 us)

commit v5 on v4

--- a/solution.py
+++ b/solution.py
@@ -91,7 +91,7 @@
     normed,
     *refs,
 ):
-    projected, scores, mixed, outer, weight = refs[8:]
+    projected, gating, scores, mixed, outer, weight = refs[8:]
     count, rows, width = mixed.shape
     share = outer.shape[1] // 2
 
@@ -99,19 +99,20 @@
     def _():
         def store_0(at, block):
             weight[at, :width] = block[:, :width]
-            weight[at, 2 * width :] = block[:, width : 2 * width]
+            weight[at, 2 * width : 3 * width] = block[:, width : 2 * width]
             outer[at, :share] = block[:, 2 * width :]
 
         def store_1(at, block):
             weight[at, width : 2 * width] = block[:, :width]
+            weight[at, 3 * width :] = block[:, width : 2 * width]
             outer[at, share:] = block[:, 2 * width :]
 
         place_rows(0, place, refs[:4], store_0)
         place_rows(1, place, refs[4:8], store_1)
 
-    projected[...] = dot_nn(normed[...].reshape(count * rows, -1), weight[...]).reshape(
-        projected.shape
-    )
+    lines = normed[...].reshape(count * rows, -1)
+    projected[...] = dot_nn(lines, weight[:, : 3 * width]).reshape(projected.shape)
+    gating[...] = dot_nn(lines, weight[:, 3 * width :]).reshape(gating.shape)
     for item in range(count):
         proj = projected[item]
         held = (proj * sigmoid(proj)).astype(jnp.bfloat16)
@@ -127,33 +128,9 @@
             mixed[item, :, start : start + HEAD_WIDTH] = dot_nn(attention, values)
 
 
-def gating_kernel(
-    place,
-    normed,
-    held_0,
-    held_1,
-    held_2,
-    held_3,
-    masked,
-    keep,
-    recv,
-    mixed,
-    gating_out,
-    grad_gated,
-    stats,
-    weight,
-):
+def gating_kernel(place, gating, masked, keep, recv, mixed, grad_gated, stats):
     count, rows, width = mixed.shape
-
-    @pl.when(pl.program_id(0) == 0)
-    def _():
-        def store(at, block):
-            weight[at, :] = block
-
-        place_rows(1, place, (held_0, held_1, held_2, held_3), store)
-
-    proj = dot_nn(normed[...].reshape(count * rows, -1), weight[...])
-    gating_out[...] = proj.reshape(gating_out.shape)
+    proj = gating[...].reshape(count * rows, width)
     core = place[1]
     mine = masked[:, :, pl.ds(pl.multiple_of(core * width, width), width)]
     others = masked[:, :, pl.ds(pl.multiple_of((1 - core) * width, width), width)]
@@ -294,14 +271,6 @@
     )
 
 
-def columns_of(value, width, at):
-    return pl.BlockSpec(
-        (*value.shape[:-1], width),
-        lambda i, *_: (0,) * (value.ndim - 1) + (at,),
-        pipeline_mode=pl.Buffered(buffer_count=1),
-    )
-
-
 def call(kernel, name, grid, prefetch, in_specs, out, inputs, scratch=(), room=18):
     moved = sum(v.size * v.dtype.itemsize for v in inputs)
     return pl.pallas_call(
@@ -333,39 +302,36 @@
         + [whole(*part.shape) for part in held],
         [
             (rows_of(rows, 3 * width, some=2), (count, rows, 3 * width), jnp.float32),
+            (rows_of(rows, width, some=2), (count, rows, width), jnp.float32),
             (rows_of(heads, rows, rows, some=2), (count, heads, rows, rows), jnp.float32),
             (rows_of(rows, width, some=2), (count, rows, width), jnp.float32),
             (whole(depth, width), (depth, width), jnp.bfloat16),
         ],
         (normed, *held),
-        [pltpu.VMEM((depth, 3 * width), jnp.bfloat16)],
-        room=28,
-    )
-
-
-def gating_forward(place, normed, gating, masked, keep, recv, mixed):
-    count, rows, depth = normed.shape
-    width = mixed.shape[2]
+        [pltpu.VMEM((depth, 4 * width), jnp.bfloat16)],
+        room=30,
+    )
+
+
+def gating_forward(place, gating, masked, keep, recv, mixed):
+    count, rows, width = mixed.shape
     return call(
         gating_kernel,
         "gating_forward",
         (count // 2,),
         (place,),
         [
-            rows_of(rows, depth, some=2),
-            *(columns_of(part, width, 1) for part in gating),
-            rows_of(rows, depth, some=2),
+            rows_of(rows, width, some=2),
+            rows_of(rows, 2 * width, some=2),
             whole(*keep.shape),
             whole(*recv.shape),
             rows_of(rows, width, some=2),
         ],
         [
-            (rows_of(rows, width, some=2), (count, rows, width), jnp.float32),
             (rows_of(rows, width, some=2), (count, rows, width), jnp.bfloat16),
             (rows_of(rows, 128, some=2), (count, rows, 128), jnp.float32),
         ],
-        (normed, *gating, masked, keep, recv, mixed),
-        [pltpu.VMEM((depth, width), jnp.bfloat16)],
+        (gating, masked, keep, recv, mixed),
         room=18,
     )
 
@@ -387,7 +353,12 @@
         "outer_term",
         (count // 2,),
         (place,),
-        [block, block, *stats_specs(count, rows, 2), rows_of(rows, 2 * width, some=2)],
+        [
+            rows_of(rows, width, some=2),
+            block,
+            *stats_specs(count, rows, 2),
+            rows_of(rows, 2 * width, some=2),
+        ],
         [(whole(*shape), shape, jnp.bfloat16)],
         (gating, mixed, stats, stats_other, masked),
         [pltpu.VMEM(shape, jnp.float32)],
@@ -521,9 +492,9 @@
             held, beside = lax.optimization_barrier((held, beside))
     first = [over_link(part, *ROUNDS[turn][2]) for turn, part in enumerate(held)]
     second = [over_link(part, *ROUNDS[turn][3]) for turn, part in enumerate(held)]
-    first, second = lax.optimization_barrier((first, second))
+    first = lax.optimization_barrier(first)
     both = [over_link(part, *ROUNDS[turn][3]) for turn, part in enumerate(first)]
-    both, beside = lax.optimization_barrier((both, join(beside)))
+    second, both, beside = lax.optimization_barrier((second, both, join(beside)))
     return list(zip(held, first, second, both)), beside
 
 
@@ -535,7 +506,7 @@
     mine, first, second, both = zip(*parts)
     both = [over_link(part, *ROUNDS[turn][3]) for turn, part in enumerate(both)]
     second = [over_link(part, *ROUNDS[turn][3]) for turn, part in enumerate(second)]
-    first, both, second = lax.optimization_barrier((first, both, second))
+    first, both = lax.optimization_barrier((first, both))
     first = [add_blocks(*pair) for pair in zip(first, both)]
     first = [over_link(part, *ROUNDS[turn][2]) for turn, part in enumerate(first)]
     mine, first, second = lax.optimization_barrier((mine, first, second))
@@ -604,13 +575,13 @@
         join,
     )
 
-    projected, scores, mixed, outer_cols = attention_forward(
+    projected, gating, scores, mixed, outer_cols = attention_forward(
         place, all_lengths, normed, (*parts[0], *parts[1])
     )
     outer_cols = outer_cols.reshape(2, half, half)
     keep = lax.dynamic_index_in_dim(outer_cols, core, axis=0, keepdims=False)
     recv = swap_cores(lax.dynamic_index_in_dim(outer_cols, 1 - core, axis=0, keepdims=False))
-    gating, grad_gated, stats = gating_forward(place, normed, parts[1], masked, keep, recv, mixed)
+    grad_gated, stats = gating_forward(place, gating, masked, keep, recv, mixed)
     stats_other = swap_cores(stats)
     outer = outer_term(place, gating, mixed, stats, stats_other, masked)
     outer_recv = swap_cores(outer[1])

time: 188 us -> 176 us (0.936)
  waiting for transfers between devices: 62.3 us -> 51.6 us
  starting transfers between devices: 33.6 us -> 31.4 us
    ppermute x19, waiting for transfers between devices: 59.2 us -> 48.5 us  [over_link(): return lax.ppermute(values, ('c', *OWN), pairs)]
    ppermute x6, starting transfers between devices: 14.7 us -> 11.9 us  [swap_cores(): return lax.ppermute(values, 'c', SWAP)]
  transfers between devices with their start and end apart: 25 -> 25, of which waited for: 17 -> 15; matrix products, arithmetic and copies ran while one was open for 7% -> 6% of each run, Pallas kernels for 3% -> 3%
where the time goes in v5:
time: 176 us; the launch traced here: 175 us
  waiting for transfers between devices  51.6 us (29%)
  blocking collectives  43.4 us (25%)
  starting transfers between devices  31.4 us (18%)
  Pallas kernels  30.9 us (18%)
  local copies, waits for them, and re-layouts  9.98 us (6%)
  other arithmetic  6.75 us (4%)
    ppermute x19, waiting for transfers between devices, over_link(): return lax.ppermute(values, ('c', *OWN), pairs)  48.5 us
    all_to_all x3, blocking collectives, exchange(): return lax.all_to_all(blocks, axes, 0, 0, tiled=True)  43.4 us
    pallas_call x6, Pallas kernels, call(): pl.pallas_call(kernel, grid_spec=pltpu.PrefetchScalarGridSpec(num_scalar_...  30.9 us
    ppermute x19, starting transfers between devices, over_link(): return lax.ppermute(values, ('c', *OWN), pairs)  19.5 us
    ppermute x6, starting transfers between devices, swap_cores(): return lax.ppermute(values, 'c', SWAP)  11.9 us
  transfers between devices with their start and end apart: 25, of which 15 were waited for; matrix products, arithmetic and copies ran while one was open for 6% of the time, Pallas kernels for 3%

profile of v5, /device:TPU:1, one launch (start us, length us, event | category | flops | bytes accessed | tf_op | source)
XLA Modules:
  0.0 175.3 jit_solution(6920129865562172195)
XLA Ops:
  2.5 3.7 %collective-permute-start.1 = (bf16[1,64,1280]{2,1,0:T(8,128)(2,1)S(1)}, bf16[1,64,1280]{2,1,0:T(8,128)(2,1)S(1)}, u32[]{:S(2)}, u32[]{:S(2)}) collective-permute-start(bf16[1,64,1280]{2,1,0:T(8,128)(2,1)S(1)} %maximum_bitcast_fusion.2), channel_id=1, source_target_pairs={{0,12},{1,13},{2,14},{3,15},{4,8},{5,9},{6,10},{7,11},{8,4},{9,5},... | collective-permute-start | bytes 491528 | tf_op jit(solution)/shard_map/ppermute | solution.py:480
  16.6 3.2 %collective-permute-done.4 = bf16[2,64,1280]{2,1,0:T(8,128)(2,1)S(1)} collective-permute-done((bf16[2,64,1280]{2,1,0:T(8,128)(2,1)S(1)}, bf16[2,64,1280]{2,1,0:T(8,128)(2,1)S(1)}, u32[]{:S(2)}, u32[]{:S(2)}) %collective-permute-start.4) | collective-permute-done | bytes 327712 | tf_op jit(solution)/shard_map/ppermute | solution.py:480
  19.8 2.0 %collective-permute-done.3 = bf16[2,64,1280]{2,1,0:T(8,128)(2,1)S(1)} collective-permute-done((bf16[2,64,1280]{2,1,0:T(8,128)(2,1)S(1)}, bf16[2,64,1280]{2,1,0:T(8,128)(2,1)S(1)}, u32[]{:S(2)}, u32[]{:S(2)}) %collective-permute-start.3) | collective-permute-done | bytes 327712 | tf_op jit(solution)/shard_map/ppermute | solution.py:480
  26.3 6.8 %collective-permute-done.8.refs_1_ = bf16[4,64,1280]{2,1,0:T(8,128)(2,1)} collective-permute-done((bf16[4,64,1280]{2,1,0:T(8,128)(2,1)S(1)}, bf16[4,64,1280]{2,1,0:T(8,128)(2,1)}, u32[]{:S(2)}, u32[]{:S(2)}) %collective-permute-start.8) | collective-permute-done | bytes 655392 | tf_op jit(solution)/shard_map/ppermute | solution.py:480
  35.5 3.3 %fusion.13 = (bf16[2,256,1024]{2,1,0:T(8,128)(2,1)}, bf16[2,256,1024]{2,1,0:T(8,128)(2,1)S(1)}, bf16[2,256,1024]{2,1,0:T(8,128)(2,1)S(1)}, bf16[2,256,1024]{2,1,0:T(8,128)(2,1)}) fusion(bf16[4,256,1024]{2,1,0:T(8,128)(2,1)S(1)} %pad_maximum_fusion, bf16[4,256,1024]{2,1,0:T(8,128)(2,1)} %copy-done.8), kind=kLoop, calls=%fused_computation.53 | loop fusion | bytes 8388608 | tf_op jit(solution)/shard_map/slice | solution.py:563
  39.0 2.6 %copy.17 = bf16[1024,1024]{0,1:T(8,128)(2,1)} copy(bf16[1024,1024]{1,0:T(8,128)(2,1)S(1)} %bitcast.33) | data formatting | bytes 4194304 | tf_op jit(solution)/shard_map/reshape | solution.py:567
  43.4 5.0 %collective-permute-done.10.refs_3_ = bf16[4,64,1280]{2,1,0:T(8,128)(2,1)} collective-permute-done((bf16[4,64,1280]{2,1,0:T(8,128)(2,1)}, bf16[4,64,1280]{2,1,0:T(8,128)(2,1)}, u32[]{:S(2)}, u32[]{:S(2)}) %collective-permute-start.10) | collective-permute-done | bytes 655392 | tf_op jit(solution)/shard_map/ppermute | solution.py:480
  48.4 8.8 %attention_forward.1 = (f32[4,256,1536]{2,1,0:T(8,128)S(1)}, f32[4,256,512]{2,1,0:T(8,128)S(1)}, f32[4,2,256,256]{3,2,1,0:T(8,128)S(1)}, f32[4,256,512]{2,1,0:T(8,128)S(1)}, bf16[1024,512]{1,0:T(8,128)(2,1)S(1)}) custom-call(s32[2]{0:T(128)S(1)} %pad_add_fusion.place, s32[4]{0:T(128)S(1)} %pad_add_fusion.1.lengths, ...), custom_call_target="tpu_custom_call" | custom-call | flops 1 | bytes 1 | tf_op jit(solution)/shard_map/attention_forward/pallas_call | solution.py:276
  57.3 2.7 %collective-permute-start.12 = (bf16[512,512]{1,0:T(8,128)(2,1)S(1)}, bf16[512,512]{1,0:T(8,128)(2,1)S(1)}, u32[]{:S(2)}, u32[]{:S(2)}) collective-permute-start(bf16[512,512]{1,0:T(8,128)(2,1)S(1)} %get-tuple-element.107), channel_id=1, source_target_pairs={{0,16},{16,0},{1,17},{17,1},{2,18},{18,2},{3,19},{19,3},{4,20},{20... | collective-permute-start | bytes 1572872 | tf_op jit(solution)/shard_map/ppermute | solution.py:472
  61.5 2.5 %gating_forward.1 = (bf16[4,256,512]{2,1,0:T(8,128)(2,1)S(1)}, f32[4,256,128]{2,1,0:T(8,128)S(1)}) custom-call(s32[2]{0:T(128)S(1)} %pad_add_fusion.place, f32[4,256,512]{2,1,0:T(8,128)S(1)} %get-tuple-element.72.gating.gating_in.projected, bf16[4,256,1024]{2,1,0:T(8,128)(2,1)S(1)} %pad_maximum_fusion.2.masked, ...), custom_call_target="tpu_custom_call" | custom-call | flops 1 | bytes 1 | tf_op jit(solution)/shard_map/gating_forward/pallas_call | solution.py:276
  66.0 3.3 %outer_term.1 = bf16[2,512,512]{2,1,0:T(8,128)(2,1)S(1)} custom-call(s32[2]{0:T(128)S(1)} %pad_add_fusion.place, f32[4,256,512]{2,1,0:T(8,128)S(1)} %get-tuple-element.72.gating.gating_in.projected, f32[4,256,512]{2,1,0:T(8,128)S(1)} %get-tuple-element.75.mixed, f32[4,256,128]{2,1,0:T(8,128)S(1)} %get-tuple-element.79.stats, ...), custom_call_target="tpu_custom_call" | custom-call | flops 1 | bytes 1 | tf_op jit(solution)/shard_map/outer_term/pallas_call | solution.py:276
  70.1 5.9 %attention_back.1 = bf16[4,256,2048]{2,1,0:T(8,128)(2,1)S(1)} custom-call(s32[4]{0:T(128)S(1)} %pad_add_fusion.1.lengths, f32[4,256,512]{2,1,0:T(8,128)S(1)} %get-tuple-element.72.gating.gating_in.projected, f32[4,256,1536]{2,1,0:T(8,128)S(1)} %get-tuple-element.73.projected, f32[4,2,256,256]{3,2,1,0:T(8,128)S(1)} %get-tuple-element.74.scores, ...), custom_call_target="tpu_custom_call" | custom-call | flops 1 | bytes 1 | tf_op jit(solution)/shard_map/attention_back/pallas_call | solution.py:276
  76.0 6.6 %terms.1 = (bf16[4,64,1280]{2,1,0:T(8,128)(2,1)S(1)}, bf16[4,64,1280]{2,1,0:T(8,128)(2,1)S(1)}, bf16[4,64,1280]{2,1,0:T(8,128)(2,1)S(1)}, bf16[4,64,1280]{2,1,0:...) custom-call(s32[2]{0:T(128)S(1)} %pad_add_fusion.place, ...), custom_call_target="tpu_custom_call" | custom-call | flops 1 | bytes 1 | tf_op jit(solution)/shard_map/terms/pallas_call | solution.py:276
  86.3 7.4 %collective-permute-done.15 = bf16[4,64,1280]{2,1,0:T(8,128)(2,1)S(1)} collective-permute-done((bf16[4,64,1280]{2,1,0:T(8,128)(2,1)S(1)}, bf16[4,64,1280]{2,1,0:T(8,128)(2,1)S(1)}, u32[]{:S(2)}, u32[]{:S(2)}) %collective-permute-start.15) | collective-permute-done | bytes 655392 | tf_op jit(solution)/shard_map/ppermute | solution.py:480
  95.7 5.1 %collective-permute-done.19 = bf16[4,64,1280]{2,1,0:T(8,128)(2,1)S(1)} collective-permute-done((bf16[4,64,1280]{2,1,0:T(8,128)(2,1)S(1)}, bf16[4,64,1280]{2,1,0:T(8,128)(2,1)S(1)}, u32[]{:S(2)}, u32[]{:S(2)}) %collective-permute-start.19) | collective-permute-done | bytes 655392 | tf_op jit(solution)/shard_map/ppermute | solution.py:480
  100.7 7.0 %collective-permute-done.18 = bf16[4,64,1280]{2,1,0:T(8,128)(2,1)S(1)} collective-permute-done((bf16[4,64,1280]{2,1,0:T(8,128)(2,1)S(1)}, bf16[4,64,1280]{2,1,0:T(8,128)(2,1)S(1)}, u32[]{:S(2)}, u32[]{:S(2)}) %collective-permute-start.18) | collective-permute-done | bytes 655392 | tf_op jit(solution)/shard_map/ppermute | solution.py:480
  108.4 2.0 %collective-permute-start.22 = (bf16[64,2560]{1,0:T(8,128)(2,1)S(1)}, bf16[64,2560]{1,0:T(8,128)(2,1)S(1)}, u32[]{:S(2)}, u32[]{:S(2)}) collective-permute-start(bf16[64,2560]{1,0:T(8,128)(2,1)S(1)} %get-tuple-element.104), channel_id=1, source_target_pairs={{0,12},{1,13},{2,14},{3,15},{4,8},{5,9},{6,10},{7,11},{8,4},{9,5},... | collective-permute-start | bytes 983048 | tf_op jit(solution)/shard_map/ppermute | solution.py:480
  111.7 3.0 %collective-permute-done.21 = bf16[64,2560]{1,0:T(8,128)(2,1)S(1)} collective-permute-done((bf16[64,2560]{1,0:T(8,128)(2,1)S(1)}, bf16[64,2560]{1,0:T(8,128)(2,1)S(1)}, u32[]{:S(2)}, u32[]{:S(2)}) %collective-permute-start.21) | collective-permute-done | bytes 327712 | tf_op jit(solution)/shard_map/ppermute | solution.py:480
  114.6 3.3 %collective-permute-done.22 = bf16[64,2560]{1,0:T(8,128)(2,1)S(1)} collective-permute-done((bf16[64,2560]{1,0:T(8,128)(2,1)S(1)}, bf16[64,2560]{1,0:T(8,128)(2,1)S(1)}, u32[]{:S(2)}, u32[]{:S(2)}) %collective-permute-start.22) | collective-permute-done | bytes 327712 | tf_op jit(solution)/shard_map/ppermute | solution.py:480
  120.1 18.4 %all_to_all.25 = bf16[8,8,2560]{2,1,0:T(8,128)(2,1)} all-to-all(bf16[8,8,2560]{2,1,0:T(8,128)(2,1)S(1)} %maximum_bitcast_fusion), channel_id=1, replica_groups=mesh['z'=8,'c'=2,'x'=4,'y'=4] {'z'}, dimensions={0} | all-to-all | bytes 655360 | tf_op jit(solution)/shard_map/all_to_all | solution.py:519
  139.6 12.6 %all_to_all.26 = bf16[8,8,2560]{2,1,0:T(8,128)(2,1)S(1)} all-to-all(bf16[8,8,2560]{2,1,0:T(8,128)(2,1)S(1)} %broadcast_in_dim.35), channel_id=1, replica_groups=mesh['z'=8,'c'=2,'x'=4,'y'=4] {'z'}, dimensions={0} | all-to-all | bytes 655360 | tf_op jit(solution)/shard_map/all_to_all | solution.py:519
  152.1 5.4 %collective-permute-start.24 = (bf16[64,2560]{1,0:T(8,128)(2,1)S(1)}, bf16[64,2560]{1,0:T(8,128)(2,1)S(1)}, u32[]{:S(2)}, u32[]{:S(2)}) collective-permute-start(bf16[64,2560]{1,0:T(8,128)(2,1)S(1)} %bitcast.36), channel_id=1, source_target_pairs={{0,16},{16,0},{1,17},{17,1},{2,18},{18,2},{3,19},{19,3},{4,20},{20... | collective-permute-start | bytes 983048 | tf_op jit(solution)/shard_map/ppermute | solution.py:472
  159.0 12.4 %all_to_all.27 = f32[32,8,128]{2,1,0:T(8,128)S(1)} all-to-all(f32[32,8,128]{2,1,0:T(8,128)S(1)} %broadcast_in_dim.36), channel_id=1, replica_groups=mesh['z'=8,'c'=2,'x'=4,'y'=4] {'c','x','y'}, dimensions={0} | all-to-all | bytes 262144 | tf_op jit(solution)/shard_map/all_to_all | solution.py:519
  171.4 3.7 %update_rows.1 = (f32[64,4096]{1,0:T(8,128)}, f32[64,4096]{1,0:T(8,128)}, f32[64,4096]{1,0:T(8,128)}, f32[64,1024]{1,0:T(8,128)}, f32[64,1024]{1,0:T(8,128)}, /*index=5*/f32[64,1024]{1,0:T(8,128)}) custom-call(s32[2]{0:T(128)S(1)} %pad_add_fusion.place, f32[256,128]{1,0:T(8,128)S(1)} %bitcast.39, bf16[64,2560]{1,0:T(8,128)(2,1)S(1)} %bitcast.37, ...), custom_call_target="tpu_custom_call" | custom-call | flops 1 | bytes 1 | tf_op jit(solution)/shard_map/update_rows/pallas_call | solution.py:276
  (94 shorter events, 37.4 us)
Async XLA Ops:
  2.5 6.4 %collective-permute-start.1 = (bf16[1,64,1280]{2,1,0:T(8,128)(2,1)S(1)}, bf16[1,64,1280]{2,1,0:T(8,128)(2,1)S(1)}, u32[]{:S(2)}, u32[]{:S(2)}) collective-permute-start(bf16[1,64,1280]{2,1,0:T(8,128)(2,1)S(1)} %maximum_bitcast_fusion.2), channel_id=1, source_target_pairs={{0,12},{1,13},{2,14},{3,15},{4,8},{5,9},{6,10},{7,11},{8,4},{9,5},... | collective-permute-start | bytes 491528 | tf_op jit(solution)/shard_map/ppermute | solution.py:480
  6.2 4.6 %collective-permute-start = (bf16[1,64,1280]{2,1,0:T(8,128)(2,1)S(1)}, bf16[1,64,1280]{2,1,0:T(8,128)(2,1)S(1)}, u32[]{:S(2)}, u32[]{:S(2)}) collective-permute-start(bf16[1,64,1280]{2,1,0:T(8,128)(2,1)S(1)} %maximum_bitcast_fusion.1), channel_id=1, source_target_pairs={{0,4},{1,5},{2,6},{3,7},{4,0},{5,1},{6,2},{7,3},{8,12},{9,13},{10,... | collective-permute-start | bytes 491528 | tf_op jit(solution)/shard_map/ppermute | solution.py:480
  6.3 4.5 %collective-permute-start.2 = (s32[2]{0:T(128)}, s32[2]{0:T(128)S(1)}, u32[]{:S(2)}, u32[]{:S(2)}) collective-permute-start(s32[2]{0:T(128)} %param.12), channel_id=1, source_target_pairs={{0,16},{16,0},{1,17},{17,1},{2,18},{18,2},{3,19},{19,3},{4,20},{20... | collective-permute-start | bytes 32 | tf_op jit(solution)/shard_map/ppermute | solution.py:472
  11.7 10.1 %collective-permute-start.5 = (bf16[4,256,1024]{2,1,0:T(8,128)(2,1)S(1)}, bf16[4,256,1024]{2,1,0:T(8,128)(2,1)S(1)}, u32[]{:S(2)}, u32[]{:S(2)}) collective-permute-start(bf16[4,256,1024]{2,1,0:T(8,128)(2,1)S(1)} %pad_maximum_fusion), channel_id=1, source_target_pairs={{0,16},{16,0},{1,17},{17,1},{2,18},{18,2},{3,19},{19,3},{4,20},{20... | collective-permute-start | bytes 6291464 | tf_op jit(solution)/shard_map/ppermute | solution.py:472
  13.5 6.2 %collective-permute-start.4 = (bf16[2,64,1280]{2,1,0:T(8,128)(2,1)S(1)}, bf16[2,64,1280]{2,1,0:T(8,128)(2,1)S(1)}, u32[]{:S(2)}, u32[]{:S(2)}) collective-permute-start(bf16[2,64,1280]{2,1,0:T(8,128)(2,1)S(1)} %pad_maximum_fusion.7), channel_id=1, source_target_pairs={{0,4},{1,5},{2,6},{3,7},{4,0},{5,1},{6,2},{7,3},{8,12},{9,13},{10,... | collective-permute-start | bytes 983048 | tf_op jit(solution)/shard_map/ppermute | solution.py:480
  14.7 7.1 %collective-permute-start.3 = (bf16[2,64,1280]{2,1,0:T(8,128)(2,1)S(1)}, bf16[2,64,1280]{2,1,0:T(8,128)(2,1)S(1)}, u32[]{:S(2)}, u32[]{:S(2)}) collective-permute-start(bf16[2,64,1280]{2,1,0:T(8,128)(2,1)S(1)} %pad_maximum_fusion.6), channel_id=1, source_target_pairs={{0,12},{1,13},{2,14},{3,15},{4,8},{5,9},{6,10},{7,11},{8,4},{9,5},... | collective-permute-start | bytes 983048 | tf_op jit(solution)/shard_map/ppermute | solution.py:480
  23.3 9.8 %collective-permute-start.8 = (bf16[4,64,1280]{2,1,0:T(8,128)(2,1)S(1)}, bf16[4,64,1280]{2,1,0:T(8,128)(2,1)}, u32[]{:S(2)}, u32[]{:S(2)}) collective-permute-start(bf16[4,64,1280]{2,1,0:T(8,128)(2,1)S(1)} %pad_maximum_fusion.3.refs_0_), channel_id=1, source_target_pairs={{0,1},{1,0},{2,3},{3,2},{4,5},{5,4},{6,7},{7,6},{8,9},{9,8},{10,11... | collective-permute-start | bytes 1966088 | tf_op jit(solution)/shard_map/ppermute | solution.py:480
  23.3 11.0 %collective-permute-start.9 = (bf16[4,64,1280]{2,1,0:T(8,128)(2,1)S(1)}, bf16[4,64,1280]{2,1,0:T(8,128)(2,1)}, u32[]{:S(2)}, u32[]{:S(2)}) collective-permute-start(bf16[4,64,1280]{2,1,0:T(8,128)(2,1)S(1)} %pad_maximum_fusion.4.refs_4_), channel_id=1, source_target_pairs={{0,3},{1,2},{2,1},{3,0},{4,7},{5,6},{6,5},{7,4},{8,11},{9,10},{10,... | collective-permute-start | bytes 1966088 | tf_op jit(solution)/shard_map/ppermute | solution.py:480
  24.5 18.9 %collective-permute-start.6 = (bf16[4,64,1280]{2,1,0:T(8,128)(2,1)S(1)}, bf16[4,64,1280]{2,1,0:T(8,128)(2,1)}, u32[]{:S(2)}, u32[]{:S(2)}) collective-permute-start(bf16[4,64,1280]{2,1,0:T(8,128)(2,1)S(1)} %pad_maximum_fusion.3.refs_0_), channel_id=1, source_target_pairs={{0,3},{1,2},{2,1},{3,0},{4,7},{5,6},{6,5},{7,4},{8,11},{9,10},{10,... | collective-permute-start | bytes 1966088 | tf_op jit(solution)/shard_map/ppermute | solution.py:480
  26.0 17.4 %collective-permute-start.7 = (bf16[4,64,1280]{2,1,0:T(8,128)(2,1)S(1)}, bf16[4,64,1280]{2,1,0:T(8,128)(2,1)}, u32[]{:S(2)}, u32[]{:S(2)}) collective-permute-start(bf16[4,64,1280]{2,1,0:T(8,128)(2,1)S(1)} %pad_maximum_fusion.4.refs_4_), channel_id=1, source_target_pairs={{0,1},{1,0},{2,3},{3,2},{4,5},{5,4},{6,7},{7,6},{8,9},{9,8},{10,11... | collective-permute-start | bytes 1966088 | tf_op jit(solution)/shard_map/ppermute | solution.py:480
  34.3 14.0 %collective-permute-start.10 = (bf16[4,64,1280]{2,1,0:T(8,128)(2,1)}, bf16[4,64,1280]{2,1,0:T(8,128)(2,1)}, u32[]{:S(2)}, u32[]{:S(2)}) collective-permute-start(bf16[4,64,1280]{2,1,0:T(8,128)(2,1)} %collective-permute-done.8.refs_1_), channel_id=1, source_target_pairs={{0,3},{1,2},{2,1},{3,0},{4,7},{5,6},{6,5},{7,4},{8,11},{9,10},{10,... | collective-permute-start | bytes 1966088 | tf_op jit(solution)/shard_map/ppermute | solution.py:480
  35.5 12.9 %collective-permute-start.11 = (bf16[4,64,1280]{2,1,0:T(8,128)(2,1)}, bf16[4,64,1280]{2,1,0:T(8,128)(2,1)}, u32[]{:S(2)}, u32[]{:S(2)}) collective-permute-start(bf16[4,64,1280]{2,1,0:T(8,128)(2,1)} %collective-permute-done.9.refs_5_), channel_id=1, source_target_pairs={{0,1},{1,0},{2,3},{3,2},{4,5},{5,4},{6,7},{7,6},{8,9},{9,8},{10,11... | collective-permute-start | bytes 1966088 | tf_op jit(solution)/shard_map/ppermute | solution.py:480
  57.3 4.2 %collective-permute-start.12 = (bf16[512,512]{1,0:T(8,128)(2,1)S(1)}, bf16[512,512]{1,0:T(8,128)(2,1)S(1)}, u32[]{:S(2)}, u32[]{:S(2)}) collective-permute-start(bf16[512,512]{1,0:T(8,128)(2,1)S(1)} %get-tuple-element.107), channel_id=1, source_target_pairs={{0,16},{16,0},{1,17},{17,1},{2,18},{18,2},{3,19},{19,3},{4,20},{20... | collective-permute-start | bytes 1572872 | tf_op jit(solution)/shard_map/ppermute | solution.py:472
  69.4 6.6 %collective-permute-start.14 = (bf16[512,512]{1,0:T(8,128)(2,1)S(1)}, bf16[512,512]{1,0:T(8,128)(2,1)S(1)}, u32[]{:S(2)}, u32[]{:S(2)}) collective-permute-start(bf16[512,512]{1,0:T(8,128)(2,1)S(1)} %get-tuple-element.105), channel_id=1, source_target_pairs={{0,16},{16,0},{1,17},{17,1},{2,18},{18,2},{3,19},{19,3},{4,20},{20... | collective-permute-start | bytes 1572872 | tf_op jit(solution)/shard_map/ppermute | solution.py:472
  82.7 11.0 %collective-permute-start.15 = (bf16[4,64,1280]{2,1,0:T(8,128)(2,1)S(1)}, bf16[4,64,1280]{2,1,0:T(8,128)(2,1)S(1)}, u32[]{:S(2)}, u32[]{:S(2)}) collective-permute-start(bf16[4,64,1280]{2,1,0:T(8,128)(2,1)S(1)} %get-tuple-element.84), channel_id=1, source_target_pairs={{0,3},{1,2},{2,1},{3,0},{4,7},{5,6},{6,5},{7,4},{8,11},{9,10},{10,... | collective-permute-start | bytes 1966088 | tf_op jit(solution)/shard_map/ppermute | solution.py:480
  83.6 10.1 %collective-permute-start.16 = (bf16[4,64,1280]{2,1,0:T(8,128)(2,1)S(1)}, bf16[4,64,1280]{2,1,0:T(8,128)(2,1)S(1)}, u32[]{:S(2)}, u32[]{:S(2)}) collective-permute-start(bf16[4,64,1280]{2,1,0:T(8,128)(2,1)S(1)} %get-tuple-element.85), channel_id=1, source_target_pairs={{0,1},{1,0},{2,3},{3,2},{4,5},{5,4},{6,7},{7,6},{8,9},{9,8},{10,11... | collective-permute-start | bytes 1966088 | tf_op jit(solution)/shard_map/ppermute | solution.py:480
  83.6 17.1 %collective-permute-start.19 = (bf16[4,64,1280]{2,1,0:T(8,128)(2,1)S(1)}, bf16[4,64,1280]{2,1,0:T(8,128)(2,1)S(1)}, u32[]{:S(2)}, u32[]{:S(2)}) collective-permute-start(bf16[4,64,1280]{2,1,0:T(8,128)(2,1)S(1)} %get-tuple-element.90), channel_id=1, source_target_pairs={{0,3},{1,2},{2,1},{3,0},{4,7},{5,6},{6,5},{7,4},{8,11},{9,10},{10,... | collective-permute-start | bytes 1966088 | tf_op jit(solution)/shard_map/ppermute | solution.py:480
  85.4 15.3 %collective-permute-start.20 = (bf16[4,64,1280]{2,1,0:T(8,128)(2,1)S(1)}, bf16[4,64,1280]{2,1,0:T(8,128)(2,1)S(1)}, u32[]{:S(2)}, u32[]{:S(2)}) collective-permute-start(bf16[4,64,1280]{2,1,0:T(8,128)(2,1)S(1)} %get-tuple-element.91), channel_id=1, source_target_pairs={{0,1},{1,0},{2,3},{3,2},{4,5},{5,4},{6,7},{7,6},{8,9},{9,8},{10,11... | collective-permute-start | bytes 1966088 | tf_op jit(solution)/shard_map/ppermute | solution.py:480
  93.9 13.9 %collective-permute-start.18 = (bf16[4,64,1280]{2,1,0:T(8,128)(2,1)S(1)}, bf16[4,64,1280]{2,1,0:T(8,128)(2,1)S(1)}, u32[]{:S(2)}, u32[]{:S(2)}) collective-permute-start(bf16[4,64,1280]{2,1,0:T(8,128)(2,1)S(1)} %add_convert_fusion.2), channel_id=1, source_target_pairs={{0,3},{1,2},{2,1},{3,0},{4,7},{5,6},{6,5},{7,4},{8,11},{9,10},{10,... | collective-permute-start | bytes 1966088 | tf_op jit(solution)/shard_map/ppermute | solution.py:480
  95.6 12.2 %collective-permute-start.17 = (bf16[4,64,1280]{2,1,0:T(8,128)(2,1)S(1)}, bf16[4,64,1280]{2,1,0:T(8,128)(2,1)S(1)}, u32[]{:S(2)}, u32[]{:S(2)}) collective-permute-start(bf16[4,64,1280]{2,1,0:T(8,128)(2,1)S(1)} %add_convert_fusion.3), channel_id=1, source_target_pairs={{0,1},{1,0},{2,3},{3,2},{4,5},{5,4},{6,7},{7,6},{8,9},{9,8},{10,11... | collective-permute-start | bytes 1966088 | tf_op jit(solution)/shard_map/ppermute | solution.py:480
  108.3 6.3 %collective-permute-start.21 = (bf16[64,2560]{1,0:T(8,128)(2,1)S(1)}, bf16[64,2560]{1,0:T(8,128)(2,1)S(1)}, u32[]{:S(2)}, u32[]{:S(2)}) collective-permute-start(bf16[64,2560]{1,0:T(8,128)(2,1)S(1)} %get-tuple-element.102), channel_id=1, source_target_pairs={{0,4},{1,5},{2,6},{3,7},{4,0},{5,1},{6,2},{7,3},{8,12},{9,13},{10,... | collective-permute-start | bytes 983048 | tf_op jit(solution)/shard_map/ppermute | solution.py:480
  108.4 9.5 %collective-permute-start.22 = (bf16[64,2560]{1,0:T(8,128)(2,1)S(1)}, bf16[64,2560]{1,0:T(8,128)(2,1)S(1)}, u32[]{:S(2)}, u32[]{:S(2)}) collective-permute-start(bf16[64,2560]{1,0:T(8,128)(2,1)S(1)} %get-tuple-element.104), channel_id=1, source_target_pairs={{0,12},{1,13},{2,14},{3,15},{4,8},{5,9},{6,10},{7,11},{8,4},{9,5},... | collective-permute-start | bytes 983048 | tf_op jit(solution)/shard_map/ppermute | solution.py:480
  110.4 9.3 %collective-permute-start.23 = (bf16[64,2560]{1,0:T(8,128)(2,1)S(1)}, bf16[64,2560]{1,0:T(8,128)(2,1)S(1)}, u32[]{:S(2)}, u32[]{:S(2)}) collective-permute-start(bf16[64,2560]{1,0:T(8,128)(2,1)S(1)} %get-tuple-element.103), channel_id=1, source_target_pairs={{0,8},{1,9},{2,10},{3,11},{4,12},{5,13},{6,14},{7,15},{8,0},{9,1},... | collective-permute-start | bytes 983048 | tf_op jit(solution)/shard_map/ppermute | solution.py:480
  152.1 19.2 %collective-permute-start.24 = (bf16[64,2560]{1,0:T(8,128)(2,1)S(1)}, bf16[64,2560]{1,0:T(8,128)(2,1)S(1)}, u32[]{:S(2)}, u32[]{:S(2)}) collective-permute-start(bf16[64,2560]{1,0:T(8,128)(2,1)S(1)} %bitcast.36), channel_id=1, source_target_pairs={{0,16},{16,0},{1,17},{17,1},{2,18},{18,2},{3,19},{19,3},{4,20},{20... | collective-permute-start | bytes 983048 | tf_op jit(solution)/shard_map/ppermute | solution.py:472
  (13 other events, 344.5 us)

commit v6 on v5

--- a/solution.py
+++ b/solution.py
@@ -485,11 +485,9 @@
     for step in range(2):
         got = [over_link(part, *ROUNDS[turn][step]) for turn, part in enumerate(held)]
         held = [jnp.concatenate(pair, axis=0) for pair in zip(held, got)]
+        held = lax.optimization_barrier(held)
         if step == 0:
-            held = lax.optimization_barrier(held)
             held[0], beside = prepare(held[0])
-        else:
-            held, beside = lax.optimization_barrier((held, beside))
     first = [over_link(part, *ROUNDS[turn][2]) for turn, part in enumerate(held)]
     second = [over_link(part, *ROUNDS[turn][3]) for turn, part in enumerate(held)]
     first = lax.optimization_barrier(first)
@@ -554,16 +552,11 @@
         row_index = jnp.arange(rows, dtype=jnp.int32)
         live = row_index[None, :] < lengths[:, None]
         masked = jnp.where(live[:, :, None], cot_rows, jnp.zeros_like(cot_rows))
-        mine = jnp.concatenate([normed, masked], axis=0)
-        return got, (mine, swap_cores(mine), lengths_other)
-
-    def join(made):
-        mine, other, lengths_other = made
-        normed, masked = (
-            jnp.concatenate([side[at : at + slots] for side in (mine, other)], axis=0)
-            for at in (0, slots)
-        )
-        all_lengths = jnp.concatenate([lengths, lengths_other], axis=0)
+        pairs = (normed, swap_cores(normed)), (masked, swap_cores(masked)), (lengths, lengths_other)
+        return got, pairs
+
+    def join(pairs):
+        normed, masked, all_lengths = (jnp.concatenate(pair, axis=0) for pair in pairs)
         return normed, masked, all_lengths, normed.reshape(-1, model_width).T
 
     parts, (normed, masked, all_lengths, normed_t) = gather_parts(

time: 176 us -> 175 us (level)
  starting transfers between devices: 31.4 us -> 37.9 us
  waiting for transfers between devices: 51.6 us -> 46.8 us
  local copies, waits for them, and re-layouts: 9.98 us -> 6.3 us
    ppermute x6 -> x7, starting transfers between devices: 11.9 us -> 18.1 us  [swap_cores(): return lax.ppermute(values, 'c', SWAP)]
    ppermute x19, waiting for transfers between devices: 48.5 us -> 43.7 us  [over_link(): return lax.ppermute(values, ('c', *OWN), pairs)]
    slice x1 -> x0, local copies, waits for them, and re-layouts: 3.32 us -> none  [join(): side[at:at + slots]]
    concatenate x4 -> x3, other arithmetic: 2.16 us -> 3.52 us  [join(): jnp.concatenate(pair, axis=0)]
  transfers between devices with their start and end apart: 25 -> 26, of which waited for: 15 -> 18; matrix products, arithmetic and copies ran while one was open for 6% -> 5% of each run, Pallas kernels for 3% -> 3%
where the time goes in v6:
time: 175 us; the launch traced here: 174 us
  waiting for transfers between devices  46.8 us (27%)
  blocking collectives  43.2 us (25%)
  starting transfers between devices  37.9 us (22%)
  Pallas kernels  30.6 us (17%)
  other arithmetic  8.46 us (5%)
  local copies, waits for them, and re-layouts  6.3 us (4%)
    ppermute x19, waiting for transfers between devices, over_link(): return lax.ppermute(values, ('c', *OWN), pairs)  43.7 us
    all_to_all x3, blocking collectives, exchange(): return lax.all_to_all(blocks, axes, 0, 0, tiled=True)  43.2 us
    pallas_call x6, Pallas kernels, call(): pl.pallas_call(kernel, grid_spec=pltpu.PrefetchScalarGridSpec(num_scalar_...  30.6 us
    ppermute x19, starting transfers between devices, over_link(): return lax.ppermute(values, ('c', *OWN), pairs)  19.8 us
    ppermute x7, starting transfers between devices, swap_cores(): return lax.ppermute(values, 'c', SWAP)  18.1 us
    concatenate x3, other arithmetic, join(): jnp.concatenate(pair, axis=0)  3.52 us
  transfers between devices with their start and end apart: 26, of which 18 were waited for; matrix products, arithmetic and copies ran while one was open for 5% of the time, Pallas kernels for 3%

profile of v6, /device:TPU:1, one launch (start us, length us, event | category | flops | bytes accessed | tf_op | source)
XLA Modules:
  0.0 174.5 jit_solution(2235725193519471646)
XLA Ops:
  2.5 3.7 %collective-permute-start.1 = (bf16[1,64,1280]{2,1,0:T(8,128)(2,1)S(1)}, bf16[1,64,1280]{2,1,0:T(8,128)(2,1)S(1)}, u32[]{:S(2)}, u32[]{:S(2)}) collective-permute-start(bf16[1,64,1280]{2,1,0:T(8,128)(2,1)S(1)} %maximum_bitcast_fusion.2), channel_id=1, source_target_pairs={{0,12},{1,13},{2,14},{3,15},{4,8},{5,9},{6,10},{7,11},{8,4},{9,5},... | collective-permute-start | bytes 491528 | tf_op jit(solution)/shard_map/ppermute | solution.py:480
  12.8 2.7 %collective-permute-start.11 = (bf16[2,256,1024]{2,1,0:T(8,128)(2,1)S(1)}, bf16[2,256,1024]{2,1,0:T(8,128)(2,1)S(1)}, u32[]{:S(2)}, u32[]{:S(2)}) collective-permute-start(bf16[2,256,1024]{2,1,0:T(8,128)(2,1)S(1)} %fusion.2), channel_id=1, source_target_pairs={{0,16},{16,0},{1,17},{17,1},{2,18},{18,2},{3,19},{19,3},{4,20},{20... | collective-permute-start | bytes 3145736 | tf_op jit(solution)/shard_map/ppermute | solution.py:472
  15.5 1.9 %collective-permute-done.4 = bf16[2,64,1280]{2,1,0:T(8,128)(2,1)S(1)} collective-permute-done((bf16[2,64,1280]{2,1,0:T(8,128)(2,1)S(1)}, bf16[2,64,1280]{2,1,0:T(8,128)(2,1)S(1)}, u32[]{:S(2)}, u32[]{:S(2)}) %collective-permute-start.4) | collective-permute-done | bytes 327712 | tf_op jit(solution)/shard_map/ppermute | solution.py:480
  22.6 3.7 %collective-permute-start.12 = (bf16[2,256,1024]{2,1,0:T(8,128)(2,1)}, bf16[2,256,1024]{2,1,0:T(8,128)(2,1)}, u32[]{:S(2)}, u32[]{:S(2)}) collective-permute-start(bf16[2,256,1024]{2,1,0:T(8,128)(2,1)} %broadcast_select_fusion), channel_id=1, source_target_pairs={{0,16},{16,0},{1,17},{17,1},{2,18},{18,2},{3,19},{19,3},{4,20},{20... | collective-permute-start | bytes 3145736 | tf_op jit(solution)/shard_map/ppermute | solution.py:472
  31.7 1.9 %collective-permute-start.9 = (bf16[4,64,1280]{2,1,0:T(8,128)(2,1)}, bf16[4,64,1280]{2,1,0:T(8,128)(2,1)}, u32[]{:S(2)}, u32[]{:S(2)}) collective-permute-start(bf16[4,64,1280]{2,1,0:T(8,128)(2,1)} %collective-permute-done.7.refs_1_), channel_id=1, source_target_pairs={{0,3},{1,2},{2,1},{3,0},{4,7},{5,6},{6,5},{7,4},{8,11},{9,10},{10,... | collective-permute-start | bytes 1966088 | tf_op jit(solution)/shard_map/ppermute | solution.py:480
  35.5 2.6 %copy.17 = bf16[1024,1024]{0,1:T(8,128)(2,1)} copy(bf16[1024,1024]{1,0:T(8,128)(2,1)S(1)} %bitcast.33) | data formatting | bytes 4194304 | tf_op jit(solution)/shard_map/reshape | solution.py:560
  39.8 5.7 %collective-permute-done.10.refs_7_ = bf16[4,64,1280]{2,1,0:T(8,128)(2,1)} collective-permute-done((bf16[4,64,1280]{2,1,0:T(8,128)(2,1)}, bf16[4,64,1280]{2,1,0:T(8,128)(2,1)}, u32[]{:S(2)}, u32[]{:S(2)}) %collective-permute-start.10) | collective-permute-done | bytes 655392 | tf_op jit(solution)/shard_map/ppermute | solution.py:480
  45.6 8.7 %attention_forward.1 = (f32[4,256,1536]{2,1,0:T(8,128)S(1)}, f32[4,256,512]{2,1,0:T(8,128)S(1)}, f32[4,2,256,256]{3,2,1,0:T(8,128)S(1)}, f32[4,256,512]{2,1,0:T(8,128)S(1)}, bf16[1024,512]{1,0:T(8,128)(2,1)S(1)}) custom-call(s32[2]{0:T(128)S(1)} %pad_add_fusion.place, s32[4]{0:T(128)S(1)} %pad_add_fusion.1.lengths, ...), custom_call_target="tpu_custom_call" | custom-call | flops 1 | bytes 1 | tf_op jit(solution)/shard_map/attention_forward/pallas_call | solution.py:276
  54.4 4.3 %collective-permute-start.13 = (bf16[512,512]{1,0:T(8,128)(2,1)S(1)}, bf16[512,512]{1,0:T(8,128)(2,1)S(1)}, u32[]{:S(2)}, u32[]{:S(2)}) collective-permute-start(bf16[512,512]{1,0:T(8,128)(2,1)S(1)} %get-tuple-element.97), channel_id=1, source_target_pairs={{0,16},{16,0},{1,17},{17,1},{2,18},{18,2},{3,19},{19,3},{4,20},{20... | collective-permute-start | bytes 1572872 | tf_op jit(solution)/shard_map/ppermute | solution.py:472
  60.3 2.5 %gating_forward.1 = (bf16[4,256,512]{2,1,0:T(8,128)(2,1)S(1)}, f32[4,256,128]{2,1,0:T(8,128)S(1)}) custom-call(s32[2]{0:T(128)S(1)} %pad_add_fusion.place, f32[4,256,512]{2,1,0:T(8,128)S(1)} %get-tuple-element.66.gating.gating_in.projected, bf16[4,256,1024]{2,1,0:T(8,128)(2,1)S(1)} %pad_maximum_fusion.1.masked, bf16[512,512]{1,0:T(8,128)(2,1)S(1)} %get-tuple-element.98.keep, ...), custom_call_target="tpu_custom_call" | custom-call | flops 1 | bytes 1 | tf_op jit(solution)/shard_map/gating_forward/pallas_call | solution.py:276
  64.8 3.3 %outer_term.1 = bf16[2,512,512]{2,1,0:T(8,128)(2,1)S(1)} custom-call(s32[2]{0:T(128)S(1)} %pad_add_fusion.place, f32[4,256,512]{2,1,0:T(8,128)S(1)} %get-tuple-element.66.gating.gating_in.projected, f32[4,256,512]{2,1,0:T(8,128)S(1)} %get-tuple-element.69.mixed, f32[4,256,128]{2,1,0:T(8,128)S(1)} %get-tuple-element.73.stats, ...), custom_call_target="tpu_custom_call" | custom-call | flops 1 | bytes 1 | tf_op jit(solution)/shard_map/outer_term/pallas_call | solution.py:276
  68.7 5.7 %attention_back.1 = bf16[4,256,2048]{2,1,0:T(8,128)(2,1)S(1)} custom-call(s32[4]{0:T(128)S(1)} %pad_add_fusion.1.lengths, f32[4,256,512]{2,1,0:T(8,128)S(1)} %get-tuple-element.66.gating.gating_in.projected, f32[4,256,1536]{2,1,0:T(8,128)S(1)} %get-tuple-element.67.projected, f32[4,2,256,256]{3,2,1,0:T(8,128)S(1)} %get-tuple-element.68.scores, ...), custom_call_target="tpu_custom_call" | custom-call | flops 1 | bytes 1 | tf_op jit(solution)/shard_map/attention_back/pallas_call | solution.py:276
  74.5 6.6 %terms.1 = (bf16[4,64,1280]{2,1,0:T(8,128)(2,1)S(1)}, bf16[4,64,1280]{2,1,0:T(8,128)(2,1)S(1)}, bf16[4,64,1280]{2,1,0:T(8,128)(2,1)S(1)}, bf16[4,64,1280]{2,1,0:...) custom-call(s32[2]{0:T(128)S(1)} %pad_add_fusion.place, ...), custom_call_target="tpu_custom_call" | custom-call | flops 1 | bytes 1 | tf_op jit(solution)/shard_map/terms/pallas_call | solution.py:276
  84.8 7.4 %collective-permute-done.16 = bf16[4,64,1280]{2,1,0:T(8,128)(2,1)S(1)} collective-permute-done((bf16[4,64,1280]{2,1,0:T(8,128)(2,1)S(1)}, bf16[4,64,1280]{2,1,0:T(8,128)(2,1)S(1)}, u32[]{:S(2)}, u32[]{:S(2)}) %collective-permute-start.16) | collective-permute-done | bytes 655392 | tf_op jit(solution)/shard_map/ppermute | solution.py:480
  94.5 4.7 %collective-permute-done.20 = bf16[4,64,1280]{2,1,0:T(8,128)(2,1)S(1)} collective-permute-done((bf16[4,64,1280]{2,1,0:T(8,128)(2,1)S(1)}, bf16[4,64,1280]{2,1,0:T(8,128)(2,1)S(1)}, u32[]{:S(2)}, u32[]{:S(2)}) %collective-permute-start.20) | collective-permute-done | bytes 655392 | tf_op jit(solution)/shard_map/ppermute | solution.py:480
  99.8 6.4 %collective-permute-done.19 = bf16[4,64,1280]{2,1,0:T(8,128)(2,1)S(1)} collective-permute-done((bf16[4,64,1280]{2,1,0:T(8,128)(2,1)S(1)}, bf16[4,64,1280]{2,1,0:T(8,128)(2,1)S(1)}, u32[]{:S(2)}, u32[]{:S(2)}) %collective-permute-start.19) | collective-permute-done | bytes 655392 | tf_op jit(solution)/shard_map/ppermute | solution.py:480
  107.9 1.9 %collective-permute-start.23 = (bf16[64,2560]{1,0:T(8,128)(2,1)S(1)}, bf16[64,2560]{1,0:T(8,128)(2,1)S(1)}, u32[]{:S(2)}, u32[]{:S(2)}) collective-permute-start(bf16[64,2560]{1,0:T(8,128)(2,1)S(1)} %get-tuple-element.94), channel_id=1, source_target_pairs={{0,12},{1,13},{2,14},{3,15},{4,8},{5,9},{6,10},{7,11},{8,4},{9,5},... | collective-permute-start | bytes 983048 | tf_op jit(solution)/shard_map/ppermute | solution.py:480
  110.8 2.9 %collective-permute-done.22 = bf16[64,2560]{1,0:T(8,128)(2,1)S(1)} collective-permute-done((bf16[64,2560]{1,0:T(8,128)(2,1)S(1)}, bf16[64,2560]{1,0:T(8,128)(2,1)S(1)}, u32[]{:S(2)}, u32[]{:S(2)}) %collective-permute-start.22) | collective-permute-done | bytes 327712 | tf_op jit(solution)/shard_map/ppermute | solution.py:480
  113.7 3.6 %collective-permute-done.23 = bf16[64,2560]{1,0:T(8,128)(2,1)S(1)} collective-permute-done((bf16[64,2560]{1,0:T(8,128)(2,1)S(1)}, bf16[64,2560]{1,0:T(8,128)(2,1)S(1)}, u32[]{:S(2)}, u32[]{:S(2)}) %collective-permute-start.23) | collective-permute-done | bytes 327712 | tf_op jit(solution)/shard_map/ppermute | solution.py:480
  119.4 18.4 %all_to_all.25 = bf16[8,8,2560]{2,1,0:T(8,128)(2,1)} all-to-all(bf16[8,8,2560]{2,1,0:T(8,128)(2,1)S(1)} %maximum_bitcast_fusion), channel_id=1, replica_groups=mesh['z'=8,'c'=2,'x'=4,'y'=4] {'z'}, dimensions={0} | all-to-all | bytes 655360 | tf_op jit(solution)/shard_map/all_to_all | solution.py:517
  138.9 12.6 %all_to_all.26 = bf16[8,8,2560]{2,1,0:T(8,128)(2,1)S(1)} all-to-all(bf16[8,8,2560]{2,1,0:T(8,128)(2,1)S(1)} %broadcast_in_dim.35), channel_id=1, replica_groups=mesh['z'=8,'c'=2,'x'=4,'y'=4] {'z'}, dimensions={0} | all-to-all | bytes 655360 | tf_op jit(solution)/shard_map/all_to_all | solution.py:517
  151.4 5.5 %collective-permute-start.25 = (bf16[64,2560]{1,0:T(8,128)(2,1)S(1)}, bf16[64,2560]{1,0:T(8,128)(2,1)S(1)}, u32[]{:S(2)}, u32[]{:S(2)}) collective-permute-start(bf16[64,2560]{1,0:T(8,128)(2,1)S(1)} %bitcast.36), channel_id=1, source_target_pairs={{0,16},{16,0},{1,17},{17,1},{2,18},{18,2},{3,19},{19,3},{4,20},{20... | collective-permute-start | bytes 983048 | tf_op jit(solution)/shard_map/ppermute | solution.py:472
  158.3 12.2 %all_to_all.27 = f32[32,8,128]{2,1,0:T(8,128)S(1)} all-to-all(f32[32,8,128]{2,1,0:T(8,128)S(1)} %broadcast_in_dim.36), channel_id=1, replica_groups=mesh['z'=8,'c'=2,'x'=4,'y'=4] {'c','x','y'}, dimensions={0} | all-to-all | bytes 262144 | tf_op jit(solution)/shard_map/all_to_all | solution.py:517
  170.6 3.7 %update_rows.1 = (f32[64,4096]{1,0:T(8,128)}, f32[64,4096]{1,0:T(8,128)}, f32[64,4096]{1,0:T(8,128)}, f32[64,1024]{1,0:T(8,128)}, f32[64,1024]{1,0:T(8,128)}, /*index=5*/f32[64,1024]{1,0:T(8,128)}) custom-call(s32[2]{0:T(128)S(1)} %pad_add_fusion.place, f32[256,128]{1,0:T(8,128)S(1)} %bitcast.39, bf16[64,2560]{1,0:T(8,128)(2,1)S(1)} %bitcast.37, ...), custom_call_target="tpu_custom_call" | custom-call | flops 1 | bytes 1 | tf_op jit(solution)/shard_map/update_rows/pallas_call | solution.py:276
  (95 shorter events, 40.6 us)
Async XLA Ops:
  2.5 6.4 %collective-permute-start.1 = (bf16[1,64,1280]{2,1,0:T(8,128)(2,1)S(1)}, bf16[1,64,1280]{2,1,0:T(8,128)(2,1)S(1)}, u32[]{:S(2)}, u32[]{:S(2)}) collective-permute-start(bf16[1,64,1280]{2,1,0:T(8,128)(2,1)S(1)} %maximum_bitcast_fusion.2), channel_id=1, source_target_pairs={{0,12},{1,13},{2,14},{3,15},{4,8},{5,9},{6,10},{7,11},{8,4},{9,5},... | collective-permute-start | bytes 491528 | tf_op jit(solution)/shard_map/ppermute | solution.py:480
  6.2 4.6 %collective-permute-start = (bf16[1,64,1280]{2,1,0:T(8,128)(2,1)S(1)}, bf16[1,64,1280]{2,1,0:T(8,128)(2,1)S(1)}, u32[]{:S(2)}, u32[]{:S(2)}) collective-permute-start(bf16[1,64,1280]{2,1,0:T(8,128)(2,1)S(1)} %maximum_bitcast_fusion.1), channel_id=1, source_target_pairs={{0,4},{1,5},{2,6},{3,7},{4,0},{5,1},{6,2},{7,3},{8,12},{9,13},{10,... | collective-permute-start | bytes 491528 | tf_op jit(solution)/shard_map/ppermute | solution.py:480
  11.1 6.3 %collective-permute-start.4 = (bf16[2,64,1280]{2,1,0:T(8,128)(2,1)S(1)}, bf16[2,64,1280]{2,1,0:T(8,128)(2,1)S(1)}, u32[]{:S(2)}, u32[]{:S(2)}) collective-permute-start(bf16[2,64,1280]{2,1,0:T(8,128)(2,1)S(1)} %pad_maximum_fusion.6), channel_id=1, source_target_pairs={{0,4},{1,5},{2,6},{3,7},{4,0},{5,1},{6,2},{7,3},{8,12},{9,13},{10,... | collective-permute-start | bytes 983048 | tf_op jit(solution)/shard_map/ppermute | solution.py:480
  11.2 7.5 %collective-permute-start.3 = (bf16[2,64,1280]{2,1,0:T(8,128)(2,1)S(1)}, bf16[2,64,1280]{2,1,0:T(8,128)(2,1)S(1)}, u32[]{:S(2)}, u32[]{:S(2)}) collective-permute-start(bf16[2,64,1280]{2,1,0:T(8,128)(2,1)S(1)} %pad_maximum_fusion.5), channel_id=1, source_target_pairs={{0,12},{1,13},{2,14},{3,15},{4,8},{5,9},{6,10},{7,11},{8,4},{9,5},... | collective-permute-start | bytes 983048 | tf_op jit(solution)/shard_map/ppermute | solution.py:480
  12.8 18.0 %collective-permute-start.11 = (bf16[2,256,1024]{2,1,0:T(8,128)(2,1)S(1)}, bf16[2,256,1024]{2,1,0:T(8,128)(2,1)S(1)}, u32[]{:S(2)}, u32[]{:S(2)}) collective-permute-start(bf16[2,256,1024]{2,1,0:T(8,128)(2,1)S(1)} %fusion.2), channel_id=1, source_target_pairs={{0,16},{16,0},{1,17},{17,1},{2,18},{18,2},{3,19},{19,3},{4,20},{20... | collective-permute-start | bytes 3145736 | tf_op jit(solution)/shard_map/ppermute | solution.py:472
  18.8 9.9 %collective-permute-start.7 = (bf16[4,64,1280]{2,1,0:T(8,128)(2,1)S(1)}, bf16[4,64,1280]{2,1,0:T(8,128)(2,1)}, u32[]{:S(2)}, u32[]{:S(2)}) collective-permute-start(bf16[4,64,1280]{2,1,0:T(8,128)(2,1)S(1)} %pad_maximum_fusion.2.refs_0_), channel_id=1, source_target_pairs={{0,1},{1,0},{2,3},{3,2},{4,5},{5,4},{6,7},{7,6},{8,9},{9,8},{10,11... | collective-permute-start | bytes 1966088 | tf_op jit(solution)/shard_map/ppermute | solution.py:480
  19.7 11.0 %collective-permute-start.8 = (bf16[4,64,1280]{2,1,0:T(8,128)(2,1)S(1)}, bf16[4,64,1280]{2,1,0:T(8,128)(2,1)}, u32[]{:S(2)}, u32[]{:S(2)}) collective-permute-start(bf16[4,64,1280]{2,1,0:T(8,128)(2,1)S(1)} %pad_maximum_fusion.3.refs_4_), channel_id=1, source_target_pairs={{0,3},{1,2},{2,1},{3,0},{4,7},{5,6},{6,5},{7,4},{8,11},{9,10},{10,... | collective-permute-start | bytes 1966088 | tf_op jit(solution)/shard_map/ppermute | solution.py:480
  22.6 15.5 %collective-permute-start.12 = (bf16[2,256,1024]{2,1,0:T(8,128)(2,1)}, bf16[2,256,1024]{2,1,0:T(8,128)(2,1)}, u32[]{:S(2)}, u32[]{:S(2)}) collective-permute-start(bf16[2,256,1024]{2,1,0:T(8,128)(2,1)} %broadcast_select_fusion), channel_id=1, source_target_pairs={{0,16},{16,0},{1,17},{17,1},{2,18},{18,2},{3,19},{19,3},{4,20},{20... | collective-permute-start | bytes 3145736 | tf_op jit(solution)/shard_map/ppermute | solution.py:472
  26.3 13.6 %collective-permute-start.5 = (bf16[4,64,1280]{2,1,0:T(8,128)(2,1)S(1)}, bf16[4,64,1280]{2,1,0:T(8,128)(2,1)}, u32[]{:S(2)}, u32[]{:S(2)}) collective-permute-start(bf16[4,64,1280]{2,1,0:T(8,128)(2,1)S(1)} %pad_maximum_fusion.2.refs_0_), channel_id=1, source_target_pairs={{0,3},{1,2},{2,1},{3,0},{4,7},{5,6},{6,5},{7,4},{8,11},{9,10},{10,... | collective-permute-start | bytes 1966088 | tf_op jit(solution)/shard_map/ppermute | solution.py:480
  28.7 11.1 %collective-permute-start.6 = (bf16[4,64,1280]{2,1,0:T(8,128)(2,1)S(1)}, bf16[4,64,1280]{2,1,0:T(8,128)(2,1)}, u32[]{:S(2)}, u32[]{:S(2)}) collective-permute-start(bf16[4,64,1280]{2,1,0:T(8,128)(2,1)S(1)} %pad_maximum_fusion.3.refs_4_), channel_id=1, source_target_pairs={{0,1},{1,0},{2,3},{3,2},{4,5},{5,4},{6,7},{7,6},{8,9},{9,8},{10,11... | collective-permute-start | bytes 1966088 | tf_op jit(solution)/shard_map/ppermute | solution.py:480
  30.7 14.8 %collective-permute-start.10 = (bf16[4,64,1280]{2,1,0:T(8,128)(2,1)}, bf16[4,64,1280]{2,1,0:T(8,128)(2,1)}, u32[]{:S(2)}, u32[]{:S(2)}) collective-permute-start(bf16[4,64,1280]{2,1,0:T(8,128)(2,1)} %collective-permute-done.8.refs_5_), channel_id=1, source_target_pairs={{0,1},{1,0},{2,3},{3,2},{4,5},{5,4},{6,7},{7,6},{8,9},{9,8},{10,11... | collective-permute-start | bytes 1966088 | tf_op jit(solution)/shard_map/ppermute | solution.py:480
  31.7 13.9 %collective-permute-start.9 = (bf16[4,64,1280]{2,1,0:T(8,128)(2,1)}, bf16[4,64,1280]{2,1,0:T(8,128)(2,1)}, u32[]{:S(2)}, u32[]{:S(2)}) collective-permute-start(bf16[4,64,1280]{2,1,0:T(8,128)(2,1)} %collective-permute-done.7.refs_1_), channel_id=1, source_target_pairs={{0,3},{1,2},{2,1},{3,0},{4,7},{5,6},{6,5},{7,4},{8,11},{9,10},{10,... | collective-permute-start | bytes 1966088 | tf_op jit(solution)/shard_map/ppermute | solution.py:480
  54.4 5.9 %collective-permute-start.13 = (bf16[512,512]{1,0:T(8,128)(2,1)S(1)}, bf16[512,512]{1,0:T(8,128)(2,1)S(1)}, u32[]{:S(2)}, u32[]{:S(2)}) collective-permute-start(bf16[512,512]{1,0:T(8,128)(2,1)S(1)} %get-tuple-element.97), channel_id=1, source_target_pairs={{0,16},{16,0},{1,17},{17,1},{2,18},{18,2},{3,19},{19,3},{4,20},{20... | collective-permute-start | bytes 1572872 | tf_op jit(solution)/shard_map/ppermute | solution.py:472
  68.1 6.4 %collective-permute-start.15 = (bf16[512,512]{1,0:T(8,128)(2,1)S(1)}, bf16[512,512]{1,0:T(8,128)(2,1)S(1)}, u32[]{:S(2)}, u32[]{:S(2)}) collective-permute-start(bf16[512,512]{1,0:T(8,128)(2,1)S(1)} %get-tuple-element.95), channel_id=1, source_target_pairs={{0,16},{16,0},{1,17},{17,1},{2,18},{18,2},{3,19},{19,3},{4,20},{20... | collective-permute-start | bytes 1572872 | tf_op jit(solution)/shard_map/ppermute | solution.py:472
  81.1 11.0 %collective-permute-start.16 = (bf16[4,64,1280]{2,1,0:T(8,128)(2,1)S(1)}, bf16[4,64,1280]{2,1,0:T(8,128)(2,1)S(1)}, u32[]{:S(2)}, u32[]{:S(2)}) collective-permute-start(bf16[4,64,1280]{2,1,0:T(8,128)(2,1)S(1)} %get-tuple-element.78), channel_id=1, source_target_pairs={{0,3},{1,2},{2,1},{3,0},{4,7},{5,6},{6,5},{7,4},{8,11},{9,10},{10,... | collective-permute-start | bytes 1966088 | tf_op jit(solution)/shard_map/ppermute | solution.py:480
  83.0 9.7 %collective-permute-start.17 = (bf16[4,64,1280]{2,1,0:T(8,128)(2,1)S(1)}, bf16[4,64,1280]{2,1,0:T(8,128)(2,1)S(1)}, u32[]{:S(2)}, u32[]{:S(2)}) collective-permute-start(bf16[4,64,1280]{2,1,0:T(8,128)(2,1)S(1)} %get-tuple-element.79), channel_id=1, source_target_pairs={{0,1},{1,0},{2,3},{3,2},{4,5},{5,4},{6,7},{7,6},{8,9},{9,8},{10,11... | collective-permute-start | bytes 1966088 | tf_op jit(solution)/shard_map/ppermute | solution.py:480
  83.0 16.2 %collective-permute-start.20 = (bf16[4,64,1280]{2,1,0:T(8,128)(2,1)S(1)}, bf16[4,64,1280]{2,1,0:T(8,128)(2,1)S(1)}, u32[]{:S(2)}, u32[]{:S(2)}) collective-permute-start(bf16[4,64,1280]{2,1,0:T(8,128)(2,1)S(1)} %get-tuple-element.84), channel_id=1, source_target_pairs={{0,3},{1,2},{2,1},{3,0},{4,7},{5,6},{6,5},{7,4},{8,11},{9,10},{10,... | collective-permute-start | bytes 1966088 | tf_op jit(solution)/shard_map/ppermute | solution.py:480
  83.9 15.9 %collective-permute-start.21 = (bf16[4,64,1280]{2,1,0:T(8,128)(2,1)S(1)}, bf16[4,64,1280]{2,1,0:T(8,128)(2,1)S(1)}, u32[]{:S(2)}, u32[]{:S(2)}) collective-permute-start(bf16[4,64,1280]{2,1,0:T(8,128)(2,1)S(1)} %get-tuple-element.85), channel_id=1, source_target_pairs={{0,1},{1,0},{2,3},{3,2},{4,5},{5,4},{6,7},{7,6},{8,9},{9,8},{10,11... | collective-permute-start | bytes 1966088 | tf_op jit(solution)/shard_map/ppermute | solution.py:480
  92.9 13.3 %collective-permute-start.19 = (bf16[4,64,1280]{2,1,0:T(8,128)(2,1)S(1)}, bf16[4,64,1280]{2,1,0:T(8,128)(2,1)S(1)}, u32[]{:S(2)}, u32[]{:S(2)}) collective-permute-start(bf16[4,64,1280]{2,1,0:T(8,128)(2,1)S(1)} %add_convert_fusion.2), channel_id=1, source_target_pairs={{0,3},{1,2},{2,1},{3,0},{4,7},{5,6},{6,5},{7,4},{8,11},{9,10},{10,... | collective-permute-start | bytes 1966088 | tf_op jit(solution)/shard_map/ppermute | solution.py:480
  94.4 12.4 %collective-permute-start.18 = (bf16[4,64,1280]{2,1,0:T(8,128)(2,1)S(1)}, bf16[4,64,1280]{2,1,0:T(8,128)(2,1)S(1)}, u32[]{:S(2)}, u32[]{:S(2)}) collective-permute-start(bf16[4,64,1280]{2,1,0:T(8,128)(2,1)S(1)} %add_convert_fusion.3), channel_id=1, source_target_pairs={{0,1},{1,0},{2,3},{3,2},{4,5},{5,4},{6,7},{7,6},{8,9},{9,8},{10,11... | collective-permute-start | bytes 1966088 | tf_op jit(solution)/shard_map/ppermute | solution.py:480
  107.4 6.3 %collective-permute-start.22 = (bf16[64,2560]{1,0:T(8,128)(2,1)S(1)}, bf16[64,2560]{1,0:T(8,128)(2,1)S(1)}, u32[]{:S(2)}, u32[]{:S(2)}) collective-permute-start(bf16[64,2560]{1,0:T(8,128)(2,1)S(1)} %get-tuple-element.92), channel_id=1, source_target_pairs={{0,4},{1,5},{2,6},{3,7},{4,0},{5,1},{6,2},{7,3},{8,12},{9,13},{10,... | collective-permute-start | bytes 983048 | tf_op jit(solution)/shard_map/ppermute | solution.py:480
  107.9 9.4 %collective-permute-start.23 = (bf16[64,2560]{1,0:T(8,128)(2,1)S(1)}, bf16[64,2560]{1,0:T(8,128)(2,1)S(1)}, u32[]{:S(2)}, u32[]{:S(2)}) collective-permute-start(bf16[64,2560]{1,0:T(8,128)(2,1)S(1)} %get-tuple-element.94), channel_id=1, source_target_pairs={{0,12},{1,13},{2,14},{3,15},{4,8},{5,9},{6,10},{7,11},{8,4},{9,5},... | collective-permute-start | bytes 983048 | tf_op jit(solution)/shard_map/ppermute | solution.py:480
  109.8 9.3 %collective-permute-start.24 = (bf16[64,2560]{1,0:T(8,128)(2,1)S(1)}, bf16[64,2560]{1,0:T(8,128)(2,1)S(1)}, u32[]{:S(2)}, u32[]{:S(2)}) collective-permute-start(bf16[64,2560]{1,0:T(8,128)(2,1)S(1)} %get-tuple-element.93), channel_id=1, source_target_pairs={{0,8},{1,9},{2,10},{3,11},{4,12},{5,13},{6,14},{7,15},{8,0},{9,1},... | collective-permute-start | bytes 983048 | tf_op jit(solution)/shard_map/ppermute | solution.py:480
  151.4 19.1 %collective-permute-start.25 = (bf16[64,2560]{1,0:T(8,128)(2,1)S(1)}, bf16[64,2560]{1,0:T(8,128)(2,1)S(1)}, u32[]{:S(2)}, u32[]{:S(2)}) collective-permute-start(bf16[64,2560]{1,0:T(8,128)(2,1)S(1)} %bitcast.36), channel_id=1, source_target_pairs={{0,16},{16,0},{1,17},{17,1},{2,18},{18,2},{3,19},{19,3},{4,20},{20... | collective-permute-start | bytes 983048 | tf_op jit(solution)/shard_map/ppermute | solution.py:472
  (15 other events, 357.4 us)
